TPU v7x, 32 devices: a whole 2x2x4 slice. The times are simulated.
32 devices in a mesh: panel: 8 (over y, x, core), row: 4 (over z).
Axes of the slice: x: 2, y: 2, z: 4, core: 2. Of those that a mesh axis runs over, the one named last changes fastest.
Arguments:
- slab: float32 [4096, 2048], P('row', 'panel'), may hold values from -6 to 6
- boundary: float32 [4096, 256], P('row'), may hold values from -6 to 6
- diag_inverse: float32 [2048, 256], P(('panel', 'row')), may hold values from -1 to 1.6, as said below
- sub_block: float32 [2048, 256], P(('panel', 'row')), may hold values from -0.375 to 0.375
- tail_coupling: float32 [2048, 256], P(('panel', 'row')), may hold values from -0.125 to 0.125
- tail_cols: float32 [4096, 256], P(('row', 'panel')), may hold values from -6 to 6
Outputs:
- factor: float32 [4096, 2048], P('row', 'panel')
- tail_out: float32 [4096, 256], P(('row', 'panel'))
Inputs may be any that keep to these rules, and one draw needn't show every extreme that they name: `diag_inverse`: each block of 256 rows is lower triangular with a positive diagonal of 0.6 to 1.6.
All inputs are finite; a program needn't handle non-finite values.
Results may differ from a plain program's by a relative error of at most 0.00029.
Values sent between devices are 32-bit elements; how exact they have to be, the bound alone decides.
No kernel may reach another device: no remote copies, remote signals or barrier semaphores. Data moves between devices by JAX's collectives and lax.ppermute only.
A program may use at most 128 MiB of HBM per device.

v0:
```python
import jax
import jax.numpy as jnp
from jax import lax
from jax.sharding import PartitionSpec as P


def entering(array, axis, combine, identity):
    count, index = (lax.axis_size(axis), lax.axis_index(axis))
    everything = jax.tree.map(lambda part: lax.all_gather(part, axis), array)
    start = jax.tree.map(
        lambda part, zero: jnp.broadcast_to(jnp.asarray(zero, part.dtype), part.shape),
        array,
        identity,
    )

    def step(k, before):
        reached = k < index
        new = combine(before, jax.tree.map(lambda part: part[k], everything))
        return jax.tree.map(lambda a, b: jnp.where(reached, a, b), new, before)

    return lax.fori_loop(0, count, step, start)


def transpose_dot(left, right):
    return lax.dot_general(
        left,
        right,
        (((1,), (1,)), ((), ())),
        precision=lax.Precision.HIGHEST,
        preferred_element_type=jnp.float32,
    )


def plain_dot(left, right):
    return jnp.dot(left, right, precision=lax.Precision.HIGHEST, preferred_element_type=jnp.float32)


def on_device(slab, boundary, diag_inverse, sub_block, tail_coupling, tail_cols):
    inverse, beneath, coupling = (
        lax.all_gather(diag_inverse, "row", axis=0, tiled=True),
        lax.all_gather(sub_block, "row", axis=0, tiled=True),
        lax.all_gather(tail_coupling, "row", axis=0, tiled=True),
    )
    is_first = lax.axis_index("panel") == 0
    step_map = -jnp.transpose(plain_dot(inverse, beneath))
    own_part = transpose_dot(slab, inverse)
    own_part = own_part + jnp.where(is_first, plain_dot(boundary, step_map), 0.0)

    def combine(earlier, later_part):
        return (
            plain_dot(earlier[0], later_part[1]) + later_part[0],
            plain_dot(earlier[1], later_part[1]),
        )

    identity = (jnp.zeros_like(own_part), jnp.eye(step_map.shape[0], dtype=jnp.float32))
    prior_rows, prior_map = entering((own_part, step_map), "panel", combine, identity)
    factor = own_part + plain_dot(prior_rows, step_map)
    summed = lax.psum_scatter(plain_dot(factor, coupling), "panel", scatter_dimension=0, tiled=True)
    return (factor, tail_cols - summed)


def solution(mesh):
    placed = (
        P("row", "panel"),
        P("row", None),
        P(("panel", "row"), None),
        P(("panel", "row"), None),
        P(("panel", "row"), None),
        P(("row", "panel"), None),
    )
    return jax.shard_map(
        on_device,
        mesh=mesh,
        in_specs=placed,
        out_specs=(P("row", "panel"), P(("row", "panel"), None)),
        check_vma=False,
    )
```

profile of v0, /device:TPU:0, one launch (start us, length us, event | category | flops | bytes accessed | tf_op | source)
XLA Modules:
  0.0 222.5 jit_solution(16723277680771530876)
XLA Ops:
  7.2 0.0 copy-start
  7.2 0.0 copy-start.4
  7.2 0.0 all-gather.5.cloned.1.call-start
  7.2 16.0 %all_gather.21 = f32[256,256]{1,0:T(8,128)S(1)} all-gather(f32[64,256]{1,0:T(8,128)} %param.10), channel_id=1, replica_groups=mesh['panel'=8,'row'=4] {'row'}, dimensions={0}, use_global_device_ids=true | all-gather | bytes 327680 | tf_op jit(solution)/shard_map/all_gather | solution.py:40
  23.2 14.8 %all_gather.22 = f32[256,256]{1,0:T(8,128)S(1)} all-gather(f32[64,256]{1,0:T(8,128)} %param.11), channel_id=1, replica_groups=mesh['panel'=8,'row'=4] {'row'}, dimensions={0}, use_global_device_ids=true | all-gather | bytes 327680 | tf_op jit(solution)/shard_map/all_gather | solution.py:41
  38.0 1.3 convolution_negate_fusion
  39.3 0.0 all-gather.5.cloned.1.call-update
  39.4 0.0 all-gather.7.cloned.1.call-start
  39.4 0.0 copy-done
  39.4 2.0 fusion.9
  41.4 0.0 copy-done.4
  41.4 0.0 copy-start.6
  41.4 2.0 convolution_add_fusion.1
  43.4 0.0 all-gather.7.cloned.1.call-update
  43.4 0.0 reduce-scatter.2.cloned.1.call-start
  43.5 0.0 copy-done.6
  43.5 14.9 %all_gather.27 = f32[256,256]{1,0:T(8,128)} all-gather(f32[64,256]{1,0:T(8,128)S(1)} %copy-done.6), channel_id=1, replica_groups=mesh['panel'=8,'row'=4] {'row'}, dimensions={0}, use_global_device_ids=true | all-gather | bytes 327680 | tf_op jit(solution)/shard_map/all_gather | solution.py:42
  58.4 10.0 %all-gather.5.cloned.1.call-done = f32[2048,256]{1,0:T(8,128)} async-done(((f32[256,256]{1,0:T(8,128)}), f32[2048,256]{1,0:T(8,128)}) %all-gather.5.cloned.1.call-update) | async-done | bytes 2097168 | tf_op jit(solution)/shard_map/all_gather | solution.py:9
  68.4 56.9 %all-gather.7.cloned.1.call-done = f32[8192,256]{1,0:T(8,128)} async-done(((f32[1024,256]{1,0:T(8,128)}), f32[8192,256]{1,0:T(8,128)}) %all-gather.7.cloned.1.call-update) | async-done | bytes 8388624 | tf_op jit(solution)/shard_map/all_gather | solution.py:9
  125.3 0.0 copy-start.2
  125.3 47.5 %while.14 = (s32[]{:T(128)}, f32[1024,256]{0,1:T(8,128)}, s32[]{:T(128)}, f32[8,256,256]{2,1,0:T(8,128)}, f32[8,1024,256]{2,1,0:T(8,128)}, /*index=5*/s32[]{:T(128)}, s32[]{:T(128)}) while((s32[]{:T(128)}, f32[1024,256]{0,1:T(8,128)}, s32[]{:T(128)}, f32[8,256,256]{2,1,0:T(8,128)}, f32[8,1024,256]{2,1,0:T(8,128)}, ...), condition=%wide.region_1.2_spmd.clone, body=%wide.region_0.1_spmd.clone.sunk | while | flops 806354944 | bytes 10750051 | solution.py:21
  125.3 1.3 constant_dynamic-slice_fusion.2
  126.6 0.3 copy.13
  126.9 1.2 copy.21
  128.2 3.1 %fusion.26 = f32[1024,256]{0,1:T(8,128)} fusion(f32[1,1024,256]{1,2,0:T(8,128)S(1)} %copy.13, f32[1024,256]{0,1:T(8,128)S(1)} %copy.21, pred[]{:T(512)S(6)} %compare.3, pred[]{:T(512)S(6)} %lt.22, f32[8,256,256]{2,1,0:T(8,128)} %get-tuple-element.178, s32[]{:T(128)} %get-tuple-element.168), kind=kOutput, calls=%fused_computation.2.clone.1 | convolution fusion | flops 806354944 | bytes 4458496 | tf_op jit(solution)/shard_map/while/body/eval_jaxpr/dot_general | solution.py:35
  131.2 1.3 constant_dynamic-slice_fusion.2
  132.5 0.3 copy.13
  132.9 1.2 copy.21
  134.1 3.1 %fusion.26 = f32[1024,256]{0,1:T(8,128)} fusion(f32[1,1024,256]{1,2,0:T(8,128)S(1)} %copy.13, f32[1024,256]{0,1:T(8,128)S(1)} %copy.21, pred[]{:T(512)S(6)} %compare.3, pred[]{:T(512)S(6)} %lt.22, f32[8,256,256]{2,1,0:T(8,128)} %get-tuple-element.178, s32[]{:T(128)} %get-tuple-element.168), kind=kOutput, calls=%fused_computation.2.clone.1 | convolution fusion | flops 806354944 | bytes 4458496 | tf_op jit(solution)/shard_map/while/body/eval_jaxpr/dot_general | solution.py:35
  137.2 1.3 constant_dynamic-slice_fusion.2
  138.5 0.3 copy.13
  138.8 1.2 copy.21
  140.0 3.1 %fusion.26 = f32[1024,256]{0,1:T(8,128)} fusion(f32[1,1024,256]{1,2,0:T(8,128)S(1)} %copy.13, f32[1024,256]{0,1:T(8,128)S(1)} %copy.21, pred[]{:T(512)S(6)} %compare.3, pred[]{:T(512)S(6)} %lt.22, f32[8,256,256]{2,1,0:T(8,128)} %get-tuple-element.178, s32[]{:T(128)} %get-tuple-element.168), kind=kOutput, calls=%fused_computation.2.clone.1 | convolution fusion | flops 806354944 | bytes 4458496 | tf_op jit(solution)/shard_map/while/body/eval_jaxpr/dot_general | solution.py:35
  143.1 1.3 constant_dynamic-slice_fusion.2
  144.4 0.3 copy.13
  144.7 1.2 copy.21
  146.0 3.1 %fusion.26 = f32[1024,256]{0,1:T(8,128)} fusion(f32[1,1024,256]{1,2,0:T(8,128)S(1)} %copy.13, f32[1024,256]{0,1:T(8,128)S(1)} %copy.21, pred[]{:T(512)S(6)} %compare.3, pred[]{:T(512)S(6)} %lt.22, f32[8,256,256]{2,1,0:T(8,128)} %get-tuple-element.178, s32[]{:T(128)} %get-tuple-element.168), kind=kOutput, calls=%fused_computation.2.clone.1 | convolution fusion | flops 806354944 | bytes 4458496 | tf_op jit(solution)/shard_map/while/body/eval_jaxpr/dot_general | solution.py:35
  149.0 1.3 constant_dynamic-slice_fusion.2
  150.3 0.3 copy.13
  150.7 1.2 copy.21
  151.9 3.1 %fusion.26 = f32[1024,256]{0,1:T(8,128)} fusion(f32[1,1024,256]{1,2,0:T(8,128)S(1)} %copy.13, f32[1024,256]{0,1:T(8,128)S(1)} %copy.21, pred[]{:T(512)S(6)} %compare.3, pred[]{:T(512)S(6)} %lt.22, f32[8,256,256]{2,1,0:T(8,128)} %get-tuple-element.178, s32[]{:T(128)} %get-tuple-element.168), kind=kOutput, calls=%fused_computation.2.clone.1 | convolution fusion | flops 806354944 | bytes 4458496 | tf_op jit(solution)/shard_map/while/body/eval_jaxpr/dot_general | solution.py:35
  155.0 1.3 constant_dynamic-slice_fusion.2
  156.3 0.3 copy.13
  156.6 1.2 copy.21
  157.8 3.1 %fusion.26 = f32[1024,256]{0,1:T(8,128)} fusion(f32[1,1024,256]{1,2,0:T(8,128)S(1)} %copy.13, f32[1024,256]{0,1:T(8,128)S(1)} %copy.21, pred[]{:T(512)S(6)} %compare.3, pred[]{:T(512)S(6)} %lt.22, f32[8,256,256]{2,1,0:T(8,128)} %get-tuple-element.178, s32[]{:T(128)} %get-tuple-element.168), kind=kOutput, calls=%fused_computation.2.clone.1 | convolution fusion | flops 806354944 | bytes 4458496 | tf_op jit(solution)/shard_map/while/body/eval_jaxpr/dot_general | solution.py:35
  160.9 1.3 constant_dynamic-slice_fusion.2
  162.2 0.3 copy.13
  162.5 1.2 copy.21
  163.8 3.1 %fusion.26 = f32[1024,256]{0,1:T(8,128)} fusion(f32[1,1024,256]{1,2,0:T(8,128)S(1)} %copy.13, f32[1024,256]{0,1:T(8,128)S(1)} %copy.21, pred[]{:T(512)S(6)} %compare.3, pred[]{:T(512)S(6)} %lt.22, f32[8,256,256]{2,1,0:T(8,128)} %get-tuple-element.178, s32[]{:T(128)} %get-tuple-element.168), kind=kOutput, calls=%fused_computation.2.clone.1 | convolution fusion | flops 806354944 | bytes 4458496 | tf_op jit(solution)/shard_map/while/body/eval_jaxpr/dot_general | solution.py:35
  166.8 1.3 constant_dynamic-slice_fusion.2
  168.1 0.3 copy.13
  168.5 1.2 copy.21
  169.7 3.1 %fusion.26 = f32[1024,256]{0,1:T(8,128)} fusion(f32[1,1024,256]{1,2,0:T(8,128)S(1)} %copy.13, f32[1024,256]{0,1:T(8,128)S(1)} %copy.21, pred[]{:T(512)S(6)} %compare.3, pred[]{:T(512)S(6)} %lt.22, f32[8,256,256]{2,1,0:T(8,128)} %get-tuple-element.178, s32[]{:T(128)} %get-tuple-element.168), kind=kOutput, calls=%fused_computation.2.clone.1 | convolution fusion | flops 806354944 | bytes 4458496 | tf_op jit(solution)/shard_map/while/body/eval_jaxpr/dot_general | solution.py:35
  172.8 0.0 copy-done.2
  172.8 3.4 %convolution_add_fusion = f32[1024,256]{1,0:T(8,128)S(1)} fusion(f32[1024,256]{1,0:T(8,128)} %convolution_add_fusion.1, f32[1024,256]{0,1:T(8,128)} %get-tuple-element.96, f32[256,256]{1,0:T(8,128)S(1)} %copy-done.2), kind=kOutput, calls=%fused_computation.13 | convolution fusion | flops 805568512 | bytes 3407872 | tf_op jit(solution)/shard_map/dot_general | solution.py:35
  176.2 0.0 copy-done.3
  176.2 0.0 copy-start.1
  176.2 0.0 copy-start.5
  176.2 2.0 fusion.10
  178.2 0.0 reduce-scatter.2.cloned.1.call-update
  178.2 36.2 %reduce-scatter.2.cloned.1.call-done = f32[128,256]{1,0:T(8,128)} async-done(((f32[1024,256]{1,0:T(8,128)}), f32[128,256]{1,0:T(8,128)}) %reduce-scatter.2.cloned.1.call-update) | async-done | bytes 131088 | tf_op jit(solution)/shard_map/reduce_scatter | solution.py:58
  214.4 0.0 copy-done.5
  214.4 1.6 sub.3
  216.0 0.0 copy-done.1
  (2 shorter events, 0.0 us)
Async XLA Ops:
  7.2 32.3 %copy-start = (f32[1024,256]{1,0:T(8,128)S(1)}, f32[1024,256]{1,0:T(8,128)}, u32[]{:S(2)}) copy-start(f32[1024,256]{1,0:T(8,128)} %param.9) | copy-start | bytes 3145732
  7.2 34.2 %copy-start.4 = (f32[1024,256]{1,0:T(8,128)S(1)}, f32[1024,256]{1,0:T(8,128)}, u32[]{:S(2)}) copy-start(f32[1024,256]{1,0:T(8,128)} %param.8) | copy-start | bytes 3145732
  7.2 61.2 %all-gather.5.cloned.1.call-start = ((), (), s32[]{:S(2)}) async-start(), calls=%async_computation.2 | async-start | bytes 2359296 | tf_op jit(solution)/shard_map/all_gather | solution.py:9
  39.4 85.9 %all-gather.7.cloned.1.call-start = ((), (), s32[]{:S(2)}) async-start(), calls=%async_computation.3 | async-start | bytes 9437184 | tf_op jit(solution)/shard_map/all_gather | solution.py:9
  41.4 2.1 copy-start.6
  43.4 170.9 %reduce-scatter.2.cloned.1.call-start = ((), (), s32[]{:S(2)}) async-start(), calls=%async_computation.1 | async-start | bytes 1179648 | tf_op jit(solution)/shard_map/reduce_scatter | solution.py:58
  125.3 47.5 %copy-start.2 = (f32[256,256]{1,0:T(8,128)S(1)}, f32[256,256]{1,0:T(8,128)}, u32[]{:S(2)}) copy-start(f32[256,256]{1,0:T(8,128)} %convolution_negate_fusion) | copy-start | bytes 786436
  172.8 3.4 %copy-start.3 = (f32[256,256]{1,0:T(8,128)S(1)}, f32[256,256]{1,0:T(8,128)}, u32[]{:S(2)}) copy-start(f32[256,256]{1,0:T(8,128)} %all_gather.27) | copy-start | bytes 786436
  176.2 39.8 %copy-start.1 = (f32[1024,256]{1,0:T(8,128)}, f32[1024,256]{1,0:T(8,128)S(1)}, u32[]{:S(2)}) copy-start(f32[1024,256]{1,0:T(8,128)S(1)} %convolution_add_fusion) | copy-start | bytes 3145732
  176.2 38.2 %copy-start.5 = (f32[128,256]{1,0:T(8,128)S(1)}, f32[128,256]{1,0:T(8,128)}, u32[]{:S(2)}) copy-start(f32[128,256]{1,0:T(8,128)} %param.13) | copy-start | bytes 393220
Sparse Core Ops, SparseCore 0:
  39.5 28.8 all-gather.4
  70.8 54.3 all-gather.6
  178.3 36.0 reduce-scatter.1
where the time goes:
time: 224 us; the launch traced here: 222 us
  waiting for transfers between devices  103 us (46%)
  blocking collectives  45.7 us (20%)
  matrix products  35.1 us (16%)
  local copies, waits for them, and re-layouts  22.9 us (10%)
  between operations  13.8 us (6%)
    all_gather x2, waiting for transfers between devices, entering(): everything = jax.tree.map(lambda part: lax.all_gather(part, axis), array)  66.8 us
    reduce_scatter x1, waiting for transfers between devices, on_device(): lax.psum_scatter(plain_dot(factor, coupling), 'panel', scatter_dimension=...  36.2 us
    dot_general x12, matrix products, plain_dot(): jnp.dot(left, right, precision=lax.Precision.HIGHEST, preferred_element_t...  33.1 us
    all_gather x1, blocking collectives, on_device(): lax.all_gather(diag_inverse, 'row', axis=0, tiled=True)  16 us
    all_gather x1, blocking collectives, on_device(): lax.all_gather(tail_coupling, 'row', axis=0, tiled=True)  14.9 us
    all_gather x1, blocking collectives, on_device(): lax.all_gather(sub_block, 'row', axis=0, tiled=True)  14.8 us
    dynamic_slice x16, local copies, waits for them, and re-layouts, step(): new = combine(before, jax.tree.map(lambda part: part[k], everything))  13 us
    while x8, local copies, waits for them, and re-layouts  9.81 us
  transfers between devices with their start and end apart: 3, of which 3 were waited for; matrix products, arithmetic and copies ran while one was open for 2% of the time, Pallas kernels for 0%

commit v1 on v0

v1 whole, which is shorter than its diff:
```python
import functools

import jax
import jax.numpy as jnp
from jax import lax
from jax.experimental import pallas as pl
from jax.experimental.pallas import tpu as pltpu
from jax.sharding import PartitionSpec as P

CHUNKS = 2
NT = (((1,), (1,)), ((), ()))
NN = (((1,), (0,)), ((), ()))
VMEM = pl.BlockSpec(memory_space=pltpu.VMEM)


def split(x):
    high = x.astype(jnp.bfloat16)
    return high, (x - high.astype(jnp.float32)).astype(jnp.bfloat16)


def dot3(left, right, dims):
    dot = functools.partial(lax.dot_general, dimension_numbers=dims, preferred_element_type=jnp.float32)
    return dot(left[0], right[0]) + (dot(left[0], right[1]) + dot(left[1], right[0]))


def chip_and_core():
    panel = lax.axis_index("panel")
    return lax.div(panel, 2), lax.rem(panel, 2)


def call(kernel, outs, args, scratch=(), products=0):
    size = sum(a.size * 4 for a in args) + sum(o[0] * o[1] * 4 for o in outs)
    return pl.pallas_call(
        kernel,
        out_shape=[jax.ShapeDtypeStruct(o, jnp.float32) for o in outs],
        in_specs=[VMEM] * len(args),
        out_specs=[VMEM] * len(outs),
        scratch_shapes=list(scratch),
        compiler_params=pltpu.CompilerParams(vmem_limit_bytes=40 << 20),
        cost_estimate=pl.CostEstimate(flops=6 * products, bytes_accessed=size, transcendentals=0),
    )(*args)


def shard_rows(count, shift, height):
    start = lax.rem(lax.axis_index("row") + count - shift, count) * height
    return pl.ds(pl.multiple_of(start, height), height)


def take(refs, count):
    return [next(refs) for _ in range(count)]


def prepare(count, chunks, *refs):
    refs = iter(refs)
    own, other = take(refs, count), take(refs, count)
    keep, got, bound, coupling = take(refs, 4)
    part_ref, map_ref, both_ref, coupling_out = take(refs, 4)
    carry_refs = take(refs, chunks)
    inverse, beneath = take(refs, 2)
    chip, core = chip_and_core()
    coupling_out[...] = coupling[...]
    height = own[0].shape[0] // 2
    for shift in range(count):
        rows = shard_rows(count, shift, height)
        for slot, shards in ((core, own), (1 - core, other)):
            inverse[slot, rows, :] = shards[shift][:height, :]
            beneath[slot, rows, :] = shards[shift][height:, :]
    inverse_a, inverse_b = split(inverse[0]), split(inverse[1])
    map_a = dot3(inverse_a, split(beneath[0]), NN)
    map_b = dot3(inverse_b, split(beneath[1]), NN)
    parts_a, parts_b = split(map_a), split(map_b)
    map_ref[...] = map_a
    both_ref[...] = dot3(parts_b, parts_a, NN)
    first = core == 0
    part_ref[...] = dot3(split(jnp.where(first, keep[...], got[...])), inverse_a, NT)

    @pl.when(chip == 0)
    def _():
        part_ref[...] -= dot3(split(bound[...]), parts_a, NT)

    carry = dot3(split(jnp.where(first, got[...], keep[...])), inverse_b, NT)
    carry -= dot3(split(part_ref[...]), parts_b, NT)
    height = carry.shape[0] // chunks
    for k in range(chunks):
        carry_refs[k][...] = carry[k * height : (k + 1) * height]


def inclusive(carry, prior, both, out):
    out[...] = carry[...] + dot3(split(prior[...]), split(both[...]), NT)


def absorb(half, prior, across, arrived, put):
    total = arrived[0][...]
    for more in arrived[1:]:
        total = total + more[...]
    chip, _ = chip_and_core()
    inner = lax.rem(chip, half) != 0

    @pl.when(inner)
    def _():
        put(prior[...] + dot3(split(total), split(across[...]), NT))

    @pl.when(jnp.logical_not(inner))
    def _():
        put(prior[...] + total)


def advance(half, prior, across, *refs):
    *arrived, out = refs

    def put(value):
        out[...] = value

    absorb(half, prior, across, arrived, put)


def extend(half, across, arrived, out):
    chip, _ = chip_and_core()
    inner = lax.rem(chip, half) != 0
    upper = lax.rem(chip, 2 * half) >= half
    out[...] = across[...]

    @pl.when(jnp.logical_and(upper, inner))
    def _():
        out[...] = dot3(split(across[...]), split(arrived[...]), NN)

    @pl.when(jnp.logical_and(upper, jnp.logical_not(inner)))
    def _():
        out[...] = arrived[...]


def joined(half, both, across, out):
    chip, _ = chip_and_core()
    out[...] = both[...]

    @pl.when(lax.rem(chip, half) != 0)
    def _():
        out[...] = dot3(split(both[...]), split(across[...]), NN)


def finish(count, chunks, half, arrivals, *refs):
    refs = iter(refs)
    part, map_ref, both = take(refs, 3)
    across = next(refs) if arrivals else None
    carries, priors = take(refs, chunks), take(refs, chunks)
    arrived = [take(refs, arrivals) for _ in range(chunks)]
    own, other = take(refs, count), take(refs, count)
    stay, leave, tail, coupling, entering = take(refs, 5)
    _, core = chip_and_core()
    height = own[0].shape[0]
    for shift in range(count):
        rows = shard_rows(count, shift, height)
        coupling[core, rows, :] = own[shift][...]
        coupling[1 - core, rows, :] = other[shift][...]
    map_a, map_ab = split(map_ref[...]), split(both[...])
    coupling_a, coupling_b = split(coupling[0]), split(coupling[1])
    first = core == 0
    height = carries[0].shape[0]
    for k in range(chunks):
        rows = slice(k * height, (k + 1) * height)

        def put(value, rows=rows):
            entering[rows, :] = value

        if arrivals:
            absorb(half, priors[k], across, arrived[k], put)
        else:
            put(priors[k][...])
        incoming = split(entering[rows, :])
        solved_a = part[rows, :] - dot3(incoming, map_a, NT)
        solved_b = carries[k][...] + dot3(incoming, map_ab, NT)
        stay[rows, :] = jnp.where(first, solved_a, solved_b)
        leave[rows, :] = jnp.where(first, solved_b, solved_a)
        tail[rows, :] = dot3(split(solved_a), coupling_a, NN) + dot3(split(solved_b), coupling_b, NN)


def between_chips(value, pairs):
    pairs = [(2 * a + core, 2 * b + core) for a, b in pairs for core in (0, 1)]
    return lax.ppermute(value, "panel", pairs)


def to_other_core(value):
    return lax.ppermute(value, "panel", [(q, q ^ 1) for q in range(lax.axis_size("panel"))])


def gather_rows(value, count):
    shifts = range(1, count)
    return [value] + [lax.ppermute(value, "row", [(j, (j + s) % count) for j in range(count)]) for s in shifts]


def on_device(slab, boundary, diag_inverse, sub_block, tail_coupling, tail_cols):
    panels, count = lax.axis_size("panel"), lax.axis_size("row")
    chips = panels // 2
    chip, core = chip_and_core()
    rows, width = slab.shape
    piece = rows // panels
    held = chips * piece

    def blocks(array, parity):
        array = array.reshape(chips, 2, piece, width)
        return lax.dynamic_index_in_dim(array, parity, 1, keepdims=False).reshape(held, width)

    own = gather_rows(jnp.concatenate([diag_inverse, sub_block]), count)
    keep, got = blocks(slab, core), to_other_core(blocks(slab, 1 - core))
    other = [to_other_core(shard) for shard in own]
    square = (width, width)
    part = (held, width)
    slice_shape = (held // CHUNKS, width)
    own_part, map_a, both, coupling, *carries = call(
        functools.partial(prepare, count, CHUNKS),
        [part, square, square, tail_coupling.shape] + [slice_shape] * CHUNKS,
        [*own, *other, keep, got, blocks(boundary, core), tail_coupling],
        [pltpu.VMEM((2, *square), jnp.float32)] * 2,
        width * width * (3 * width + 4 * held),
    )

    priors, across = None, None
    half = 1
    while True:
        last = 2 * half >= chips
        sources = [s for s in range(half - 1, chips - 1, 2 * half)]
        inner = [s for s in sources if s >= half]
        arrived = []
        for k in range(CHUNKS):
            value = carries[k]
            if priors is not None:
                (value,) = call(inclusive, [slice_shape], [value, priors[k], both], (), width * value.size)
            arrived.append(
                [
                    between_chips(value, [(s, s + 1 + j) for s in sources if s + 1 + j < chips])
                    for j in reversed(range(half))
                ]
            )
        step_map = None
        if not last:
            send = both
            if across is not None:
                (send,) = call(functools.partial(joined, half), [square], [both, across], (), width**3)
            step_map = sum(between_chips(send, [(s, s + 1 + j) for s in inner if s + 1 + j < chips]) for j in range(half))
        if last and priors is not None:
            break
        if priors is None:
            priors = [a[0] for a in arrived]
            across = step_map
        else:
            advanced = functools.partial(advance, half)
            priors = [
                call(advanced, [slice_shape], [priors[k], across, *arrived[k]], (), width * priors[k].size)[0]
                for k in range(CHUNKS)
            ]
            (across,) = call(functools.partial(extend, half), [square], [across, step_map], (), width**3)
        if last:
            arrived = [[] for _ in range(CHUNKS)]
            break
        half *= 2

    own = gather_rows(coupling, count)
    other = [to_other_core(shard) for shard in own]
    arrivals = len(arrived[0])
    stay, leave, tail = call(
        functools.partial(finish, count, CHUNKS, half, arrivals),
        [part] * 3,
        [own_part, map_a, both]
        + ([across] if arrivals else [])
        + [*carries, *priors]
        + [a for chunk in arrived for a in chunk]
        + [*own, *other],
        [pltpu.VMEM((2, *square), jnp.float32), pltpu.VMEM(part, jnp.float32)],
        5 * width * width * held,
    )
    tail = tail.reshape(chips, piece, width)

    def tail_of(index):
        return lax.dynamic_index_in_dim(tail, index, 0, keepdims=False)

    summed = tail_of(chip)
    for shift in reversed(range(1, chips)):
        if chips & (chips - 1) == 0:
            there, pairs = chip ^ shift, [(a, a ^ shift) for a in range(chips)]
        else:
            there, pairs = lax.rem(chip + shift, chips), [(a, (a + shift) % chips) for a in range(chips)]
        summed = summed + between_chips(tail_of(there), pairs)
    came = to_other_core(leave)
    first = core == 0
    parts = [part.reshape(chips, 1, piece, width) for part in (jnp.where(first, stay, came), jnp.where(first, came, stay))]
    factor = jnp.concatenate(parts, axis=1).reshape(rows, width)
    return factor, tail_cols - summed


def solution(mesh):
    placed = (
        P("row", "panel"),
        P("row", None),
        P(("panel", "row"), None),
        P(("panel", "row"), None),
        P(("panel", "row"), None),
        P(("row", "panel"), None),
    )
    return jax.shard_map(
        on_device,
        mesh=mesh,
        in_specs=placed,
        out_specs=(P("row", "panel"), P(("row", "panel"), None)),
        check_vma=False,
    )
```

time: 224 us -> 72.6 us (0.32)
  waiting for transfers between devices: 103 us -> 19.8 us
  blocking collectives: 45.7 us -> 0 us
  starting transfers between devices: 0.12 us -> 41.6 us
  matrix products: 35.1 us -> 0 us
  local copies, waits for them, and re-layouts: 22.9 us -> 3.53 us
  between operations: 13.8 us -> 0.93 us
  Pallas kernels: 0 us -> 4.55 us
    all_gather x2 -> x0, waiting for transfers between devices: 66.8 us -> none  [entering(): everything = jax.tree.map(lambda part: lax.all_gather(part, axis), array)]
    all_gather x3 -> x0, blocking collectives: 45.7 us -> none  [the longest x1 16 us: on_device(): lax.all_gather(diag_inverse, 'row', axis=0, tiled=True)]
    ppermute x0 -> x26, starting transfers between devices: none -> 41.6 us  [the longest x10 27.5 us: between_chips(): return lax.ppermute(value, 'panel', pairs)]
    reduce_scatter x1 -> x0, waiting for transfers between devices: 36.2 us -> none  [on_device(): lax.psum_scatter(plain_dot(factor, coupling), 'panel', scatter_dimension=...]
    dot_general x13 -> x0, matrix products: 35.1 us -> none  [the longest x12 33.1 us: plain_dot(): jnp.dot(left, right, precision=lax.Precision.HIGHEST, preferred_element_t...]
    ppermute x0 -> x26, waiting for transfers between devices: none -> 19.8 us  [the longest x6 11.8 us: gather_rows(): lax.ppermute(value, 'row', [(j, (j + s) % count) for j in range(count)])]
    dynamic_slice x16 -> x2, local copies, waits for them, and re-layouts: 13 us -> 1.41 us  [blocks(): lax.dynamic_index_in_dim(array, parity, 1, keepdims=False)]
    while x8 -> x0, local copies, waits for them, and re-layouts: 9.81 us -> none
  transfers between devices with their start and end apart: 3 -> 26, of which waited for: 3 -> 10; matrix products, arithmetic and copies ran while one was open for 2% -> 3% of each run, Pallas kernels for 0% -> 1%
where the time goes in v1:
time: 72.6 us; the launch traced here: 72.3 us
  starting transfers between devices  41.6 us (57%)
  waiting for transfers between devices  19.8 us (27%)
  Pallas kernels  4.55 us (6%)
  local copies, waits for them, and re-layouts  3.53 us (5%)
  other arithmetic  1.8 us (2%)
  between operations  0.93 us (1%)
    ppermute x10, starting transfers between devices, between_chips(): return lax.ppermute(value, 'panel', pairs)  27.5 us
    ppermute x6, starting transfers between devices, gather_rows(): lax.ppermute(value, 'row', [(j, (j + s) % count) for j in range(count)])  12.5 us
    ppermute x6, waiting for transfers between devices, gather_rows(): lax.ppermute(value, 'row', [(j, (j + s) % count) for j in range(count)])  11.8 us
    ppermute x10, waiting for transfers between devices, between_chips(): return lax.ppermute(value, 'panel', pairs)  7.02 us
    pallas_call x4, Pallas kernels, call(): pl.pallas_call(kernel, out_shape=[jax.ShapeDtypeStruct(o, jnp.float32) fo...  4.55 us
    sub x1, other arithmetic, on_device(): return (factor, tail_cols - summed)  1.66 us
    ppermute x10, starting transfers between devices, to_other_core(): lax.ppermute(value, 'panel', [(q, q ^ 1) for q in range(lax.axis_size('pa...  1.63 us
  transfers between devices with their start and end apart: 26, of which 10 were waited for; matrix products, arithmetic and copies ran while one was open for 3% of the time, Pallas kernels for 1%

profile of v1, /device:TPU:0, one launch (start us, length us, event | category | flops | bytes accessed | tf_op | source)
XLA Modules:
  0.0 72.3 jit_solution(214763596960478502)
XLA Ops:
  0.6 0.0 copy-start
  0.7 1.4 %constant_dynamic-slice_fusion.1 = (f32[4,1,128,256]{3,2,1,0:T(8,128)S(1)}, f32[4,1,128,256]{3,2,1,0:T(8,128)S(1)}) fusion(f32[4,2,128,256]{3,2,1,0:T(8,128)} %bitcast.37, s32[]{:T(128)S(6)} %select_n.35, s32[]{:T(128)S(6)} %select_n.34), kind=kLoop, calls=%fused_computation.13 | loop fusion | bytes 2097160 | tf_op jit(solution)/shard_map/jit(dynamic_index_in_dim)/dynamic_slice | solution.py:201
  2.0 0.0 copy-start.4
  2.1 0.5 collective-permute-start.7
  2.6 0.3 copy-done.4
  2.9 3.0 %collective-permute-start = (f32[128,256]{1,0:T(8,128)S(1)}, f32[128,256]{1,0:T(8,128)S(1)}, u32[]{:S(2)}, u32[]{:S(2)}) collective-permute-start(f32[128,256]{1,0:T(8,128)S(1)} %constant_dynamic-update-slice_fusion.refs_0_), channel_id=1, source_target_pairs={{0,1},{1,2},{2,3},{3,0},{4,5},{5,6},{6,7},{7,4},{8,9},{9,10},{10,1... | collective-permute-start | bytes 393224 | tf_op jit(solution)/shard_map/ppermute | solution.py:188
  5.9 2.6 %collective-permute-start.1 = (f32[128,256]{1,0:T(8,128)S(1)}, f32[128,256]{1,0:T(8,128)S(1)}, u32[]{:S(2)}, u32[]{:S(2)}) collective-permute-start(f32[128,256]{1,0:T(8,128)S(1)} %constant_dynamic-update-slice_fusion.refs_0_), channel_id=1, source_target_pairs={{0,2},{1,3},{2,0},{3,1},{4,6},{5,7},{6,4},{7,5},{8,10},{9,11},{10,... | collective-permute-start | bytes 393224 | tf_op jit(solution)/shard_map/ppermute | solution.py:188
  8.5 1.3 %collective-permute-start.2 = (f32[128,256]{1,0:T(8,128)S(1)}, f32[128,256]{1,0:T(8,128)S(1)}, u32[]{:S(2)}, u32[]{:S(2)}) collective-permute-start(f32[128,256]{1,0:T(8,128)S(1)} %constant_dynamic-update-slice_fusion.refs_0_), channel_id=1, source_target_pairs={{0,3},{1,0},{2,1},{3,2},{4,7},{5,4},{6,5},{7,6},{8,11},{9,8},{10,9... | collective-permute-start | bytes 393224 | tf_op jit(solution)/shard_map/ppermute | solution.py:188
  9.9 0.0 collective-permute-start.3
  9.9 2.5 %collective-permute-done.refs_1_ = f32[128,256]{1,0:T(8,128)S(1)} collective-permute-done((f32[128,256]{1,0:T(8,128)S(1)}, f32[128,256]{1,0:T(8,128)S(1)}, u32[]{:S(2)}, u32[]{:S(2)}) %collective-permute-start) | collective-permute-done | bytes 131104 | tf_op jit(solution)/shard_map/ppermute | solution.py:188
  12.4 0.0 collective-permute-start.4
  12.4 4.8 %collective-permute-done.1.refs_2_ = f32[128,256]{1,0:T(8,128)S(1)} collective-permute-done((f32[128,256]{1,0:T(8,128)S(1)}, f32[128,256]{1,0:T(8,128)S(1)}, u32[]{:S(2)}, u32[]{:S(2)}) %collective-permute-start.1) | collective-permute-done | bytes 131104 | tf_op jit(solution)/shard_map/ppermute | solution.py:188
  17.2 0.0 collective-permute-start.5
  17.2 0.0 collective-permute-done.2.refs_3_
  17.2 0.5 collective-permute-start.6
  17.7 0.0 collective-permute-done.3.refs_4_
  17.7 0.0 collective-permute-done.4.refs_5_
  17.7 0.8 %collective-permute-done.5.refs_6_ = f32[128,256]{1,0:T(8,128)S(1)} collective-permute-done((f32[128,256]{1,0:T(8,128)S(1)}, f32[128,256]{1,0:T(8,128)S(1)}, u32[]{:S(2)}, u32[]{:S(2)}) %collective-permute-start.5) | collective-permute-done | bytes 131104 | tf_op jit(solution)/shard_map/ppermute | solution.py:183
  18.5 0.2 collective-permute-done.6.refs_7_
  18.7 0.0 collective-permute-done.7.refs_9_
  18.7 1.9 %shard_map.77 = (f32[512,256]{1,0:T(8,128)S(1)}, f32[256,256]{1,0:T(8,128)S(1)}, f32[256,256]{1,0:T(8,128)S(1)}, f32[64,256]{1,0:T(8,128)S(1)}, f32[256,256]{1,0:T(8,128)S(1)}, /*index=5*/f32[256,256]{1,0:T(8,128)S(1)}) custom-call(f32[128,256]{1,0:T(8,128)S(1)} %constant_dynamic-update-slice_fusion.refs_0_, f32[128,256]{1,0:T(8,128)S(1)} %collective-permute-done.refs_1_, ...), custom_call_target="tpu_custom_call" | custom-call | flops 1107296256 | bytes 4325376 | tf_op jit(solution)/shard_map/pallas_call | solution.py:33
  20.6 3.0 %collective-permute-start.10 = (f32[256,256]{1,0:T(8,128)S(1)}, f32[256,256]{1,0:T(8,128)S(1)}, u32[]{:S(2)}, u32[]{:S(2)}) collective-permute-start(f32[256,256]{1,0:T(8,128)S(1)} %get-tuple-element.15.carry.refs_5_), channel_id=1, source_target_pairs={{0,8},{4,12},{16,24},{20,28},{1,9},{5,13},{17,25},{21,29},{2,10},{... | collective-permute-start | bytes 786440 | tf_op jit(solution)/shard_map/ppermute | solution.py:179
  23.6 1.3 %collective-permute-start.9 = (f32[256,256]{1,0:T(8,128)S(1)}, f32[256,256]{1,0:T(8,128)S(1)}, u32[]{:S(2)}, u32[]{:S(2)}) collective-permute-start(f32[256,256]{1,0:T(8,128)S(1)} %get-tuple-element.14.carry.refs_4_), channel_id=1, source_target_pairs={{0,8},{4,12},{16,24},{20,28},{1,9},{5,13},{17,25},{21,29},{2,10},{... | collective-permute-start | bytes 786440 | tf_op jit(solution)/shard_map/ppermute | solution.py:179
  25.0 3.1 %collective-permute-start.15 = (f32[64,256]{1,0:T(8,128)S(1)}, f32[64,256]{1,0:T(8,128)S(1)}, u32[]{:S(2)}, u32[]{:S(2)}) collective-permute-start(f32[64,256]{1,0:T(8,128)S(1)} %get-tuple-element.16.refs_12_), channel_id=1, source_target_pairs={{0,1},{1,2},{2,3},{3,0},{4,5},{5,6},{6,7},{7,4},{8,9},{9,10},{10,1... | collective-permute-start | bytes 196616 | tf_op jit(solution)/shard_map/ppermute | solution.py:188
  28.1 1.8 %collective-permute-start.16 = (f32[64,256]{1,0:T(8,128)S(1)}, f32[64,256]{1,0:T(8,128)S(1)}, u32[]{:S(2)}, u32[]{:S(2)}) collective-permute-start(f32[64,256]{1,0:T(8,128)S(1)} %get-tuple-element.16.refs_12_), channel_id=1, source_target_pairs={{0,2},{1,3},{2,0},{3,1},{4,6},{5,7},{6,4},{7,5},{8,10},{9,11},{10,... | collective-permute-start | bytes 196616 | tf_op jit(solution)/shard_map/ppermute | solution.py:188
  29.9 0.6 collective-permute-start.17
  30.5 1.8 %collective-permute-done.15.refs_13_ = f32[64,256]{1,0:T(8,128)S(1)} collective-permute-done((f32[64,256]{1,0:T(8,128)S(1)}, f32[64,256]{1,0:T(8,128)S(1)}, u32[]{:S(2)}, u32[]{:S(2)}) %collective-permute-start.15) | collective-permute-done | bytes 65568 | tf_op jit(solution)/shard_map/ppermute | solution.py:188
  32.3 0.0 collective-permute-start.18
  32.3 2.2 %collective-permute-done.16.refs_14_ = f32[64,256]{1,0:T(8,128)S(1)} collective-permute-done((f32[64,256]{1,0:T(8,128)S(1)}, f32[64,256]{1,0:T(8,128)S(1)}, u32[]{:S(2)}, u32[]{:S(2)}) %collective-permute-start.16) | collective-permute-done | bytes 65568 | tf_op jit(solution)/shard_map/ppermute | solution.py:188
  34.6 0.0 collective-permute-start.19
  34.6 0.5 collective-permute-done.17.refs_15_
  35.1 0.0 collective-permute-start.20
  35.1 0.0 collective-permute-done.10.prior.refs_7_
  35.1 0.5 collective-permute-start.21
  35.6 0.3 shard_map.79
  35.9 0.0 collective-permute-done.9.prior.refs_6_
  35.9 0.7 collective-permute-start.8
  36.6 0.3 shard_map.78
  36.9 0.0 collective-permute-done.18.refs_16_
  36.9 0.7 collective-permute-start.13
  37.6 0.0 collective-permute-done.19.refs_17_
  37.6 0.7 collective-permute-start.14
  38.3 0.0 collective-permute-done.20.refs_18_
  38.3 0.7 collective-permute-start.11
  39.0 0.0 collective-permute-done.21.refs_19_
  39.0 0.7 collective-permute-start.12
  39.7 0.0 collective-permute-done.8.refs_3_
  39.7 0.0 collective-permute-done.13.refs_10_
  39.7 0.0 collective-permute-done.14.refs_11_
  39.7 0.0 collective-permute-done.11.refs_8_
  39.8 2.0 %shard_map.80 = (f32[512,256]{1,0:T(8,128)S(1)}, f32[512,256]{1,0:T(8,128)S(1)}, f32[512,256]{1,0:T(8,128)S(1)}) custom-call(f32[512,256]{1,0:T(8,128)S(1)} %get-tuple-element.11.refs_0_, f32[256,256]{1,0:T(8,128)S(1)} %get-tuple-element.12.refs_1_, f32[256,256]{1,0:T(8,128)S(1)} %get-tuple-element.13.both.refs_2_, ...), custom_call_target="tpu_custom_call" | custom-call | flops 1006632960 | bytes 5505024 | tf_op jit(solution)/shard_map/pallas_call | solution.py:33
  41.8 0.1 collective-permute-start.22
  41.9 0.0 copy-start.2
  41.9 0.7 %dynamic-slice_bitcast_fusion.2 = (f32[128,256]{1,0:T(8,128)}, f32[128,256]{1,0:T(8,128)S(1)}, f32[128,256]{1,0:T(8,128)}) fusion(f32[4,128,256]{2,1,0:T(8,128)S(1)} %bitcast.30, s32[]{:T(128)S(6)} %select_n.39, s32[]{:T(128)S(6)} %select_n.41, s32[]{:T(128)S(6)} %select_n.40), kind=kLoop, calls=%fused_computation.9 | loop fusion | bytes 786444 | tf_op jit(solution)/shard_map/jit(dynamic_index_in_dim)/squeeze | solution.py:274
  42.6 16.4 %collective-permute-start.23 = (f32[128,256]{1,0:T(8,128)}, f32[128,256]{1,0:T(8,128)S(1)}, u32[]{:S(2)}, u32[]{:S(2)}) collective-permute-start(f32[128,256]{1,0:T(8,128)} %get-tuple-element.24), channel_id=1, source_target_pairs={{0,24},{4,28},{8,16},{12,20},{16,8},{20,12},{24,0},{28,4},{1,25},{... | collective-permute-start | bytes 393224 | tf_op jit(solution)/shard_map/ppermute | solution.py:179
  59.0 2.0 %collective-permute-start.24 = (f32[128,256]{1,0:T(8,128)}, f32[128,256]{1,0:T(8,128)}, u32[]{:S(2)}, u32[]{:S(2)}) collective-permute-start(f32[128,256]{1,0:T(8,128)} %get-tuple-element.26), channel_id=1, source_target_pairs={{0,16},{4,20},{8,24},{12,28},{16,0},{20,4},{24,8},{28,12},{1,17},{... | collective-permute-start | bytes 393224 | tf_op jit(solution)/shard_map/ppermute | solution.py:179
  61.1 1.4 %collective-permute-start.25 = (f32[128,256]{1,0:T(8,128)S(1)}, f32[128,256]{1,0:T(8,128)}, u32[]{:S(2)}, u32[]{:S(2)}) collective-permute-start(f32[128,256]{1,0:T(8,128)S(1)} %get-tuple-element.25), channel_id=1, source_target_pairs={{0,8},{4,12},{8,0},{12,4},{16,24},{20,28},{24,16},{28,20},{1,9},{5... | collective-permute-start | bytes 393224 | tf_op jit(solution)/shard_map/ppermute | solution.py:179
  62.4 1.0 %collective-permute-done.23 = f32[128,256]{1,0:T(8,128)S(1)} collective-permute-done((f32[128,256]{1,0:T(8,128)}, f32[128,256]{1,0:T(8,128)S(1)}, u32[]{:S(2)}, u32[]{:S(2)}) %collective-permute-start.23) | collective-permute-done | bytes 131104 | tf_op jit(solution)/shard_map/ppermute | solution.py:179
  63.4 4.0 %collective-permute-done.24 = f32[128,256]{1,0:T(8,128)} collective-permute-done((f32[128,256]{1,0:T(8,128)}, f32[128,256]{1,0:T(8,128)}, u32[]{:S(2)}, u32[]{:S(2)}) %collective-permute-start.24) | collective-permute-done | bytes 131104 | tf_op jit(solution)/shard_map/ppermute | solution.py:179
  67.4 2.0 %collective-permute-done.25 = f32[128,256]{1,0:T(8,128)} collective-permute-done((f32[128,256]{1,0:T(8,128)S(1)}, f32[128,256]{1,0:T(8,128)}, u32[]{:S(2)}, u32[]{:S(2)}) %collective-permute-start.25) | collective-permute-done | bytes 131104 | tf_op jit(solution)/shard_map/ppermute | solution.py:179
  69.4 1.7 %fusion.2 = f32[128,256]{1,0:T(8,128)} fusion(f32[128,256]{1,0:T(8,128)S(1)} %copy-done.2, f32[128,256]{1,0:T(8,128)} %collective-permute-done.25, f32[128,256]{1,0:T(8,128)} %collective-permute-done.24, f32[128,256]{1,0:T(8,128)S(1)} %collective-permute-done.23, f32[4,128,256]{2,1,0:T(8,128)S(1)} %bitcast.31, s32[]{:T(128)S(6)} %select_n.38), kind=kLoop, calls=%fused_computation.6 | loop fusion | flops 131072 | bytes 786436 | tf_op jit(solution)/shard_map/sub | solution.py:287
  71.1 0.1 broadcast_select_fusion.1
  71.2 0.1 pad_maximum_fusion
  71.2 1.0 %copy.11 = f32[4,2,128,256]{3,2,1,0:T(8,128)} copy(f32[4,2,128,256]{3,2,0,1:T(8,128)S(1)} %pad_maximum_fusion) | data formatting | bytes 2097152 | tf_op jit(solution)/shard_map/concatenate | solution.py:286
  (11 shorter events, 0.1 us)
Async XLA Ops:
  0.6 17.0 %copy-start = (f32[1024,256]{1,0:T(8,128)S(1)}, f32[1024,256]{1,0:T(8,128)}, u32[]{:S(2)}) copy-start(f32[1024,256]{1,0:T(8,128)} %param.7) | copy-start | bytes 3145732
  0.7 1.9 %copy-start.3 = (f32[64,256]{1,0:T(8,128)S(1)}, f32[64,256]{1,0:T(8,128)}, u32[]{:S(2)}) copy-start(f32[64,256]{1,0:T(8,128)} %param.8) | copy-start | bytes 196612
  2.0 0.8 %copy-start.4 = (f32[64,256]{1,0:T(8,128)S(1)}, f32[64,256]{1,0:T(8,128)}, u32[]{:S(2)}) copy-start(f32[64,256]{1,0:T(8,128)} %param.9) | copy-start | bytes 196612
  2.1 16.6 %collective-permute-start.7 = (f32[512,256]{1,0:T(8,128)S(1)}, f32[512,256]{1,0:T(8,128)S(1)}, u32[]{:S(2)}, u32[]{:S(2)}) collective-permute-start(f32[512,256]{1,0:T(8,128)S(1)} %bitcast.38), channel_id=1, source_target_pairs={{0,4},{4,0},{8,12},{12,8},{16,20},{20,16},{24,28},{28,24},{1,5},{5... | collective-permute-start | bytes 1572872 | tf_op jit(solution)/shard_map/ppermute | solution.py:183
  2.9 9.5 %collective-permute-start = (f32[128,256]{1,0:T(8,128)S(1)}, f32[128,256]{1,0:T(8,128)S(1)}, u32[]{:S(2)}, u32[]{:S(2)}) collective-permute-start(f32[128,256]{1,0:T(8,128)S(1)} %constant_dynamic-update-slice_fusion.refs_0_), channel_id=1, source_target_pairs={{0,1},{1,2},{2,3},{3,0},{4,5},{5,6},{6,7},{7,4},{8,9},{9,10},{10,1... | collective-permute-start | bytes 393224 | tf_op jit(solution)/shard_map/ppermute | solution.py:188
  5.9 11.2 %collective-permute-start.1 = (f32[128,256]{1,0:T(8,128)S(1)}, f32[128,256]{1,0:T(8,128)S(1)}, u32[]{:S(2)}, u32[]{:S(2)}) collective-permute-start(f32[128,256]{1,0:T(8,128)S(1)} %constant_dynamic-update-slice_fusion.refs_0_), channel_id=1, source_target_pairs={{0,2},{1,3},{2,0},{3,1},{4,6},{5,7},{6,4},{7,5},{8,10},{9,11},{10,... | collective-permute-start | bytes 393224 | tf_op jit(solution)/shard_map/ppermute | solution.py:188
  8.5 8.6 %collective-permute-start.2 = (f32[128,256]{1,0:T(8,128)S(1)}, f32[128,256]{1,0:T(8,128)S(1)}, u32[]{:S(2)}, u32[]{:S(2)}) collective-permute-start(f32[128,256]{1,0:T(8,128)S(1)} %constant_dynamic-update-slice_fusion.refs_0_), channel_id=1, source_target_pairs={{0,3},{1,0},{2,1},{3,2},{4,7},{5,4},{6,5},{7,6},{8,11},{9,8},{10,9... | collective-permute-start | bytes 393224 | tf_op jit(solution)/shard_map/ppermute | solution.py:188
  9.9 7.9 %collective-permute-start.3 = (f32[128,256]{1,0:T(8,128)S(1)}, f32[128,256]{1,0:T(8,128)S(1)}, u32[]{:S(2)}, u32[]{:S(2)}) collective-permute-start(f32[128,256]{1,0:T(8,128)S(1)} %constant_dynamic-update-slice_fusion.refs_0_), channel_id=1, source_target_pairs={{0,4},{4,0},{8,12},{12,8},{16,20},{20,16},{24,28},{28,24},{1,5},{5... | collective-permute-start | bytes 393224 | tf_op jit(solution)/shard_map/ppermute | solution.py:183
  12.4 5.4 %collective-permute-start.4 = (f32[128,256]{1,0:T(8,128)S(1)}, f32[128,256]{1,0:T(8,128)S(1)}, u32[]{:S(2)}, u32[]{:S(2)}) collective-permute-start(f32[128,256]{1,0:T(8,128)S(1)} %collective-permute-done.refs_1_), channel_id=1, source_target_pairs={{0,4},{4,0},{8,12},{12,8},{16,20},{20,16},{24,28},{28,24},{1,5},{5... | collective-permute-start | bytes 393224 | tf_op jit(solution)/shard_map/ppermute | solution.py:183
  17.2 1.3 %collective-permute-start.5 = (f32[128,256]{1,0:T(8,128)S(1)}, f32[128,256]{1,0:T(8,128)S(1)}, u32[]{:S(2)}, u32[]{:S(2)}) collective-permute-start(f32[128,256]{1,0:T(8,128)S(1)} %collective-permute-done.1.refs_2_), channel_id=1, source_target_pairs={{0,4},{4,0},{8,12},{12,8},{16,20},{20,16},{24,28},{28,24},{1,5},{5... | collective-permute-start | bytes 393224 | tf_op jit(solution)/shard_map/ppermute | solution.py:183
  17.2 1.5 %collective-permute-start.6 = (f32[128,256]{1,0:T(8,128)S(1)}, f32[128,256]{1,0:T(8,128)S(1)}, u32[]{:S(2)}, u32[]{:S(2)}) collective-permute-start(f32[128,256]{1,0:T(8,128)S(1)} %collective-permute-done.2.refs_3_), channel_id=1, source_target_pairs={{0,4},{4,0},{8,12},{12,8},{16,20},{20,16},{24,28},{28,24},{1,5},{5... | collective-permute-start | bytes 393224 | tf_op jit(solution)/shard_map/ppermute | solution.py:183
  17.7 1.0 %copy-start.1 = (f32[64,256]{1,0:T(8,128)S(1)}, f32[64,256]{1,0:T(8,128)}, u32[]{:S(2)}) copy-start(f32[64,256]{1,0:T(8,128)} %refs_11_.1) | copy-start | bytes 196612
  20.6 14.5 %collective-permute-start.10 = (f32[256,256]{1,0:T(8,128)S(1)}, f32[256,256]{1,0:T(8,128)S(1)}, u32[]{:S(2)}, u32[]{:S(2)}) collective-permute-start(f32[256,256]{1,0:T(8,128)S(1)} %get-tuple-element.15.carry.refs_5_), channel_id=1, source_target_pairs={{0,8},{4,12},{16,24},{20,28},{1,9},{5,13},{17,25},{21,29},{2,10},{... | collective-permute-start | bytes 786440 | tf_op jit(solution)/shard_map/ppermute | solution.py:179
  23.6 12.3 %collective-permute-start.9 = (f32[256,256]{1,0:T(8,128)S(1)}, f32[256,256]{1,0:T(8,128)S(1)}, u32[]{:S(2)}, u32[]{:S(2)}) collective-permute-start(f32[256,256]{1,0:T(8,128)S(1)} %get-tuple-element.14.carry.refs_4_), channel_id=1, source_target_pairs={{0,8},{4,12},{16,24},{20,28},{1,9},{5,13},{17,25},{21,29},{2,10},{... | collective-permute-start | bytes 786440 | tf_op jit(solution)/shard_map/ppermute | solution.py:179
  25.0 7.4 %collective-permute-start.15 = (f32[64,256]{1,0:T(8,128)S(1)}, f32[64,256]{1,0:T(8,128)S(1)}, u32[]{:S(2)}, u32[]{:S(2)}) collective-permute-start(f32[64,256]{1,0:T(8,128)S(1)} %get-tuple-element.16.refs_12_), channel_id=1, source_target_pairs={{0,1},{1,2},{2,3},{3,0},{4,5},{5,6},{6,7},{7,4},{8,9},{9,10},{10,1... | collective-permute-start | bytes 196616 | tf_op jit(solution)/shard_map/ppermute | solution.py:188
  28.1 6.5 %collective-permute-start.16 = (f32[64,256]{1,0:T(8,128)S(1)}, f32[64,256]{1,0:T(8,128)S(1)}, u32[]{:S(2)}, u32[]{:S(2)}) collective-permute-start(f32[64,256]{1,0:T(8,128)S(1)} %get-tuple-element.16.refs_12_), channel_id=1, source_target_pairs={{0,2},{1,3},{2,0},{3,1},{4,6},{5,7},{6,4},{7,5},{8,10},{9,11},{10,... | collective-permute-start | bytes 196616 | tf_op jit(solution)/shard_map/ppermute | solution.py:188
  29.9 5.2 %collective-permute-start.17 = (f32[64,256]{1,0:T(8,128)S(1)}, f32[64,256]{1,0:T(8,128)S(1)}, u32[]{:S(2)}, u32[]{:S(2)}) collective-permute-start(f32[64,256]{1,0:T(8,128)S(1)} %get-tuple-element.16.refs_12_), channel_id=1, source_target_pairs={{0,3},{1,0},{2,1},{3,2},{4,7},{5,4},{6,5},{7,6},{8,11},{9,8},{10,9... | collective-permute-start | bytes 196616 | tf_op jit(solution)/shard_map/ppermute | solution.py:188
  32.3 4.6 %collective-permute-start.18 = (f32[64,256]{1,0:T(8,128)S(1)}, f32[64,256]{1,0:T(8,128)S(1)}, u32[]{:S(2)}, u32[]{:S(2)}) collective-permute-start(f32[64,256]{1,0:T(8,128)S(1)} %get-tuple-element.16.refs_12_), channel_id=1, source_target_pairs={{0,4},{4,0},{8,12},{12,8},{16,20},{20,16},{24,28},{28,24},{1,5},{5... | collective-permute-start | bytes 196616 | tf_op jit(solution)/shard_map/ppermute | solution.py:183
  34.6 3.1 %collective-permute-start.19 = (f32[64,256]{1,0:T(8,128)S(1)}, f32[64,256]{1,0:T(8,128)S(1)}, u32[]{:S(2)}, u32[]{:S(2)}) collective-permute-start(f32[64,256]{1,0:T(8,128)S(1)} %collective-permute-done.15.refs_13_), channel_id=1, source_target_pairs={{0,4},{4,0},{8,12},{12,8},{16,20},{20,16},{24,28},{28,24},{1,5},{5... | collective-permute-start | bytes 196616 | tf_op jit(solution)/shard_map/ppermute | solution.py:183
  35.1 3.2 %collective-permute-start.20 = (f32[64,256]{1,0:T(8,128)S(1)}, f32[64,256]{1,0:T(8,128)S(1)}, u32[]{:S(2)}, u32[]{:S(2)}) collective-permute-start(f32[64,256]{1,0:T(8,128)S(1)} %collective-permute-done.16.refs_14_), channel_id=1, source_target_pairs={{0,4},{4,0},{8,12},{12,8},{16,20},{20,16},{24,28},{28,24},{1,5},{5... | collective-permute-start | bytes 196616 | tf_op jit(solution)/shard_map/ppermute | solution.py:183
  35.1 3.9 %collective-permute-start.21 = (f32[64,256]{1,0:T(8,128)S(1)}, f32[64,256]{1,0:T(8,128)S(1)}, u32[]{:S(2)}, u32[]{:S(2)}) collective-permute-start(f32[64,256]{1,0:T(8,128)S(1)} %collective-permute-done.17.refs_15_), channel_id=1, source_target_pairs={{0,4},{4,0},{8,12},{12,8},{16,20},{20,16},{24,28},{28,24},{1,5},{5... | collective-permute-start | bytes 196616 | tf_op jit(solution)/shard_map/ppermute | solution.py:183
  35.9 3.8 %collective-permute-start.8 = (f32[256,256]{1,0:T(8,128)S(1)}, f32[256,256]{1,0:T(8,128)S(1)}, u32[]{:S(2)}, u32[]{:S(2)}) collective-permute-start(f32[256,256]{1,0:T(8,128)S(1)} %get-tuple-element.13.both.refs_2_), channel_id=1, source_target_pairs={{16,24},{20,28},{17,25},{21,29},{18,26},{22,30},{19,27},{23,31}} | collective-permute-start | bytes 786440 | tf_op jit(solution)/shard_map/ppermute | solution.py:179
  36.9 2.8 %collective-permute-start.13 = (f32[256,256]{1,0:T(8,128)S(1)}, f32[256,256]{1,0:T(8,128)S(1)}, u32[]{:S(2)}, u32[]{:S(2)}) collective-permute-start(f32[256,256]{1,0:T(8,128)S(1)} %shard_map.79), channel_id=1, source_target_pairs={{8,24},{12,28},{9,25},{13,29},{10,26},{14,30},{11,27},{15,31}} | collective-permute-start | bytes 786440 | tf_op jit(solution)/shard_map/ppermute | solution.py:179
  37.6 2.1 %collective-permute-start.14 = (f32[256,256]{1,0:T(8,128)S(1)}, f32[256,256]{1,0:T(8,128)S(1)}, u32[]{:S(2)}, u32[]{:S(2)}) collective-permute-start(f32[256,256]{1,0:T(8,128)S(1)} %shard_map.79), channel_id=1, source_target_pairs={{8,16},{12,20},{9,17},{13,21},{10,18},{14,22},{11,19},{15,23}} | collective-permute-start | bytes 786440 | tf_op jit(solution)/shard_map/ppermute | solution.py:179
  38.3 1.4 %collective-permute-start.11 = (f32[256,256]{1,0:T(8,128)S(1)}, f32[256,256]{1,0:T(8,128)S(1)}, u32[]{:S(2)}, u32[]{:S(2)}) collective-permute-start(f32[256,256]{1,0:T(8,128)S(1)} %shard_map.78), channel_id=1, source_target_pairs={{8,24},{12,28},{9,25},{13,29},{10,26},{14,30},{11,27},{15,31}} | collective-permute-start | bytes 786440 | tf_op jit(solution)/shard_map/ppermute | solution.py:179
  39.0 0.7 %collective-permute-start.12 = (f32[256,256]{1,0:T(8,128)S(1)}, f32[256,256]{1,0:T(8,128)S(1)}, u32[]{:S(2)}, u32[]{:S(2)}) collective-permute-start(f32[256,256]{1,0:T(8,128)S(1)} %shard_map.78), channel_id=1, source_target_pairs={{8,16},{12,20},{9,17},{13,21},{10,18},{14,22},{11,19},{15,23}} | collective-permute-start | bytes 786440 | tf_op jit(solution)/shard_map/ppermute | solution.py:179
  41.8 29.3 %collective-permute-start.22 = (f32[512,256]{1,0:T(8,128)S(1)}, f32[512,256]{1,0:T(8,128)S(1)}, u32[]{:S(2)}, u32[]{:S(2)}) collective-permute-start(f32[512,256]{1,0:T(8,128)S(1)} %get-tuple-element.18), channel_id=1, source_target_pairs={{0,4},{4,0},{8,12},{12,8},{16,20},{20,16},{24,28},{28,24},{1,5},{5... | collective-permute-start | bytes 1572872 | tf_op jit(solution)/shard_map/ppermute | solution.py:183
  41.9 27.5 %copy-start.2 = (f32[128,256]{1,0:T(8,128)S(1)}, f32[128,256]{1,0:T(8,128)}, u32[]{:S(2)}) copy-start(f32[128,256]{1,0:T(8,128)} %param.11) | copy-start | bytes 393220
  42.6 20.8 %collective-permute-start.23 = (f32[128,256]{1,0:T(8,128)}, f32[128,256]{1,0:T(8,128)S(1)}, u32[]{:S(2)}, u32[]{:S(2)}) collective-permute-start(f32[128,256]{1,0:T(8,128)} %get-tuple-element.24), channel_id=1, source_target_pairs={{0,24},{4,28},{8,16},{12,20},{16,8},{20,12},{24,0},{28,4},{1,25},{... | collective-permute-start | bytes 393224 | tf_op jit(solution)/shard_map/ppermute | solution.py:179
  59.0 8.4 %collective-permute-start.24 = (f32[128,256]{1,0:T(8,128)}, f32[128,256]{1,0:T(8,128)}, u32[]{:S(2)}, u32[]{:S(2)}) collective-permute-start(f32[128,256]{1,0:T(8,128)} %get-tuple-element.26), channel_id=1, source_target_pairs={{0,16},{4,20},{8,24},{12,28},{16,0},{20,4},{24,8},{28,12},{1,17},{... | collective-permute-start | bytes 393224 | tf_op jit(solution)/shard_map/ppermute | solution.py:179
  61.1 8.4 %collective-permute-start.25 = (f32[128,256]{1,0:T(8,128)S(1)}, f32[128,256]{1,0:T(8,128)}, u32[]{:S(2)}, u32[]{:S(2)}) collective-permute-start(f32[128,256]{1,0:T(8,128)S(1)} %get-tuple-element.25), channel_id=1, source_target_pairs={{0,8},{4,12},{8,0},{12,4},{16,24},{20,28},{24,16},{28,20},{1,9},{5... | collective-permute-start | bytes 393224 | tf_op jit(solution)/shard_map/ppermute | solution.py:179

commit v2 on v1

v2 whole, which is shorter than its diff:
```python
import functools
import math

import jax
import jax.numpy as jnp
from jax import lax
from jax.experimental import pallas as pl
from jax.experimental.pallas import tpu as pltpu
from jax.sharding import PartitionSpec as P

CHUNKS = 2
NT = (((1,), (1,)), ((), ()))
NN = (((1,), (0,)), ((), ()))
VMEM = pl.BlockSpec(memory_space=pltpu.VMEM)
HBM = pl.BlockSpec(memory_space=pltpu.HBM)
ANY = pl.BlockSpec(memory_space=pl.ANY)


def split(x):
    high = x.astype(jnp.bfloat16)
    return high, (x - high.astype(jnp.float32)).astype(jnp.bfloat16)


def dot3(left, right, dims):
    dot = functools.partial(lax.dot_general, dimension_numbers=dims, preferred_element_type=jnp.float32)
    return dot(left[0], right[0]) + (dot(left[0], right[1]) + dot(left[1], right[0]))


def chip_and_core():
    panel = lax.axis_index("panel")
    return lax.div(panel, 2), lax.rem(panel, 2)


def call(kernel, outs, args, scratch=(), products=0, after=()):
    size = sum(a.size * 4 for a in args) + sum(math.prod(o) * 4 for o in outs)
    inputs = len(args)

    def body(*refs):
        kernel(*refs[:inputs], *refs[inputs + len(after) :])

    return pl.pallas_call(
        body,
        out_shape=[jax.ShapeDtypeStruct(o, jnp.float32) for o in outs],
        in_specs=[VMEM] * inputs + [ANY] * len(after),
        out_specs=[VMEM] * len(outs),
        scratch_shapes=list(scratch),
        compiler_params=pltpu.CompilerParams(vmem_limit_bytes=40 << 20),
        cost_estimate=pl.CostEstimate(flops=6 * products, bytes_accessed=size, transcendentals=0),
    )(*args, *after)


def shard_rows(count, shift, height):
    start = lax.rem(lax.axis_index("row") + count - shift, count) * height
    return pl.ds(pl.multiple_of(start, height), height)


def take(refs, count):
    return [next(refs) for _ in range(count)]


def chunked(ref, chunks, *index):
    height = ref.shape[-2] // chunks
    return [
        ref[(chip, *index, slice(k * height, (k + 1) * height))] for k in range(chunks) for chip in range(ref.shape[0])
    ]


def extract(chunks, slab, bound, kept, entering):
    _, core = chip_and_core()
    kept[...] = jnp.concatenate(chunked(slab, chunks, core))
    entering[...] = jnp.concatenate(chunked(bound, chunks, core))


def prepare(count, chunks, *refs):
    refs = iter(refs)
    own, other = take(refs, count), take(refs, count)
    coupling, given, kept, bound = take(refs, 4)
    map_ref, both_ref, coupling_out = take(refs, 3)
    part_refs, carry_refs = take(refs, chunks), take(refs, chunks)
    inverse, beneath, part = take(refs, 3)
    chip, core = chip_and_core()
    coupling_out[...] = coupling[...]
    height = own[0].shape[0] // 2
    for shift in range(count):
        rows = shard_rows(count, shift, height)
        for slot, shards in ((core, own), (1 - core, other)):
            inverse[slot, rows, :] = shards[shift][:height, :]
            beneath[slot, rows, :] = shards[shift][height:, :]
    inverse_a, inverse_b = split(inverse[0]), split(inverse[1])
    map_a = dot3(inverse_a, split(beneath[0]), NN)
    map_b = dot3(inverse_b, split(beneath[1]), NN)
    parts_a, parts_b = split(map_a), split(map_b)
    map_ref[...] = map_a
    both_ref[...] = dot3(parts_b, parts_a, NN)
    first = core == 0
    got = jnp.concatenate(chunked(given, chunks, core))
    part[...] = dot3(split(jnp.where(first, kept[...], got)), inverse_a, NT)

    @pl.when(chip == 0)
    def _():
        part[...] -= dot3(split(bound[...]), parts_a, NT)

    carry = dot3(split(jnp.where(first, got, kept[...])), inverse_b, NT)
    carry -= dot3(split(part[...]), parts_b, NT)
    height = carry.shape[0] // chunks
    for k in range(chunks):
        rows = slice(k * height, (k + 1) * height)
        part_refs[k][...] = part[rows, :]
        carry_refs[k][...] = carry[rows]


def inclusive(carry, prior, both, out):
    out[...] = carry[...] + dot3(split(prior[...]), split(both[...]), NT)


def absorb(half, prior, across, arrived, put):
    total = arrived[0][...]
    for more in arrived[1:]:
        total = total + more[...]
    chip, _ = chip_and_core()
    inner = lax.rem(chip, half) != 0

    @pl.when(inner)
    def _():
        put(prior[...] + dot3(split(total), split(across[...]), NT))

    @pl.when(jnp.logical_not(inner))
    def _():
        put(prior[...] + total)


def advance(half, prior, across, *refs):
    *arrived, out = refs

    def put(value):
        out[...] = value

    absorb(half, prior, across, arrived, put)


def extend(half, across, arrived, out):
    chip, _ = chip_and_core()
    inner = lax.rem(chip, half) != 0
    upper = lax.rem(chip, 2 * half) >= half
    out[...] = across[...]

    @pl.when(jnp.logical_and(upper, inner))
    def _():
        out[...] = dot3(split(across[...]), split(arrived[...]), NN)

    @pl.when(jnp.logical_and(upper, jnp.logical_not(inner)))
    def _():
        out[...] = arrived[...]


def joined(half, both, across, out):
    chip, _ = chip_and_core()
    out[...] = both[...]

    @pl.when(lax.rem(chip, half) != 0)
    def _():
        out[...] = dot3(split(both[...]), split(across[...]), NN)


def finish(half, arrivals, *refs):
    refs = iter(refs)
    part, carry, prior, map_ref, both = take(refs, 5)
    across = next(refs) if arrivals else None
    arrived = take(refs, arrivals)
    stay, leave, entering = take(refs, 3)
    _, core = chip_and_core()
    first = core == 0

    def put(value):
        entering[...] = value

    if arrivals:
        absorb(half, prior, across, arrived, put)
    else:
        put(prior[...])
    incoming = split(entering[...])
    solved_a = part[...] - dot3(incoming, split(map_ref[...]), NT)
    solved_b = carry[...] + dot3(incoming, split(both[...]), NT)
    stay[...] = jnp.where(first, solved_a, solved_b)
    leave[...] = jnp.where(first, solved_b, solved_a)


def shared(chips, chunks, *refs):
    refs = iter(refs)
    stays, leaves = take(refs, chunks), take(refs, chunks)
    own, other = take(refs, 2)
    outs, tail = take(refs, chips), next(refs)
    chip, _ = chip_and_core()
    own, other = split(own[...]), split(other[...])
    height = stays[0].shape[0] // chips
    for k in range(chunks):
        tail[k] = dot3(split(stays[k][...]), own, NN) + dot3(split(leaves[k][...]), other, NN)
    for shift in range(chips):
        start = pl.multiple_of(destination(chip, shift, chips) * height, height)
        for k in range(chunks):
            outs[shift][k * height : (k + 1) * height, :] = tail[k, pl.ds(start, height), :]


def destination(chip, shift, chips):
    return chip ^ shift if chips & (chips - 1) == 0 else (chip + shift) % chips


def stacked(count, *refs):
    *shards, out = refs
    height = shards[0].shape[0]
    for shift in range(count):
        out[shard_rows(count, shift, height), :] = shards[shift][...]


def interleave(chips, chunks, *refs):
    *sources, out, token, sems = refs
    _, core = chip_and_core()
    height = sources[0].shape[0] // chips
    copies = [
        pltpu.make_async_copy(
            source.at[pl.ds(chip * height, height)],
            out.at[chip, core if at < chunks else 1 - core, pl.ds(at % chunks * height, height)],
            sems.at[at, chip],
        )
        for at, source in enumerate(sources)
        for chip in range(chips)
    ]
    for copy in copies:
        copy.start()
    token[...] = jnp.zeros_like(token)
    for copy in copies:
        copy.wait()


def subtract(cols, *refs):
    *shares, out = refs
    total = shares[0][...]
    for share in shares[1:]:
        total = total + share[...]
    out[...] = cols[...] - total


def between_chips(value, pairs):
    pairs = [(2 * a + core, 2 * b + core) for a, b in pairs for core in (0, 1)]
    return lax.ppermute(value, "panel", pairs)


def to_other_core(value):
    return lax.ppermute(value, "panel", [(q, q ^ 1) for q in range(lax.axis_size("panel"))])


def gather_rows(value, count):
    order = sorted(range(1, count), key=lambda s: min(s, count - s))
    sent = {s: lax.ppermute(value, "row", [(j, (j + s) % count) for j in range(count)]) for s in order}
    return [value] + [sent[s] for s in range(1, count)]


def on_device(slab, boundary, diag_inverse, sub_block, tail_coupling, tail_cols):
    panels, count = lax.axis_size("panel"), lax.axis_size("row")
    chips = panels // 2
    chip, core = chip_and_core()
    rows, width = slab.shape
    piece = rows // panels
    held = chips * piece

    def blocks(array):
        return array.reshape(chips, 2, piece, width)

    own = gather_rows(jnp.concatenate([diag_inverse, sub_block]), count)
    across_slab = to_other_core(slab)
    other = [to_other_core(shard) for shard in own]
    square = (width, width)
    part = (held, width)
    slice_shape = (held // CHUNKS, width)
    kept, bound = call(functools.partial(extract, CHUNKS), [part] * 2, [blocks(slab), blocks(boundary)])
    map_a, both, coupling, *made = call(
        functools.partial(prepare, count, CHUNKS),
        [square, square, tail_coupling.shape] + [slice_shape] * (2 * CHUNKS),
        [*own, *other, tail_coupling, blocks(across_slab), kept, bound],
        [pltpu.VMEM((2, *square), jnp.float32)] * 2 + [pltpu.VMEM(part, jnp.float32)],
        width * width * (3 * width + 4 * held),
    )
    parts, carries = made[:CHUNKS], made[CHUNKS:]

    priors, across = None, None
    half = 1
    while True:
        last = 2 * half >= chips
        sources = [s for s in range(half - 1, chips - 1, 2 * half)]
        inner = [s for s in sources if s >= half]
        arrived = []
        done = []
        for k in range(CHUNKS):
            value = carries[k]
            if priors is not None:
                if k == CHUNKS - 1:
                    done.append(across)
                (value,) = call(inclusive, [slice_shape], [value, priors[k], both], (), width * value.size, after=done)
                done = [value]
            arrived.append(
                [
                    between_chips(value, [(s, s + 1 + j) for s in sources if s + 1 + j < chips])
                    for j in reversed(range(half))
                ]
            )
        step_map = None
        if not last:
            send = both
            if across is not None:
                (send,) = call(functools.partial(joined, half), [square], [both, across], (), width**3)
            step_map = sum(between_chips(send, [(s, s + 1 + j) for s in inner if s + 1 + j < chips]) for j in range(half))
        if last and priors is not None:
            break
        if priors is None:
            priors = [a[0] for a in arrived]
            across = step_map
        else:
            advanced = functools.partial(advance, half)
            priors = [
                call(advanced, [slice_shape], [priors[k], across, *arrived[k]], (), width * priors[k].size)[0]
                for k in range(CHUNKS)
            ]
            (across,) = call(functools.partial(extend, half), [square], [across, step_map], (), width**3)
        if last:
            arrived = [[] for _ in range(CHUNKS)]
            break
        half *= 2

    (own_coupling,) = call(functools.partial(stacked, count), [square], gather_rows(coupling, count), after=[value])
    other_coupling = to_other_core(own_coupling)
    arrivals = len(arrived[0])
    stays, leaves = [], []
    for k in range(CHUNKS):
        stay, leave = call(
            functools.partial(finish, half, arrivals),
            [slice_shape] * 2,
            [parts[k], carries[k], priors[k], map_a, both] + ([across] if arrivals else []) + arrived[k],
            [pltpu.VMEM(slice_shape, jnp.float32)],
            3 * width * width * held // CHUNKS,
            after=stays[-1:],
        )
        stays.append(stay)
        leaves.append(leave)
    shares = call(
        functools.partial(shared, chips, CHUNKS),
        [(piece, width)] * chips,
        [*stays, *leaves, own_coupling, other_coupling],
        [pltpu.VMEM((CHUNKS, *slice_shape), jnp.float32)],
        2 * width * width * held,
    )
    shares = list(shares)
    for k in reversed(range(1, chips)):
        shares[k] = between_chips(shares[k], [(a, destination(a, k, chips)) for a in range(chips)])
    came = [to_other_core(leave) for leave in leaves]
    factor, token = pl.pallas_call(
        functools.partial(interleave, chips, CHUNKS),
        out_shape=[
            jax.ShapeDtypeStruct((chips, 2, piece, width), jnp.float32),
            jax.ShapeDtypeStruct((8, 128), jnp.float32),
        ],
        in_specs=[VMEM] * (2 * CHUNKS),
        out_specs=[HBM, VMEM],
        scratch_shapes=[pltpu.SemaphoreType.DMA((2 * CHUNKS, chips))],
        compiler_params=pltpu.CompilerParams(vmem_limit_bytes=4 << 20),
        cost_estimate=pl.CostEstimate(flops=0, bytes_accessed=16 * held * width, transcendentals=0),
    )(*stays, *came)
    (tail_out,) = call(subtract, [tail_cols.shape], [tail_cols, *shares], after=[token])
    return factor.reshape(rows, width), tail_out


def solution(mesh):
    placed = (
        P("row", "panel"),
        P("row", None),
        P(("panel", "row"), None),
        P(("panel", "row"), None),
        P(("panel", "row"), None),
        P(("row", "panel"), None),
    )
    return jax.shard_map(
        on_device,
        mesh=mesh,
        in_specs=placed,
        out_specs=(P("row", "panel"), P(("row", "panel"), None)),
        check_vma=False,
    )
```

time: 72.6 us -> 70 us (0.964)
  starting transfers between devices: 41.6 us -> 27.7 us
  waiting for transfers between devices: 19.8 us -> 31 us
  other arithmetic: 1.8 us -> 0 us
  Pallas kernels: 4.55 us -> 6 us
    ppermute x10, starting transfers between devices: 27.5 us -> 16.7 us  [between_chips(): return lax.ppermute(value, 'panel', pairs)]
    ppermute x6, waiting for transfers between devices: 11.8 us -> 18.9 us  [gather_rows(): lax.ppermute(value, 'row', [(j, (j + s) % count) for j in range(count)])]
    ppermute x10, waiting for transfers between devices: 7.02 us -> 12.1 us  [between_chips(): return lax.ppermute(value, 'panel', pairs)]
    unnamed x11, local copies, waits for them, and re-layouts: 0.33 us -> 4.01 us
    ppermute x6, starting transfers between devices: 12.5 us -> 9.32 us  [gather_rows(): lax.ppermute(value, 'row', [(j, (j + s) % count) for j in range(count)])]
    sub x1 -> x0, other arithmetic: 1.66 us -> none  [on_device(): return (factor, tail_cols - summed)]
    pallas_call x4 -> x10, Pallas kernels: 4.55 us -> 6 us  [the longest x9 4.91 us: call(): pl.pallas_call(body, out_shape=[jax.ShapeDtypeStruct(o, jnp.float32) for...]
    dynamic_slice x2 -> x0, local copies, waits for them, and re-layouts: 1.41 us -> none  [blocks(): lax.dynamic_index_in_dim(array, parity, 1, keepdims=False)]
  transfers between devices with their start and end apart: 26 -> 24, of which waited for: 10 -> 8; matrix products, arithmetic and copies ran while one was open for 3% -> 1% of each run, Pallas kernels for 1% -> 5%
where the time goes in v2:
time: 70 us; the launch traced here: 69.6 us
  waiting for transfers between devices  31 us (44%)
  starting transfers between devices  27.7 us (40%)
  Pallas kernels  6 us (9%)
  local copies, waits for them, and re-layouts  4.02 us (6%)
  between operations  0.87 us (1%)
    ppermute x6, waiting for transfers between devices, gather_rows(): lax.ppermute(value, 'row', [(j, (j + s) % count) for j in range(count)])  18.9 us
    ppermute x10, starting transfers between devices, between_chips(): return lax.ppermute(value, 'panel', pairs)  16.7 us
    ppermute x10, waiting for transfers between devices, between_chips(): return lax.ppermute(value, 'panel', pairs)  12.1 us
    ppermute x6, starting transfers between devices, gather_rows(): lax.ppermute(value, 'row', [(j, (j + s) % count) for j in range(count)])  9.32 us
    pallas_call x9, Pallas kernels, call(): pl.pallas_call(body, out_shape=[jax.ShapeDtypeStruct(o, jnp.float32) for...  4.91 us
    unnamed x11, local copies, waits for them, and re-layouts  4.01 us
    ppermute x8, starting transfers between devices, to_other_core(): lax.ppermute(value, 'panel', [(q, q ^ 1) for q in range(lax.axis_size('pa...  1.73 us
  transfers between devices with their start and end apart: 24, of which 8 were waited for; matrix products, arithmetic and copies ran while one was open for 1% of the time, Pallas kernels for 5%

profile of v2, /device:TPU:0, one launch (start us, length us, event | category | flops | bytes accessed | tf_op | source)
XLA Modules:
  0.0 69.6 jit_solution(1110250632470159526)
XLA Ops:
  0.6 0.0 copy-start.4
  0.6 0.5 collective-permute-start.7
  1.2 0.8 %constant_dynamic-update-slice_fusion.1 = f32[128,256]{1,0:T(8,128)S(1)} fusion(f32[64,256]{1,0:T(8,128)} %param.8), kind=kLoop, calls=%fused_computation.1 | loop fusion | bytes 131072
  2.0 0.0 copy-done.4
  2.0 4.7 %collective-permute-start.2 = (f32[128,256]{1,0:T(8,128)S(1)}, f32[128,256]{1,0:T(8,128)S(1)}, u32[]{:S(2)}, u32[]{:S(2)}) collective-permute-start(f32[128,256]{1,0:T(8,128)S(1)} %constant_dynamic-update-slice_fusion.refs_0_), channel_id=1, source_target_pairs={{0,3},{1,0},{2,1},{3,2},{4,7},{5,4},{6,5},{7,6},{8,11},{9,8},{10,9... | collective-permute-start | bytes 393224 | tf_op jit(solution)/shard_map/ppermute | solution.py:254
  6.7 0.0 collective-permute-start.1
  6.7 1.0 %collective-permute-start = (f32[128,256]{1,0:T(8,128)S(1)}, f32[128,256]{1,0:T(8,128)S(1)}, u32[]{:S(2)}, u32[]{:S(2)}) collective-permute-start(f32[128,256]{1,0:T(8,128)S(1)} %constant_dynamic-update-slice_fusion.refs_0_), channel_id=1, source_target_pairs={{0,1},{1,2},{2,3},{3,0},{4,5},{5,6},{6,7},{7,4},{8,9},{9,10},{10,1... | collective-permute-start | bytes 393224 | tf_op jit(solution)/shard_map/ppermute | solution.py:254
  7.7 0.0 collective-permute-start.3
  7.7 2.9 %collective-permute-done.2.refs_3_ = f32[128,256]{1,0:T(8,128)S(1)} collective-permute-done((f32[128,256]{1,0:T(8,128)S(1)}, f32[128,256]{1,0:T(8,128)S(1)}, u32[]{:S(2)}, u32[]{:S(2)}) %collective-permute-start.2) | collective-permute-done | bytes 131104 | tf_op jit(solution)/shard_map/ppermute | solution.py:254
  10.6 0.0 collective-permute-start.6
  10.6 8.2 %collective-permute-done.1.refs_2_ = f32[128,256]{1,0:T(8,128)S(1)} collective-permute-done((f32[128,256]{1,0:T(8,128)S(1)}, f32[128,256]{1,0:T(8,128)S(1)}, u32[]{:S(2)}, u32[]{:S(2)}) %collective-permute-start.1) | collective-permute-done | bytes 131104 | tf_op jit(solution)/shard_map/ppermute | solution.py:254
  18.8 0.0 collective-permute-start.5
  18.8 0.0 collective-permute-done.refs_1_
  18.8 0.5 collective-permute-start.4
  19.3 1.2 %copy-done = f32[1024,256]{1,0:T(8,128)S(1)} copy-done((f32[1024,256]{1,0:T(8,128)S(1)}, f32[1024,256]{1,0:T(8,128)}, u32[]{:S(2)}) %copy-start) | copy-done | bytes 1048600
  20.6 1.2 %copy-done.1 = f32[1024,256]{1,0:T(8,128)S(1)} copy-done((f32[1024,256]{1,0:T(8,128)S(1)}, f32[1024,256]{1,0:T(8,128)}, u32[]{:S(2)}) %copy-start.1) | copy-done | bytes 1048600
  21.8 0.1 shard_map.77
  21.9 0.0 collective-permute-done.3.refs_4_
  21.9 0.0 collective-permute-done.6.refs_7_
  21.9 0.0 collective-permute-done.5.refs_6_
  21.9 0.0 collective-permute-done.4.refs_5_
  21.9 0.0 collective-permute-done.7
  21.9 0.7 %copy-done.3 = f32[64,256]{1,0:T(8,128)S(1)} copy-done((f32[64,256]{1,0:T(8,128)S(1)}, f32[64,256]{1,0:T(8,128)}, u32[]{:S(2)}) %copy-start.3) | copy-done | bytes 65560
  22.6 2.0 %shard_map.78 = (f32[256,256]{1,0:T(8,128)S(1)}, f32[256,256]{1,0:T(8,128)S(1)}, f32[64,256]{1,0:T(8,128)S(1)}, f32[256,256]{1,0:T(8,128)S(1)}, f32[256,256]{1,0...) custom-call(f32[128,256]{1,0:T(8,128)S(1)} %constant_dynamic-update-slice_fusion.refs_0_, ...), custom_call_target="tpu_custom_call" | custom-call | flops 1107296256 | bytes 4849664 | tf_op jit(solution)/shard_map/pallas_call | solution.py:41
  24.6 3.0 %collective-permute-start.8 = (f32[256,256]{1,0:T(8,128)S(1)}, f32[256,256]{1,0:T(8,128)S(1)}, u32[]{:S(2)}, u32[]{:S(2)}) collective-permute-start(f32[256,256]{1,0:T(8,128)S(1)} %get-tuple-element.24.refs_0_.refs_1_), channel_id=1, source_target_pairs={{0,8},{4,12},{16,24},{20,28},{1,9},{5,13},{17,25},{21,29},{2,10},{... | collective-permute-start | bytes 786440 | tf_op jit(solution)/shard_map/ppermute | solution.py:245
  27.6 1.3 %collective-permute-start.12 = (f32[256,256]{1,0:T(8,128)S(1)}, f32[256,256]{1,0:T(8,128)S(1)}, u32[]{:S(2)}, u32[]{:S(2)}) collective-permute-start(f32[256,256]{1,0:T(8,128)S(1)} %get-tuple-element.29.refs_0_.refs_1_), channel_id=1, source_target_pairs={{0,8},{4,12},{16,24},{20,28},{1,9},{5,13},{17,25},{21,29},{2,10},{... | collective-permute-start | bytes 786440 | tf_op jit(solution)/shard_map/ppermute | solution.py:245
  28.9 0.7 collective-permute-start.9
  29.6 1.2 %collective-permute-start.19 = (f32[64,256]{1,0:T(8,128)S(1)}, f32[64,256]{1,0:T(8,128)S(1)}, u32[]{:S(2)}, u32[]{:S(2)}) collective-permute-start(f32[64,256]{1,0:T(8,128)S(1)} %get-tuple-element.34.refs_0_), channel_id=1, source_target_pairs={{0,3},{1,0},{2,1},{3,2},{4,7},{5,4},{6,5},{7,6},{8,11},{9,8},{10,9... | collective-permute-start | bytes 196616 | tf_op jit(solution)/shard_map/ppermute | solution.py:254
  30.8 3.4 %collective-permute-done.8.refs_1_.refs_2_ = f32[256,256]{1,0:T(8,128)S(1)} collective-permute-done((f32[256,256]{1,0:T(8,128)S(1)}, f32[256,256]{1,0:T(8,128)S(1)}, u32[]{:S(2)}, u32[]{:S(2)}) %collective-permute-start.8) | collective-permute-done | bytes 262176 | tf_op jit(solution)/shard_map/ppermute | solution.py:245
  34.2 0.3 shard_map.79.refs_3_
  34.5 0.7 collective-permute-start.11
  35.2 0.7 collective-permute-start.10
  35.9 3.0 %collective-permute-done.12.refs_1_.refs_2_ = f32[256,256]{1,0:T(8,128)S(1)} collective-permute-done((f32[256,256]{1,0:T(8,128)S(1)}, f32[256,256]{1,0:T(8,128)S(1)}, u32[]{:S(2)}, u32[]{:S(2)}) %collective-permute-start.12) | collective-permute-done | bytes 262176 | tf_op jit(solution)/shard_map/ppermute | solution.py:245
  38.9 2.4 %collective-permute-start.18 = (f32[64,256]{1,0:T(8,128)S(1)}, f32[64,256]{1,0:T(8,128)S(1)}, u32[]{:S(2)}, u32[]{:S(2)}) collective-permute-start(f32[64,256]{1,0:T(8,128)S(1)} %get-tuple-element.34.refs_0_), channel_id=1, source_target_pairs={{0,2},{1,3},{2,0},{3,1},{4,6},{5,7},{6,4},{7,5},{8,10},{9,11},{10,... | collective-permute-start | bytes 196616 | tf_op jit(solution)/shard_map/ppermute | solution.py:254
  41.3 0.0 collective-permute-done.9.refs_5_.refs_4_
  41.3 0.3 shard_map.81.refs_4_
  41.6 0.7 collective-permute-start.14
  42.3 0.0 collective-permute-done.19.refs_3_
  42.3 0.7 collective-permute-start.13
  43.0 1.7 %collective-permute-done.18.refs_2_ = f32[64,256]{1,0:T(8,128)S(1)} collective-permute-done((f32[64,256]{1,0:T(8,128)S(1)}, f32[64,256]{1,0:T(8,128)S(1)}, u32[]{:S(2)}, u32[]{:S(2)}) %collective-permute-start.18) | collective-permute-done | bytes 65568 | tf_op jit(solution)/shard_map/ppermute | solution.py:254
  44.7 0.0 collective-permute-start.17
  44.7 6.1 %collective-permute-done.17.refs_1_ = f32[64,256]{1,0:T(8,128)S(1)} collective-permute-done((f32[64,256]{1,0:T(8,128)S(1)}, f32[64,256]{1,0:T(8,128)S(1)}, u32[]{:S(2)}, u32[]{:S(2)}) %collective-permute-start.17) | collective-permute-done | bytes 65568 | tf_op jit(solution)/shard_map/ppermute | solution.py:254
  50.8 0.1 collective-permute-start.20
  50.8 0.0 collective-permute-done.11.refs_7_
  50.9 0.0 collective-permute-done.10.refs_6_
  50.9 0.5 shard_map.80
  51.3 0.0 collective-permute-done.14.refs_7_
  51.4 0.0 collective-permute-done.13.refs_6_
  51.4 0.5 shard_map.82
  51.8 0.5 collective-permute-start.16
  52.4 0.1 collective-permute-start.15
  52.5 0.0 collective-permute-done.20.refs_5_
  52.5 0.6 shard_map.85
  53.1 7.5 %collective-permute-start.21 = (f32[128,256]{1,0:T(8,128)S(1)}, f32[128,256]{1,0:T(8,128)S(1)}, u32[]{:S(2)}, u32[]{:S(2)}) collective-permute-start(f32[128,256]{1,0:T(8,128)S(1)} %get-tuple-element.36), channel_id=1, source_target_pairs={{0,8},{4,12},{8,0},{12,4},{16,24},{20,28},{24,16},{28,20},{1,9},{5... | collective-permute-start | bytes 393224 | tf_op jit(solution)/shard_map/ppermute | solution.py:245
  60.6 0.3 collective-permute-start.22
  60.8 1.3 %collective-permute-start.23 = (f32[128,256]{1,0:T(8,128)S(1)}, f32[128,256]{1,0:T(8,128)S(1)}, u32[]{:S(2)}, u32[]{:S(2)}) collective-permute-start(f32[128,256]{1,0:T(8,128)S(1)} %get-tuple-element.38), channel_id=1, source_target_pairs={{0,24},{4,28},{8,16},{12,20},{16,8},{20,12},{24,0},{28,4},{1,25},{... | collective-permute-start | bytes 393224 | tf_op jit(solution)/shard_map/ppermute | solution.py:245
  62.1 0.0 collective-permute-done.16.refs_3_
  62.1 0.0 collective-permute-done.15.refs_2_
  62.1 1.1 %shard_map.83 = (f32[4,2,128,256]{3,2,1,0:T(8,128)}, f32[8,128]{1,0:T(8,128)S(1)}) custom-call(f32[256,256]{1,0:T(8,128)S(1)} %get-tuple-element.27.refs_8_.refs_0_, f32[256,256]{1,0:T(8,128)S(1)} %get-tuple-element.30.refs_1_, f32[256,256]{1,0:T(8,128)S(1)} %collective-permute-done.15.refs_2_, f32[256,256]{1,0:T(8,128)S(1)} %collective-permute-done.16.refs_3_), custom_call_target="tpu_custom_call" | custom-call | bytes 2097152 | tf_op jit(solution)/shard_map/pallas_call | solution.py:355
  63.2 1.5 %collective-permute-done.21.refs_2_ = f32[128,256]{1,0:T(8,128)S(1)} collective-permute-done((f32[128,256]{1,0:T(8,128)S(1)}, f32[128,256]{1,0:T(8,128)S(1)}, u32[]{:S(2)}, u32[]{:S(2)}) %collective-permute-start.21) | collective-permute-done | bytes 131104 | tf_op jit(solution)/shard_map/ppermute | solution.py:245
  64.7 4.2 %collective-permute-done.22.refs_3_ = f32[128,256]{1,0:T(8,128)S(1)} collective-permute-done((f32[128,256]{1,0:T(8,128)S(1)}, f32[128,256]{1,0:T(8,128)S(1)}, u32[]{:S(2)}, u32[]{:S(2)}) %collective-permute-start.22) | collective-permute-done | bytes 131104 | tf_op jit(solution)/shard_map/ppermute | solution.py:245
  68.9 0.0 collective-permute-done.23.refs_4_
  68.9 0.0 copy-done.2
  68.9 0.7 %shard_map.86 = f32[128,256]{1,0:T(8,128)} custom-call(f32[128,256]{1,0:T(8,128)S(1)} %copy-done.2, f32[128,256]{1,0:T(8,128)S(1)} %get-tuple-element.35.refs_1_, f32[128,256]{1,0:T(8,128)S(1)} %collective-permute-done.21.refs_2_, f32[128,256]{1,0:T(8,128)S(1)} %collective-permute-done.22.refs_3_, f32[128,256]{1,0:T(8,128)S(1)} %collective-permute-done.23.refs_4_, ...), custom_call_target="tpu_custom_call" | custom-call | bytes 786432 | tf_op jit(solution)/shard_map/pallas_call | solution.py:41
  (6 shorter events, 0.0 us)
Async XLA Ops:
  0.6 1.4 %copy-start.4 = (f32[64,256]{1,0:T(8,128)S(1)}, f32[64,256]{1,0:T(8,128)}, u32[]{:S(2)}) copy-start(f32[64,256]{1,0:T(8,128)} %param.9) | copy-start | bytes 196612
  0.6 21.3 %collective-permute-start.7 = (f32[1024,256]{1,0:T(8,128)}, f32[1024,256]{1,0:T(8,128)S(1)}, u32[]{:S(2)}, u32[]{:S(2)}) collective-permute-start(f32[1024,256]{1,0:T(8,128)} %param.6), channel_id=1, source_target_pairs={{0,4},{4,0},{8,12},{12,8},{16,20},{20,16},{24,28},{28,24},{1,5},{5... | collective-permute-start | bytes 3145736 | tf_op jit(solution)/shard_map/ppermute | solution.py:249
  2.0 8.6 %collective-permute-start.2 = (f32[128,256]{1,0:T(8,128)S(1)}, f32[128,256]{1,0:T(8,128)S(1)}, u32[]{:S(2)}, u32[]{:S(2)}) collective-permute-start(f32[128,256]{1,0:T(8,128)S(1)} %constant_dynamic-update-slice_fusion.refs_0_), channel_id=1, source_target_pairs={{0,3},{1,0},{2,1},{3,2},{4,7},{5,4},{6,5},{7,6},{8,11},{9,8},{10,9... | collective-permute-start | bytes 393224 | tf_op jit(solution)/shard_map/ppermute | solution.py:254
  6.7 12.1 %collective-permute-start.1 = (f32[128,256]{1,0:T(8,128)S(1)}, f32[128,256]{1,0:T(8,128)S(1)}, u32[]{:S(2)}, u32[]{:S(2)}) collective-permute-start(f32[128,256]{1,0:T(8,128)S(1)} %constant_dynamic-update-slice_fusion.refs_0_), channel_id=1, source_target_pairs={{0,2},{1,3},{2,0},{3,1},{4,6},{5,7},{6,4},{7,5},{8,10},{9,11},{10,... | collective-permute-start | bytes 393224 | tf_op jit(solution)/shard_map/ppermute | solution.py:254
  6.7 12.1 %collective-permute-start = (f32[128,256]{1,0:T(8,128)S(1)}, f32[128,256]{1,0:T(8,128)S(1)}, u32[]{:S(2)}, u32[]{:S(2)}) collective-permute-start(f32[128,256]{1,0:T(8,128)S(1)} %constant_dynamic-update-slice_fusion.refs_0_), channel_id=1, source_target_pairs={{0,1},{1,2},{2,3},{3,0},{4,5},{5,6},{6,7},{7,4},{8,9},{9,10},{10,1... | collective-permute-start | bytes 393224 | tf_op jit(solution)/shard_map/ppermute | solution.py:254
  7.7 14.2 %collective-permute-start.3 = (f32[128,256]{1,0:T(8,128)S(1)}, f32[128,256]{1,0:T(8,128)S(1)}, u32[]{:S(2)}, u32[]{:S(2)}) collective-permute-start(f32[128,256]{1,0:T(8,128)S(1)} %constant_dynamic-update-slice_fusion.refs_0_), channel_id=1, source_target_pairs={{0,4},{4,0},{8,12},{12,8},{16,20},{20,16},{24,28},{28,24},{1,5},{5... | collective-permute-start | bytes 393224 | tf_op jit(solution)/shard_map/ppermute | solution.py:249
  10.6 11.3 %collective-permute-start.6 = (f32[128,256]{1,0:T(8,128)S(1)}, f32[128,256]{1,0:T(8,128)S(1)}, u32[]{:S(2)}, u32[]{:S(2)}) collective-permute-start(f32[128,256]{1,0:T(8,128)S(1)} %collective-permute-done.2.refs_3_), channel_id=1, source_target_pairs={{0,4},{4,0},{8,12},{12,8},{16,20},{20,16},{24,28},{28,24},{1,5},{5... | collective-permute-start | bytes 393224 | tf_op jit(solution)/shard_map/ppermute | solution.py:249
  18.8 3.1 %collective-permute-start.5 = (f32[128,256]{1,0:T(8,128)S(1)}, f32[128,256]{1,0:T(8,128)S(1)}, u32[]{:S(2)}, u32[]{:S(2)}) collective-permute-start(f32[128,256]{1,0:T(8,128)S(1)} %collective-permute-done.1.refs_2_), channel_id=1, source_target_pairs={{0,4},{4,0},{8,12},{12,8},{16,20},{20,16},{24,28},{28,24},{1,5},{5... | collective-permute-start | bytes 393224 | tf_op jit(solution)/shard_map/ppermute | solution.py:249
  18.8 3.1 %collective-permute-start.4 = (f32[128,256]{1,0:T(8,128)S(1)}, f32[128,256]{1,0:T(8,128)S(1)}, u32[]{:S(2)}, u32[]{:S(2)}) collective-permute-start(f32[128,256]{1,0:T(8,128)S(1)} %collective-permute-done.refs_1_), channel_id=1, source_target_pairs={{0,4},{4,0},{8,12},{12,8},{16,20},{20,16},{24,28},{28,24},{1,5},{5... | collective-permute-start | bytes 393224 | tf_op jit(solution)/shard_map/ppermute | solution.py:249
  19.3 1.2 %copy-start = (f32[1024,256]{1,0:T(8,128)S(1)}, f32[1024,256]{1,0:T(8,128)}, u32[]{:S(2)}) copy-start(f32[1024,256]{1,0:T(8,128)} %param.7) | copy-start | bytes 3145732
  20.6 1.2 %copy-start.1 = (f32[1024,256]{1,0:T(8,128)S(1)}, f32[1024,256]{1,0:T(8,128)}, u32[]{:S(2)}) copy-start(f32[1024,256]{1,0:T(8,128)} %param.6) | copy-start | bytes 3145732
  21.8 0.8 %copy-start.3 = (f32[64,256]{1,0:T(8,128)S(1)}, f32[64,256]{1,0:T(8,128)}, u32[]{:S(2)}) copy-start(f32[64,256]{1,0:T(8,128)} %refs_8_.1) | copy-start | bytes 196612
  24.6 9.7 %collective-permute-start.8 = (f32[256,256]{1,0:T(8,128)S(1)}, f32[256,256]{1,0:T(8,128)S(1)}, u32[]{:S(2)}, u32[]{:S(2)}) collective-permute-start(f32[256,256]{1,0:T(8,128)S(1)} %get-tuple-element.24.refs_0_.refs_1_), channel_id=1, source_target_pairs={{0,8},{4,12},{16,24},{20,28},{1,9},{5,13},{17,25},{21,29},{2,10},{... | collective-permute-start | bytes 786440 | tf_op jit(solution)/shard_map/ppermute | solution.py:245
  27.6 11.3 %collective-permute-start.12 = (f32[256,256]{1,0:T(8,128)S(1)}, f32[256,256]{1,0:T(8,128)S(1)}, u32[]{:S(2)}, u32[]{:S(2)}) collective-permute-start(f32[256,256]{1,0:T(8,128)S(1)} %get-tuple-element.29.refs_0_.refs_1_), channel_id=1, source_target_pairs={{0,8},{4,12},{16,24},{20,28},{1,9},{5,13},{17,25},{21,29},{2,10},{... | collective-permute-start | bytes 786440 | tf_op jit(solution)/shard_map/ppermute | solution.py:245
  28.9 12.4 %collective-permute-start.9 = (f32[256,256]{1,0:T(8,128)S(1)}, f32[256,256]{1,0:T(8,128)S(1)}, u32[]{:S(2)}, u32[]{:S(2)}) collective-permute-start(f32[256,256]{1,0:T(8,128)S(1)} %get-tuple-element.26.refs_2_.refs_4_), channel_id=1, source_target_pairs={{16,24},{20,28},{17,25},{21,29},{18,26},{22,30},{19,27},{23,31}} | collective-permute-start | bytes 786440 | tf_op jit(solution)/shard_map/ppermute | solution.py:245
  29.6 12.7 %collective-permute-start.19 = (f32[64,256]{1,0:T(8,128)S(1)}, f32[64,256]{1,0:T(8,128)S(1)}, u32[]{:S(2)}, u32[]{:S(2)}) collective-permute-start(f32[64,256]{1,0:T(8,128)S(1)} %get-tuple-element.34.refs_0_), channel_id=1, source_target_pairs={{0,3},{1,0},{2,1},{3,2},{4,7},{5,4},{6,5},{7,6},{8,11},{9,8},{10,9... | collective-permute-start | bytes 196616 | tf_op jit(solution)/shard_map/ppermute | solution.py:254
  34.5 16.3 %collective-permute-start.11 = (f32[256,256]{1,0:T(8,128)S(1)}, f32[256,256]{1,0:T(8,128)S(1)}, u32[]{:S(2)}, u32[]{:S(2)}) collective-permute-start(f32[256,256]{1,0:T(8,128)S(1)} %shard_map.79.refs_3_), channel_id=1, source_target_pairs={{8,16},{12,20},{9,17},{13,21},{10,18},{14,22},{11,19},{15,23}} | collective-permute-start | bytes 786440 | tf_op jit(solution)/shard_map/ppermute | solution.py:245
  35.2 15.6 %collective-permute-start.10 = (f32[256,256]{1,0:T(8,128)S(1)}, f32[256,256]{1,0:T(8,128)S(1)}, u32[]{:S(2)}, u32[]{:S(2)}) collective-permute-start(f32[256,256]{1,0:T(8,128)S(1)} %shard_map.79.refs_3_), channel_id=1, source_target_pairs={{8,24},{12,28},{9,25},{13,29},{10,26},{14,30},{11,27},{15,31}} | collective-permute-start | bytes 786440 | tf_op jit(solution)/shard_map/ppermute | solution.py:245
  38.9 5.8 %collective-permute-start.18 = (f32[64,256]{1,0:T(8,128)S(1)}, f32[64,256]{1,0:T(8,128)S(1)}, u32[]{:S(2)}, u32[]{:S(2)}) collective-permute-start(f32[64,256]{1,0:T(8,128)S(1)} %get-tuple-element.34.refs_0_), channel_id=1, source_target_pairs={{0,2},{1,3},{2,0},{3,1},{4,6},{5,7},{6,4},{7,5},{8,10},{9,11},{10,... | collective-permute-start | bytes 196616 | tf_op jit(solution)/shard_map/ppermute | solution.py:254
  41.6 9.7 %collective-permute-start.14 = (f32[256,256]{1,0:T(8,128)S(1)}, f32[256,256]{1,0:T(8,128)S(1)}, u32[]{:S(2)}, u32[]{:S(2)}) collective-permute-start(f32[256,256]{1,0:T(8,128)S(1)} %shard_map.81.refs_4_), channel_id=1, source_target_pairs={{8,16},{12,20},{9,17},{13,21},{10,18},{14,22},{11,19},{15,23}} | collective-permute-start | bytes 786440 | tf_op jit(solution)/shard_map/ppermute | solution.py:245
  42.3 9.1 %collective-permute-start.13 = (f32[256,256]{1,0:T(8,128)S(1)}, f32[256,256]{1,0:T(8,128)S(1)}, u32[]{:S(2)}, u32[]{:S(2)}) collective-permute-start(f32[256,256]{1,0:T(8,128)S(1)} %shard_map.81.refs_4_), channel_id=1, source_target_pairs={{8,24},{12,28},{9,25},{13,29},{10,26},{14,30},{11,27},{15,31}} | collective-permute-start | bytes 786440 | tf_op jit(solution)/shard_map/ppermute | solution.py:245
  44.7 6.1 %collective-permute-start.17 = (f32[64,256]{1,0:T(8,128)S(1)}, f32[64,256]{1,0:T(8,128)S(1)}, u32[]{:S(2)}, u32[]{:S(2)}) collective-permute-start(f32[64,256]{1,0:T(8,128)S(1)} %get-tuple-element.34.refs_0_), channel_id=1, source_target_pairs={{0,1},{1,2},{2,3},{3,0},{4,5},{5,6},{6,7},{7,4},{8,9},{9,10},{10,1... | collective-permute-start | bytes 196616 | tf_op jit(solution)/shard_map/ppermute | solution.py:254
  50.8 1.7 %collective-permute-start.20 = (f32[256,256]{1,0:T(8,128)S(1)}, f32[256,256]{1,0:T(8,128)S(1)}, u32[]{:S(2)}, u32[]{:S(2)}) collective-permute-start(f32[256,256]{1,0:T(8,128)S(1)} %shard_map.84.refs_4_), channel_id=1, source_target_pairs={{0,4},{4,0},{8,12},{12,8},{16,20},{20,16},{24,28},{28,24},{1,5},{5... | collective-permute-start | bytes 786440 | tf_op jit(solution)/shard_map/ppermute | solution.py:249
  51.8 10.3 %collective-permute-start.16 = (f32[256,256]{1,0:T(8,128)S(1)}, f32[256,256]{1,0:T(8,128)S(1)}, u32[]{:S(2)}, u32[]{:S(2)}) collective-permute-start(f32[256,256]{1,0:T(8,128)S(1)} %get-tuple-element.32.refs_3_), channel_id=1, source_target_pairs={{0,4},{4,0},{8,12},{12,8},{16,20},{20,16},{24,28},{28,24},{1,5},{5... | collective-permute-start | bytes 786440 | tf_op jit(solution)/shard_map/ppermute | solution.py:249
  52.4 9.7 %collective-permute-start.15 = (f32[256,256]{1,0:T(8,128)S(1)}, f32[256,256]{1,0:T(8,128)S(1)}, u32[]{:S(2)}, u32[]{:S(2)}) collective-permute-start(f32[256,256]{1,0:T(8,128)S(1)} %get-tuple-element.31.refs_2_), channel_id=1, source_target_pairs={{0,4},{4,0},{8,12},{12,8},{16,20},{20,16},{24,28},{28,24},{1,5},{5... | collective-permute-start | bytes 786440 | tf_op jit(solution)/shard_map/ppermute | solution.py:249
  53.1 11.6 %collective-permute-start.21 = (f32[128,256]{1,0:T(8,128)S(1)}, f32[128,256]{1,0:T(8,128)S(1)}, u32[]{:S(2)}, u32[]{:S(2)}) collective-permute-start(f32[128,256]{1,0:T(8,128)S(1)} %get-tuple-element.36), channel_id=1, source_target_pairs={{0,8},{4,12},{8,0},{12,4},{16,24},{20,28},{24,16},{28,20},{1,9},{5... | collective-permute-start | bytes 393224 | tf_op jit(solution)/shard_map/ppermute | solution.py:245
  60.6 8.4 %collective-permute-start.22 = (f32[128,256]{1,0:T(8,128)S(1)}, f32[128,256]{1,0:T(8,128)S(1)}, u32[]{:S(2)}, u32[]{:S(2)}) collective-permute-start(f32[128,256]{1,0:T(8,128)S(1)} %get-tuple-element.37), channel_id=1, source_target_pairs={{0,16},{4,20},{8,24},{12,28},{16,0},{20,4},{24,8},{28,12},{1,17},{... | collective-permute-start | bytes 393224 | tf_op jit(solution)/shard_map/ppermute | solution.py:245
  60.8 8.1 %copy-start.2 = (f32[128,256]{1,0:T(8,128)S(1)}, f32[128,256]{1,0:T(8,128)}, u32[]{:S(2)}) copy-start(f32[128,256]{1,0:T(8,128)} %refs_0_.1) | copy-start | bytes 393220
  60.8 8.1 %collective-permute-start.23 = (f32[128,256]{1,0:T(8,128)S(1)}, f32[128,256]{1,0:T(8,128)S(1)}, u32[]{:S(2)}, u32[]{:S(2)}) collective-permute-start(f32[128,256]{1,0:T(8,128)S(1)} %get-tuple-element.38), channel_id=1, source_target_pairs={{0,24},{4,28},{8,16},{12,20},{16,8},{20,12},{24,0},{28,4},{1,25},{... | collective-permute-start | bytes 393224 | tf_op jit(solution)/shard_map/ppermute | solution.py:245

commit v3 on v2

--- a/solution.py
+++ b/solution.py
@@ -31,9 +31,10 @@
     return lax.div(panel, 2), lax.rem(panel, 2)
 
 
-def call(kernel, outs, args, scratch=(), products=0, after=()):
+def call(kernel, outs, args, scratch=(), products=0, hbm=0, after=()):
     size = sum(a.size * 4 for a in args) + sum(math.prod(o) * 4 for o in outs)
     inputs = len(args)
+    args = [*args[: inputs - hbm], *(pltpu.with_memory_space_constraint(a, pltpu.HBM) for a in args[inputs - hbm :])]
 
     def body(*refs):
         kernel(*refs[:inputs], *refs[inputs + len(after) :])
@@ -41,7 +42,7 @@
     return pl.pallas_call(
         body,
         out_shape=[jax.ShapeDtypeStruct(o, jnp.float32) for o in outs],
-        in_specs=[VMEM] * inputs + [ANY] * len(after),
+        in_specs=[VMEM] * (inputs - hbm) + [HBM] * hbm + [ANY] * len(after),
         out_specs=[VMEM] * len(outs),
         scratch_shapes=list(scratch),
         compiler_params=pltpu.CompilerParams(vmem_limit_bytes=40 << 20),
@@ -49,6 +50,10 @@
     )(*args, *after)
 
 
+def shifts(count):
+    return [0] + sorted(range(1, count), key=lambda s: (min(s, count - s), s))
+
+
 def shard_rows(count, shift, height):
     start = lax.rem(lax.axis_index("row") + count - shift, count) * height
     return pl.ds(pl.multiple_of(start, height), height)
@@ -60,32 +65,35 @@
 
 def chunked(ref, chunks, *index):
     height = ref.shape[-2] // chunks
-    return [
-        ref[(chip, *index, slice(k * height, (k + 1) * height))] for k in range(chunks) for chip in range(ref.shape[0])
-    ]
-
-
-def extract(chunks, slab, bound, kept, entering):
-    _, core = chip_and_core()
-    kept[...] = jnp.concatenate(chunked(slab, chunks, core))
-    entering[...] = jnp.concatenate(chunked(bound, chunks, core))
+    return jnp.concatenate(
+        [ref[(chip, *index, slice(k * height, (k + 1) * height))] for k in range(chunks) for chip in range(ref.shape[0])]
+    )
 
 
 def prepare(count, chunks, *refs):
     refs = iter(refs)
     own, other = take(refs, count), take(refs, count)
-    coupling, given, kept, bound = take(refs, 4)
+    given, coupling, slab, bound = take(refs, 4)
     map_ref, both_ref, coupling_out = take(refs, 3)
     part_refs, carry_refs = take(refs, chunks), take(refs, chunks)
-    inverse, beneath, part = take(refs, 3)
+    inverse, beneath, part, kept, entering, sems = take(refs, 6)
     chip, core = chip_and_core()
-    coupling_out[...] = coupling[...]
+    slab_copy = pltpu.make_async_copy(slab.at[:, core], kept, sems.at[0])
+    bound_copy = pltpu.make_async_copy(bound.at[:, core], entering, sems.at[1])
+    coupling_copy = pltpu.make_async_copy(coupling, coupling_out, sems.at[2])
+    slab_copy.start()
+
+    @pl.when(chip == 0)
+    def _():
+        bound_copy.start()
+
+    coupling_copy.start()
     height = own[0].shape[0] // 2
-    for shift in range(count):
+    for at, shift in enumerate(shifts(count)):
         rows = shard_rows(count, shift, height)
         for slot, shards in ((core, own), (1 - core, other)):
-            inverse[slot, rows, :] = shards[shift][:height, :]
-            beneath[slot, rows, :] = shards[shift][height:, :]
+            inverse[slot, rows, :] = shards[at][:height, :]
+            beneath[slot, rows, :] = shards[at][height:, :]
     inverse_a, inverse_b = split(inverse[0]), split(inverse[1])
     map_a = dot3(inverse_a, split(beneath[0]), NN)
     map_b = dot3(inverse_b, split(beneath[1]), NN)
@@ -93,20 +101,24 @@
     map_ref[...] = map_a
     both_ref[...] = dot3(parts_b, parts_a, NN)
     first = core == 0
-    got = jnp.concatenate(chunked(given, chunks, core))
-    part[...] = dot3(split(jnp.where(first, kept[...], got)), inverse_a, NT)
+    got = chunked(given, chunks, core)
+    slab_copy.wait()
+    keep = chunked(kept, chunks)
+    part[...] = dot3(split(jnp.where(first, keep, got)), inverse_a, NT)
 
     @pl.when(chip == 0)
     def _():
-        part[...] -= dot3(split(bound[...]), parts_a, NT)
-
-    carry = dot3(split(jnp.where(first, got, kept[...])), inverse_b, NT)
+        bound_copy.wait()
+        part[...] -= dot3(split(chunked(entering, chunks)), parts_a, NT)
+
+    carry = dot3(split(jnp.where(first, got, keep)), inverse_b, NT)
     carry -= dot3(split(part[...]), parts_b, NT)
     height = carry.shape[0] // chunks
     for k in range(chunks):
         rows = slice(k * height, (k + 1) * height)
         part_refs[k][...] = part[rows, :]
         carry_refs[k][...] = carry[rows]
+    coupling_copy.wait()
 
 
 def inclusive(carry, prior, both, out):
@@ -208,8 +220,8 @@
 def stacked(count, *refs):
     *shards, out = refs
     height = shards[0].shape[0]
-    for shift in range(count):
-        out[shard_rows(count, shift, height), :] = shards[shift][...]
+    for at, shift in enumerate(shifts(count)):
+        out[shard_rows(count, shift, height), :] = shards[at][...]
 
 
 def interleave(chips, chunks, *refs):
@@ -250,9 +262,8 @@
 
 
 def gather_rows(value, count):
-    order = sorted(range(1, count), key=lambda s: min(s, count - s))
-    sent = {s: lax.ppermute(value, "row", [(j, (j + s) % count) for j in range(count)]) for s in order}
-    return [value] + [sent[s] for s in range(1, count)]
+    moved = [lax.ppermute(value, "row", [(j, (j + s) % count) for j in range(count)]) for s in shifts(count)[1:]]
+    return [value, *moved]
 
 
 def on_device(slab, boundary, diag_inverse, sub_block, tail_coupling, tail_cols):
@@ -272,16 +283,23 @@
     square = (width, width)
     part = (held, width)
     slice_shape = (held // CHUNKS, width)
-    kept, bound = call(functools.partial(extract, CHUNKS), [part] * 2, [blocks(slab), blocks(boundary)])
     map_a, both, coupling, *made = call(
         functools.partial(prepare, count, CHUNKS),
         [square, square, tail_coupling.shape] + [slice_shape] * (2 * CHUNKS),
-        [*own, *other, tail_coupling, blocks(across_slab), kept, bound],
-        [pltpu.VMEM((2, *square), jnp.float32)] * 2 + [pltpu.VMEM(part, jnp.float32)],
+        [*own, *other, blocks(across_slab), tail_coupling, blocks(slab), blocks(boundary)],
+        [pltpu.VMEM((2, *square), jnp.float32)] * 2
+        + [pltpu.VMEM(part, jnp.float32)]
+        + [pltpu.VMEM((chips, piece, width), jnp.float32)] * 2
+        + [pltpu.SemaphoreType.DMA((3,))],
         width * width * (3 * width + 4 * held),
+        hbm=3,
     )
     parts, carries = made[:CHUNKS], made[CHUNKS:]
 
+    def spread(after):
+        return call(functools.partial(stacked, count), [square], gather_rows(coupling, count), after=after)[0]
+
+    own_coupling = None
     priors, across = None, None
     half = 1
     while True:
@@ -293,8 +311,9 @@
         for k in range(CHUNKS):
             value = carries[k]
             if priors is not None:
-                if k == CHUNKS - 1:
-                    done.append(across)
+                if k == CHUNKS - 1 and last:
+                    own_coupling = spread(done)
+                    done.append(own_coupling)
                 (value,) = call(inclusive, [slice_shape], [value, priors[k], both], (), width * value.size, after=done)
                 done = [value]
             arrived.append(
@@ -326,7 +345,8 @@
             break
         half *= 2
 
-    (own_coupling,) = call(functools.partial(stacked, count), [square], gather_rows(coupling, count), after=[value])
+    if own_coupling is None:
+        own_coupling = spread([])
     other_coupling = to_other_core(own_coupling)
     arrivals = len(arrived[0])
     stays, leaves = [], []

time: 70 us -> 63.2 us (0.903)
  waiting for transfers between devices: 31 us -> 22.7 us
  starting transfers between devices: 27.7 us -> 31.8 us
  local copies, waits for them, and re-layouts: 4.02 us -> 0.86 us
  Pallas kernels: 6 us -> 6.73 us
    ppermute x10, waiting for transfers between devices: 12.1 us -> 6.33 us  [between_chips(): return lax.ppermute(value, 'panel', pairs)]
    ppermute x10, starting transfers between devices: 16.7 us -> 21 us  [between_chips(): return lax.ppermute(value, 'panel', pairs)]
    ppermute x6, waiting for transfers between devices: 18.9 us -> 15 us  [gather_rows(): lax.ppermute(value, 'row', [(j, (j + s) % count) for j in range(count)])]
    unnamed x11 -> x5, local copies, waits for them, and re-layouts: 4.01 us -> 0.85 us
    ppermute x8, waiting for transfers between devices: 0.02 us -> 1.31 us  [to_other_core(): lax.ppermute(value, 'panel', [(q, q ^ 1) for q in range(lax.axis_size('pa...]
    pallas_call x9 -> x8, Pallas kernels: 4.91 us -> 5.64 us  [call(): pl.pallas_call(body, out_shape=[jax.ShapeDtypeStruct(o, jnp.float32) for...]
  transfers between devices with their start and end apart: 24 -> 24, of which waited for: 8 -> 9; matrix products, arithmetic and copies ran while one was open for 1% -> 1% of each run, Pallas kernels for 5% -> 5%
where the time goes in v3:
time: 63.2 us; the launch traced here: 62.9 us
  starting transfers between devices  31.8 us (50%)
  waiting for transfers between devices  22.7 us (36%)
  Pallas kernels  6.73 us (11%)
  local copies, waits for them, and re-layouts  0.86 us (1%)
  between operations  0.84 us (1%)
    ppermute x10, starting transfers between devices, between_chips(): return lax.ppermute(value, 'panel', pairs)  21 us
    ppermute x6, waiting for transfers between devices, gather_rows(): lax.ppermute(value, 'row', [(j, (j + s) % count) for j in range(count)])  15 us
    ppermute x6, starting transfers between devices, gather_rows(): lax.ppermute(value, 'row', [(j, (j + s) % count) for j in range(count)])  9.55 us
    ppermute x10, waiting for transfers between devices, between_chips(): return lax.ppermute(value, 'panel', pairs)  6.33 us
    pallas_call x8, Pallas kernels, call(): pl.pallas_call(body, out_shape=[jax.ShapeDtypeStruct(o, jnp.float32) for...  5.64 us
    ppermute x8, waiting for transfers between devices, to_other_core(): lax.ppermute(value, 'panel', [(q, q ^ 1) for q in range(lax.axis_size('pa...  1.31 us
    ppermute x8, starting transfers between devices, to_other_core(): lax.ppermute(value, 'panel', [(q, q ^ 1) for q in range(lax.axis_size('pa...  1.28 us
  transfers between devices with their start and end apart: 24, of which 9 were waited for; matrix products, arithmetic and copies ran while one was open for 1% of the time, Pallas kernels for 5%

profile of v3, /device:TPU:0, one launch (start us, length us, event | category | flops | bytes accessed | tf_op | source)
XLA Modules:
  0.0 62.9 jit_solution(2556322835912383909)
XLA Ops:
  0.6 0.0 copy-start.1
  0.6 0.5 collective-permute-start.7
  1.2 0.8 %constant_dynamic-update-slice_fusion.1 = f32[128,256]{1,0:T(8,128)S(1)} fusion(f32[64,256]{1,0:T(8,128)} %param.8), kind=kLoop, calls=%fused_computation.1 | loop fusion | bytes 131072
  2.0 0.0 copy-done.1
  2.0 2.6 %collective-permute-start = (f32[128,256]{1,0:T(8,128)S(1)}, f32[128,256]{1,0:T(8,128)S(1)}, u32[]{:S(2)}, u32[]{:S(2)}) collective-permute-start(f32[128,256]{1,0:T(8,128)S(1)} %constant_dynamic-update-slice_fusion.refs_0_), channel_id=1, source_target_pairs={{0,1},{1,2},{2,3},{3,0},{4,5},{5,6},{6,7},{7,4},{8,9},{9,10},{10,1... | collective-permute-start | bytes 393224 | tf_op jit(solution)/shard_map/ppermute | solution.py:265
  4.7 2.1 %collective-permute-start.1 = (f32[128,256]{1,0:T(8,128)S(1)}, f32[128,256]{1,0:T(8,128)S(1)}, u32[]{:S(2)}, u32[]{:S(2)}) collective-permute-start(f32[128,256]{1,0:T(8,128)S(1)} %constant_dynamic-update-slice_fusion.refs_0_), channel_id=1, source_target_pairs={{0,3},{1,0},{2,1},{3,2},{4,7},{5,4},{6,5},{7,6},{8,11},{9,8},{10,9... | collective-permute-start | bytes 393224 | tf_op jit(solution)/shard_map/ppermute | solution.py:265
  6.7 0.9 %collective-permute-start.2 = (f32[128,256]{1,0:T(8,128)S(1)}, f32[128,256]{1,0:T(8,128)S(1)}, u32[]{:S(2)}, u32[]{:S(2)}) collective-permute-start(f32[128,256]{1,0:T(8,128)S(1)} %constant_dynamic-update-slice_fusion.refs_0_), channel_id=1, source_target_pairs={{0,2},{1,3},{2,0},{3,1},{4,6},{5,7},{6,4},{7,5},{8,10},{9,11},{10,... | collective-permute-start | bytes 393224 | tf_op jit(solution)/shard_map/ppermute | solution.py:265
  7.7 0.0 collective-permute-start.3
  7.7 3.4 %collective-permute-done.refs_1_ = f32[128,256]{1,0:T(8,128)S(1)} collective-permute-done((f32[128,256]{1,0:T(8,128)S(1)}, f32[128,256]{1,0:T(8,128)S(1)}, u32[]{:S(2)}, u32[]{:S(2)}) %collective-permute-start) | collective-permute-done | bytes 131104 | tf_op jit(solution)/shard_map/ppermute | solution.py:265
  11.1 0.0 collective-permute-start.4
  11.1 2.0 %collective-permute-done.1.refs_2_ = f32[128,256]{1,0:T(8,128)S(1)} collective-permute-done((f32[128,256]{1,0:T(8,128)S(1)}, f32[128,256]{1,0:T(8,128)S(1)}, u32[]{:S(2)}, u32[]{:S(2)}) %collective-permute-start.1) | collective-permute-done | bytes 131104 | tf_op jit(solution)/shard_map/ppermute | solution.py:265
  13.1 0.0 collective-permute-start.5
  13.1 6.2 %collective-permute-done.2.refs_3_ = f32[128,256]{1,0:T(8,128)S(1)} collective-permute-done((f32[128,256]{1,0:T(8,128)S(1)}, f32[128,256]{1,0:T(8,128)S(1)}, u32[]{:S(2)}, u32[]{:S(2)}) %collective-permute-start.2) | collective-permute-done | bytes 131104 | tf_op jit(solution)/shard_map/ppermute | solution.py:265
  19.3 0.0 collective-permute-start.6
  19.3 0.0 collective-permute-done.3.refs_4_
  19.3 0.0 collective-permute-done.4.refs_5_
  19.3 0.0 collective-permute-done.5.refs_6_
  19.3 1.3 %collective-permute-done.6.refs_7_ = f32[128,256]{1,0:T(8,128)S(1)} collective-permute-done((f32[128,256]{1,0:T(8,128)S(1)}, f32[128,256]{1,0:T(8,128)S(1)}, u32[]{:S(2)}, u32[]{:S(2)}) %collective-permute-start.6) | collective-permute-done | bytes 131104 | tf_op jit(solution)/shard_map/ppermute | solution.py:261
  20.6 0.0 collective-permute-done.7
  20.6 2.8 %shard_map.77 = (f32[256,256]{1,0:T(8,128)S(1)}, f32[256,256]{1,0:T(8,128)S(1)}, f32[64,256]{1,0:T(8,128)S(1)}, f32[256,256]{1,0:T(8,128)S(1)}, f32[256,256]{1,0...) custom-call(f32[128,256]{1,0:T(8,128)S(1)} %constant_dynamic-update-slice_fusion.refs_0_, ...), custom_call_target="tpu_custom_call" | custom-call | flops 1107296256 | bytes 5898240 | tf_op jit(solution)/shard_map/pallas_call | solution.py:42
  23.4 3.0 %collective-permute-start.8 = (f32[256,256]{1,0:T(8,128)S(1)}, f32[256,256]{1,0:T(8,128)S(1)}, u32[]{:S(2)}, u32[]{:S(2)}) collective-permute-start(f32[256,256]{1,0:T(8,128)S(1)} %get-tuple-element.20.refs_0_.refs_1_), channel_id=1, source_target_pairs={{0,8},{4,12},{16,24},{20,28},{1,9},{5,13},{17,25},{21,29},{2,10},{... | collective-permute-start | bytes 786440 | tf_op jit(solution)/shard_map/ppermute | solution.py:257
  26.4 1.3 %collective-permute-start.12 = (f32[256,256]{1,0:T(8,128)S(1)}, f32[256,256]{1,0:T(8,128)S(1)}, u32[]{:S(2)}, u32[]{:S(2)}) collective-permute-start(f32[256,256]{1,0:T(8,128)S(1)} %get-tuple-element.25.refs_0_.refs_1_), channel_id=1, source_target_pairs={{0,8},{4,12},{16,24},{20,28},{1,9},{5,13},{17,25},{21,29},{2,10},{... | collective-permute-start | bytes 786440 | tf_op jit(solution)/shard_map/ppermute | solution.py:257
  27.7 0.7 %collective-permute-start.9 = (f32[256,256]{1,0:T(8,128)S(1)}, f32[256,256]{1,0:T(8,128)S(1)}, u32[]{:S(2)}, u32[]{:S(2)}) collective-permute-start(f32[256,256]{1,0:T(8,128)S(1)} %get-tuple-element.22.refs_2_.refs_4_), channel_id=1, source_target_pairs={{16,24},{20,28},{17,25},{21,29},{18,26},{22,30},{19,27},{23,31}} | collective-permute-start | bytes 786440 | tf_op jit(solution)/shard_map/ppermute | solution.py:257
  28.4 0.1 collective-permute-start.13
  28.5 3.8 %collective-permute-start.14 = (f32[64,256]{1,0:T(8,128)S(1)}, f32[64,256]{1,0:T(8,128)S(1)}, u32[]{:S(2)}, u32[]{:S(2)}) collective-permute-start(f32[64,256]{1,0:T(8,128)S(1)} %get-tuple-element.26.refs_0_), channel_id=1, source_target_pairs={{0,3},{1,0},{2,1},{3,2},{4,7},{5,4},{6,5},{7,6},{8,11},{9,8},{10,9... | collective-permute-start | bytes 196616 | tf_op jit(solution)/shard_map/ppermute | solution.py:265
  32.3 0.8 %collective-permute-done.8.refs_1_.refs_2_ = f32[256,256]{1,0:T(8,128)S(1)} collective-permute-done((f32[256,256]{1,0:T(8,128)S(1)}, f32[256,256]{1,0:T(8,128)S(1)}, u32[]{:S(2)}, u32[]{:S(2)}) %collective-permute-start.8) | collective-permute-done | bytes 262176 | tf_op jit(solution)/shard_map/ppermute | solution.py:257
  33.0 0.0 collective-permute-start.15
  33.0 0.3 shard_map.78.refs_4_.refs_3_
  33.3 1.9 %collective-permute-done.13.refs_1_ = f32[64,256]{1,0:T(8,128)S(1)} collective-permute-done((f32[64,256]{1,0:T(8,128)S(1)}, f32[64,256]{1,0:T(8,128)S(1)}, u32[]{:S(2)}, u32[]{:S(2)}) %collective-permute-start.13) | collective-permute-done | bytes 65568 | tf_op jit(solution)/shard_map/ppermute | solution.py:265
  35.2 0.7 %collective-permute-start.10 = (f32[256,256]{1,0:T(8,128)S(1)}, f32[256,256]{1,0:T(8,128)S(1)}, u32[]{:S(2)}, u32[]{:S(2)}) collective-permute-start(f32[256,256]{1,0:T(8,128)S(1)} %shard_map.78.refs_4_.refs_3_), channel_id=1, source_target_pairs={{8,24},{12,28},{9,25},{13,29},{10,26},{14,30},{11,27},{15,31}} | collective-permute-start | bytes 786440 | tf_op jit(solution)/shard_map/ppermute | solution.py:257
  35.9 0.0 collective-permute-done.14.refs_2_
  35.9 0.7 %collective-permute-start.11 = (f32[256,256]{1,0:T(8,128)S(1)}, f32[256,256]{1,0:T(8,128)S(1)}, u32[]{:S(2)}, u32[]{:S(2)}) collective-permute-start(f32[256,256]{1,0:T(8,128)S(1)} %shard_map.78.refs_4_.refs_3_), channel_id=1, source_target_pairs={{8,16},{12,20},{9,17},{13,21},{10,18},{14,22},{11,19},{15,23}} | collective-permute-start | bytes 786440 | tf_op jit(solution)/shard_map/ppermute | solution.py:257
  36.6 1.6 %collective-permute-done.15.refs_3_ = f32[64,256]{1,0:T(8,128)S(1)} collective-permute-done((f32[64,256]{1,0:T(8,128)S(1)}, f32[64,256]{1,0:T(8,128)S(1)}, u32[]{:S(2)}, u32[]{:S(2)}) %collective-permute-start.15) | collective-permute-done | bytes 65568 | tf_op jit(solution)/shard_map/ppermute | solution.py:265
  38.2 0.0 collective-permute-done.12.refs_1_.refs_2_
  38.2 0.3 shard_map.81
  38.6 0.7 %collective-permute-start.16 = (f32[256,256]{1,0:T(8,128)S(1)}, f32[256,256]{1,0:T(8,128)S(1)}, u32[]{:S(2)}, u32[]{:S(2)}) collective-permute-start(f32[256,256]{1,0:T(8,128)S(1)} %shard_map.81), channel_id=1, source_target_pairs={{8,24},{12,28},{9,25},{13,29},{10,26},{14,30},{11,27},{15,31}} | collective-permute-start | bytes 786440 | tf_op jit(solution)/shard_map/ppermute | solution.py:257
  39.2 0.7 %collective-permute-start.17 = (f32[256,256]{1,0:T(8,128)S(1)}, f32[256,256]{1,0:T(8,128)S(1)}, u32[]{:S(2)}, u32[]{:S(2)}) collective-permute-start(f32[256,256]{1,0:T(8,128)S(1)} %shard_map.81), channel_id=1, source_target_pairs={{8,16},{12,20},{9,17},{13,21},{10,18},{14,22},{11,19},{15,23}} | collective-permute-start | bytes 786440 | tf_op jit(solution)/shard_map/ppermute | solution.py:257
  39.9 0.0 collective-permute-done.9.refs_5_
  39.9 0.1 collective-permute-start.20
  40.0 0.0 collective-permute-done.10.refs_6_
  40.0 0.0 collective-permute-done.11.refs_7_
  40.0 0.5 shard_map.79
  40.5 0.5 collective-permute-start.18
  41.1 0.0 collective-permute-done.16.refs_6_
  41.1 0.0 collective-permute-done.17.refs_7_
  41.1 0.5 shard_map.82
  41.5 0.1 collective-permute-start.19
  41.6 0.0 collective-permute-done.20.refs_5_
  41.6 0.6 shard_map.84
  42.3 10.2 %collective-permute-start.21 = (f32[128,256]{1,0:T(8,128)S(1)}, f32[128,256]{1,0:T(8,128)S(1)}, u32[]{:S(2)}, u32[]{:S(2)}) collective-permute-start(f32[128,256]{1,0:T(8,128)S(1)} %get-tuple-element.32), channel_id=1, source_target_pairs={{0,8},{4,12},{8,0},{12,4},{16,24},{20,28},{24,16},{28,20},{1,9},{5... | collective-permute-start | bytes 393224 | tf_op jit(solution)/shard_map/ppermute | solution.py:257
  52.4 1.7 %collective-permute-start.22 = (f32[128,256]{1,0:T(8,128)S(1)}, f32[128,256]{1,0:T(8,128)S(1)}, u32[]{:S(2)}, u32[]{:S(2)}) collective-permute-start(f32[128,256]{1,0:T(8,128)S(1)} %get-tuple-element.33), channel_id=1, source_target_pairs={{0,16},{4,20},{8,24},{12,28},{16,0},{20,4},{24,8},{28,12},{1,17},{... | collective-permute-start | bytes 393224 | tf_op jit(solution)/shard_map/ppermute | solution.py:257
  54.2 0.0 copy-start
  54.2 1.4 %collective-permute-start.23 = (f32[128,256]{1,0:T(8,128)S(1)}, f32[128,256]{1,0:T(8,128)S(1)}, u32[]{:S(2)}, u32[]{:S(2)}) collective-permute-start(f32[128,256]{1,0:T(8,128)S(1)} %get-tuple-element.34), channel_id=1, source_target_pairs={{0,24},{4,28},{8,16},{12,20},{16,8},{20,12},{24,0},{28,4},{1,25},{... | collective-permute-start | bytes 393224 | tf_op jit(solution)/shard_map/ppermute | solution.py:257
  55.5 0.0 collective-permute-done.18.refs_2_
  55.5 0.0 collective-permute-done.19.refs_3_
  55.6 1.1 %shard_map.83 = (f32[4,2,128,256]{3,2,1,0:T(8,128)}, f32[8,128]{1,0:T(8,128)S(1)}) custom-call(f32[256,256]{1,0:T(8,128)S(1)} %get-tuple-element.23.refs_8_.refs_0_, f32[256,256]{1,0:T(8,128)S(1)} %get-tuple-element.27.refs_1_, f32[256,256]{1,0:T(8,128)S(1)} %collective-permute-done.18.refs_2_, f32[256,256]{1,0:T(8,128)S(1)} %collective-permute-done.19.refs_3_), custom_call_target="tpu_custom_call" | custom-call | bytes 2097152 | tf_op jit(solution)/shard_map/pallas_call | solution.py:375
  56.6 0.0 collective-permute-done.21.refs_2_
  56.7 3.7 %collective-permute-done.22.refs_3_ = f32[128,256]{1,0:T(8,128)S(1)} collective-permute-done((f32[128,256]{1,0:T(8,128)S(1)}, f32[128,256]{1,0:T(8,128)S(1)}, u32[]{:S(2)}, u32[]{:S(2)}) %collective-permute-start.22) | collective-permute-done | bytes 131104 | tf_op jit(solution)/shard_map/ppermute | solution.py:257
  60.4 1.8 %collective-permute-done.23.refs_4_ = f32[128,256]{1,0:T(8,128)S(1)} collective-permute-done((f32[128,256]{1,0:T(8,128)S(1)}, f32[128,256]{1,0:T(8,128)S(1)}, u32[]{:S(2)}, u32[]{:S(2)}) %collective-permute-start.23) | collective-permute-done | bytes 131104 | tf_op jit(solution)/shard_map/ppermute | solution.py:257
  62.2 0.0 copy-done
  62.2 0.7 %shard_map.85 = f32[128,256]{1,0:T(8,128)} custom-call(f32[128,256]{1,0:T(8,128)S(1)} %copy-done, f32[128,256]{1,0:T(8,128)S(1)} %get-tuple-element.31.refs_1_, f32[128,256]{1,0:T(8,128)S(1)} %collective-permute-done.21.refs_2_, f32[128,256]{1,0:T(8,128)S(1)} %collective-permute-done.22.refs_3_, f32[128,256]{1,0:T(8,128)S(1)} %collective-permute-done.23.refs_4_, ...), custom_call_target="tpu_custom_call" | custom-call | bytes 786432 | tf_op jit(solution)/shard_map/pallas_call | solution.py:42
  (2 shorter events, 0.0 us)
Async XLA Ops:
  0.6 1.4 %copy-start.1 = (f32[64,256]{1,0:T(8,128)S(1)}, f32[64,256]{1,0:T(8,128)}, u32[]{:S(2)}) copy-start(f32[64,256]{1,0:T(8,128)} %param.9) | copy-start | bytes 196612
  0.6 20.0 %collective-permute-start.7 = (f32[1024,256]{1,0:T(8,128)}, f32[1024,256]{1,0:T(8,128)S(1)}, u32[]{:S(2)}, u32[]{:S(2)}) collective-permute-start(f32[1024,256]{1,0:T(8,128)} %param.6), channel_id=1, source_target_pairs={{0,4},{4,0},{8,12},{12,8},{16,20},{20,16},{24,28},{28,24},{1,5},{5... | collective-permute-start | bytes 3145736 | tf_op jit(solution)/shard_map/ppermute | solution.py:261
  2.0 9.1 %collective-permute-start = (f32[128,256]{1,0:T(8,128)S(1)}, f32[128,256]{1,0:T(8,128)S(1)}, u32[]{:S(2)}, u32[]{:S(2)}) collective-permute-start(f32[128,256]{1,0:T(8,128)S(1)} %constant_dynamic-update-slice_fusion.refs_0_), channel_id=1, source_target_pairs={{0,1},{1,2},{2,3},{3,0},{4,5},{5,6},{6,7},{7,4},{8,9},{9,10},{10,1... | collective-permute-start | bytes 393224 | tf_op jit(solution)/shard_map/ppermute | solution.py:265
  4.7 8.4 %collective-permute-start.1 = (f32[128,256]{1,0:T(8,128)S(1)}, f32[128,256]{1,0:T(8,128)S(1)}, u32[]{:S(2)}, u32[]{:S(2)}) collective-permute-start(f32[128,256]{1,0:T(8,128)S(1)} %constant_dynamic-update-slice_fusion.refs_0_), channel_id=1, source_target_pairs={{0,3},{1,0},{2,1},{3,2},{4,7},{5,4},{6,5},{7,6},{8,11},{9,8},{10,9... | collective-permute-start | bytes 393224 | tf_op jit(solution)/shard_map/ppermute | solution.py:265
  6.7 12.5 %collective-permute-start.2 = (f32[128,256]{1,0:T(8,128)S(1)}, f32[128,256]{1,0:T(8,128)S(1)}, u32[]{:S(2)}, u32[]{:S(2)}) collective-permute-start(f32[128,256]{1,0:T(8,128)S(1)} %constant_dynamic-update-slice_fusion.refs_0_), channel_id=1, source_target_pairs={{0,2},{1,3},{2,0},{3,1},{4,6},{5,7},{6,4},{7,5},{8,10},{9,11},{10,... | collective-permute-start | bytes 393224 | tf_op jit(solution)/shard_map/ppermute | solution.py:265
  7.7 11.6 %collective-permute-start.3 = (f32[128,256]{1,0:T(8,128)S(1)}, f32[128,256]{1,0:T(8,128)S(1)}, u32[]{:S(2)}, u32[]{:S(2)}) collective-permute-start(f32[128,256]{1,0:T(8,128)S(1)} %constant_dynamic-update-slice_fusion.refs_0_), channel_id=1, source_target_pairs={{0,4},{4,0},{8,12},{12,8},{16,20},{20,16},{24,28},{28,24},{1,5},{5... | collective-permute-start | bytes 393224 | tf_op jit(solution)/shard_map/ppermute | solution.py:261
  11.1 8.2 %collective-permute-start.4 = (f32[128,256]{1,0:T(8,128)S(1)}, f32[128,256]{1,0:T(8,128)S(1)}, u32[]{:S(2)}, u32[]{:S(2)}) collective-permute-start(f32[128,256]{1,0:T(8,128)S(1)} %collective-permute-done.refs_1_), channel_id=1, source_target_pairs={{0,4},{4,0},{8,12},{12,8},{16,20},{20,16},{24,28},{28,24},{1,5},{5... | collective-permute-start | bytes 393224 | tf_op jit(solution)/shard_map/ppermute | solution.py:261
  13.1 6.2 %collective-permute-start.5 = (f32[128,256]{1,0:T(8,128)S(1)}, f32[128,256]{1,0:T(8,128)S(1)}, u32[]{:S(2)}, u32[]{:S(2)}) collective-permute-start(f32[128,256]{1,0:T(8,128)S(1)} %collective-permute-done.1.refs_2_), channel_id=1, source_target_pairs={{0,4},{4,0},{8,12},{12,8},{16,20},{20,16},{24,28},{28,24},{1,5},{5... | collective-permute-start | bytes 393224 | tf_op jit(solution)/shard_map/ppermute | solution.py:261
  19.3 1.3 %collective-permute-start.6 = (f32[128,256]{1,0:T(8,128)S(1)}, f32[128,256]{1,0:T(8,128)S(1)}, u32[]{:S(2)}, u32[]{:S(2)}) collective-permute-start(f32[128,256]{1,0:T(8,128)S(1)} %collective-permute-done.2.refs_3_), channel_id=1, source_target_pairs={{0,4},{4,0},{8,12},{12,8},{16,20},{20,16},{24,28},{28,24},{1,5},{5... | collective-permute-start | bytes 393224 | tf_op jit(solution)/shard_map/ppermute | solution.py:261
  23.4 9.6 %collective-permute-start.8 = (f32[256,256]{1,0:T(8,128)S(1)}, f32[256,256]{1,0:T(8,128)S(1)}, u32[]{:S(2)}, u32[]{:S(2)}) collective-permute-start(f32[256,256]{1,0:T(8,128)S(1)} %get-tuple-element.20.refs_0_.refs_1_), channel_id=1, source_target_pairs={{0,8},{4,12},{16,24},{20,28},{1,9},{5,13},{17,25},{21,29},{2,10},{... | collective-permute-start | bytes 786440 | tf_op jit(solution)/shard_map/ppermute | solution.py:257
  26.4 11.8 %collective-permute-start.12 = (f32[256,256]{1,0:T(8,128)S(1)}, f32[256,256]{1,0:T(8,128)S(1)}, u32[]{:S(2)}, u32[]{:S(2)}) collective-permute-start(f32[256,256]{1,0:T(8,128)S(1)} %get-tuple-element.25.refs_0_.refs_1_), channel_id=1, source_target_pairs={{0,8},{4,12},{16,24},{20,28},{1,9},{5,13},{17,25},{21,29},{2,10},{... | collective-permute-start | bytes 786440 | tf_op jit(solution)/shard_map/ppermute | solution.py:257
  27.7 12.2 %collective-permute-start.9 = (f32[256,256]{1,0:T(8,128)S(1)}, f32[256,256]{1,0:T(8,128)S(1)}, u32[]{:S(2)}, u32[]{:S(2)}) collective-permute-start(f32[256,256]{1,0:T(8,128)S(1)} %get-tuple-element.22.refs_2_.refs_4_), channel_id=1, source_target_pairs={{16,24},{20,28},{17,25},{21,29},{18,26},{22,30},{19,27},{23,31}} | collective-permute-start | bytes 786440 | tf_op jit(solution)/shard_map/ppermute | solution.py:257
  28.4 6.8 %collective-permute-start.13 = (f32[64,256]{1,0:T(8,128)S(1)}, f32[64,256]{1,0:T(8,128)S(1)}, u32[]{:S(2)}, u32[]{:S(2)}) collective-permute-start(f32[64,256]{1,0:T(8,128)S(1)} %get-tuple-element.26.refs_0_), channel_id=1, source_target_pairs={{0,1},{1,2},{2,3},{3,0},{4,5},{5,6},{6,7},{7,4},{8,9},{9,10},{10,1... | collective-permute-start | bytes 196616 | tf_op jit(solution)/shard_map/ppermute | solution.py:265
  28.5 7.4 %collective-permute-start.14 = (f32[64,256]{1,0:T(8,128)S(1)}, f32[64,256]{1,0:T(8,128)S(1)}, u32[]{:S(2)}, u32[]{:S(2)}) collective-permute-start(f32[64,256]{1,0:T(8,128)S(1)} %get-tuple-element.26.refs_0_), channel_id=1, source_target_pairs={{0,3},{1,0},{2,1},{3,2},{4,7},{5,4},{6,5},{7,6},{8,11},{9,8},{10,9... | collective-permute-start | bytes 196616 | tf_op jit(solution)/shard_map/ppermute | solution.py:265
  33.0 5.2 %collective-permute-start.15 = (f32[64,256]{1,0:T(8,128)S(1)}, f32[64,256]{1,0:T(8,128)S(1)}, u32[]{:S(2)}, u32[]{:S(2)}) collective-permute-start(f32[64,256]{1,0:T(8,128)S(1)} %get-tuple-element.26.refs_0_), channel_id=1, source_target_pairs={{0,2},{1,3},{2,0},{3,1},{4,6},{5,7},{6,4},{7,5},{8,10},{9,11},{10,... | collective-permute-start | bytes 196616 | tf_op jit(solution)/shard_map/ppermute | solution.py:265
  35.2 4.8 %collective-permute-start.10 = (f32[256,256]{1,0:T(8,128)S(1)}, f32[256,256]{1,0:T(8,128)S(1)}, u32[]{:S(2)}, u32[]{:S(2)}) collective-permute-start(f32[256,256]{1,0:T(8,128)S(1)} %shard_map.78.refs_4_.refs_3_), channel_id=1, source_target_pairs={{8,24},{12,28},{9,25},{13,29},{10,26},{14,30},{11,27},{15,31}} | collective-permute-start | bytes 786440 | tf_op jit(solution)/shard_map/ppermute | solution.py:257
  35.9 4.1 %collective-permute-start.11 = (f32[256,256]{1,0:T(8,128)S(1)}, f32[256,256]{1,0:T(8,128)S(1)}, u32[]{:S(2)}, u32[]{:S(2)}) collective-permute-start(f32[256,256]{1,0:T(8,128)S(1)} %shard_map.78.refs_4_.refs_3_), channel_id=1, source_target_pairs={{8,16},{12,20},{9,17},{13,21},{10,18},{14,22},{11,19},{15,23}} | collective-permute-start | bytes 786440 | tf_op jit(solution)/shard_map/ppermute | solution.py:257
  38.6 2.5 %collective-permute-start.16 = (f32[256,256]{1,0:T(8,128)S(1)}, f32[256,256]{1,0:T(8,128)S(1)}, u32[]{:S(2)}, u32[]{:S(2)}) collective-permute-start(f32[256,256]{1,0:T(8,128)S(1)} %shard_map.81), channel_id=1, source_target_pairs={{8,24},{12,28},{9,25},{13,29},{10,26},{14,30},{11,27},{15,31}} | collective-permute-start | bytes 786440 | tf_op jit(solution)/shard_map/ppermute | solution.py:257
  39.2 1.8 %collective-permute-start.17 = (f32[256,256]{1,0:T(8,128)S(1)}, f32[256,256]{1,0:T(8,128)S(1)}, u32[]{:S(2)}, u32[]{:S(2)}) collective-permute-start(f32[256,256]{1,0:T(8,128)S(1)} %shard_map.81), channel_id=1, source_target_pairs={{8,16},{12,20},{9,17},{13,21},{10,18},{14,22},{11,19},{15,23}} | collective-permute-start | bytes 786440 | tf_op jit(solution)/shard_map/ppermute | solution.py:257
  39.9 1.7 %collective-permute-start.20 = (f32[256,256]{1,0:T(8,128)S(1)}, f32[256,256]{1,0:T(8,128)S(1)}, u32[]{:S(2)}, u32[]{:S(2)}) collective-permute-start(f32[256,256]{1,0:T(8,128)S(1)} %shard_map.80.refs_4_), channel_id=1, source_target_pairs={{0,4},{4,0},{8,12},{12,8},{16,20},{20,16},{24,28},{28,24},{1,5},{5... | collective-permute-start | bytes 786440 | tf_op jit(solution)/shard_map/ppermute | solution.py:261
  40.5 15.0 %collective-permute-start.18 = (f32[256,256]{1,0:T(8,128)S(1)}, f32[256,256]{1,0:T(8,128)S(1)}, u32[]{:S(2)}, u32[]{:S(2)}) collective-permute-start(f32[256,256]{1,0:T(8,128)S(1)} %get-tuple-element.28.refs_2_), channel_id=1, source_target_pairs={{0,4},{4,0},{8,12},{12,8},{16,20},{20,16},{24,28},{28,24},{1,5},{5... | collective-permute-start | bytes 786440 | tf_op jit(solution)/shard_map/ppermute | solution.py:261
  41.5 14.0 %collective-permute-start.19 = (f32[256,256]{1,0:T(8,128)S(1)}, f32[256,256]{1,0:T(8,128)S(1)}, u32[]{:S(2)}, u32[]{:S(2)}) collective-permute-start(f32[256,256]{1,0:T(8,128)S(1)} %get-tuple-element.29.refs_3_), channel_id=1, source_target_pairs={{0,4},{4,0},{8,12},{12,8},{16,20},{20,16},{24,28},{28,24},{1,5},{5... | collective-permute-start | bytes 786440 | tf_op jit(solution)/shard_map/ppermute | solution.py:261
  42.3 14.4 %collective-permute-start.21 = (f32[128,256]{1,0:T(8,128)S(1)}, f32[128,256]{1,0:T(8,128)S(1)}, u32[]{:S(2)}, u32[]{:S(2)}) collective-permute-start(f32[128,256]{1,0:T(8,128)S(1)} %get-tuple-element.32), channel_id=1, source_target_pairs={{0,8},{4,12},{8,0},{12,4},{16,24},{20,28},{24,16},{28,20},{1,9},{5... | collective-permute-start | bytes 393224 | tf_op jit(solution)/shard_map/ppermute | solution.py:257
  52.4 7.9 %collective-permute-start.22 = (f32[128,256]{1,0:T(8,128)S(1)}, f32[128,256]{1,0:T(8,128)S(1)}, u32[]{:S(2)}, u32[]{:S(2)}) collective-permute-start(f32[128,256]{1,0:T(8,128)S(1)} %get-tuple-element.33), channel_id=1, source_target_pairs={{0,16},{4,20},{8,24},{12,28},{16,0},{20,4},{24,8},{28,12},{1,17},{... | collective-permute-start | bytes 393224 | tf_op jit(solution)/shard_map/ppermute | solution.py:257
  54.2 8.1 %copy-start = (f32[128,256]{1,0:T(8,128)S(1)}, f32[128,256]{1,0:T(8,128)}, u32[]{:S(2)}) copy-start(f32[128,256]{1,0:T(8,128)} %refs_0_.1) | copy-start | bytes 393220
  54.2 8.1 %collective-permute-start.23 = (f32[128,256]{1,0:T(8,128)S(1)}, f32[128,256]{1,0:T(8,128)S(1)}, u32[]{:S(2)}, u32[]{:S(2)}) collective-permute-start(f32[128,256]{1,0:T(8,128)S(1)} %get-tuple-element.34), channel_id=1, source_target_pairs={{0,24},{4,28},{8,16},{12,20},{16,8},{20,12},{24,0},{28,4},{1,25},{... | collective-permute-start | bytes 393224 | tf_op jit(solution)/shard_map/ppermute | solution.py:257

commit v4 on v3

v4 whole, which is shorter than its diff:
```python
import functools
import math

import jax
import jax.numpy as jnp
from jax import lax
from jax.experimental import pallas as pl
from jax.experimental.pallas import tpu as pltpu
from jax.sharding import PartitionSpec as P

CHUNKS = 2
FIRST = 1 / 2
NT = (((1,), (1,)), ((), ()))
NN = (((1,), (0,)), ((), ()))
VMEM = pl.BlockSpec(memory_space=pltpu.VMEM)
HBM = pl.BlockSpec(memory_space=pltpu.HBM)
ANY = pl.BlockSpec(memory_space=pl.ANY)


def split(x):
    high = x.astype(jnp.bfloat16)
    return high, (x - high.astype(jnp.float32)).astype(jnp.bfloat16)


def dot3(left, right, dims):
    dot = functools.partial(lax.dot_general, dimension_numbers=dims, preferred_element_type=jnp.float32)
    return dot(left[0], right[0]) + (dot(left[0], right[1]) + dot(left[1], right[0]))


def chip_and_core():
    panel = lax.axis_index("panel")
    return lax.div(panel, 2), lax.rem(panel, 2)


def call(kernel, outs, args, scratch=(), products=0, hbm=0, after=()):
    size = sum(a.size * 4 for a in args) + sum(math.prod(o) * 4 for o in outs)
    inputs = len(args)
    args = [*args[: inputs - hbm], *(pltpu.with_memory_space_constraint(a, pltpu.HBM) for a in args[inputs - hbm :])]

    def body(*refs):
        kernel(*refs[:inputs], *refs[inputs + len(after) :])

    return pl.pallas_call(
        body,
        out_shape=[jax.ShapeDtypeStruct(o, jnp.float32) for o in outs],
        in_specs=[VMEM] * (inputs - hbm) + [HBM] * hbm + [ANY] * len(after),
        out_specs=[VMEM] * len(outs),
        scratch_shapes=list(scratch),
        compiler_params=pltpu.CompilerParams(vmem_limit_bytes=40 << 20),
        cost_estimate=pl.CostEstimate(flops=6 * products, bytes_accessed=size, transcendentals=0),
    )(*args, *after)


def weight_shifts(count):
    return sorted(range(count), key=lambda s: (min(s, count - s), s))


def shard_rows(count, shift, height):
    start = lax.rem(lax.axis_index("row") + count - shift, count) * height
    return pl.ds(pl.multiple_of(start, height), height)


def take(refs, count):
    return [next(refs) for _ in range(count)]


def cuts(piece):
    unit = 16 if piece % 16 == 0 and piece > 16 else 8
    first = max(unit, int(piece * FIRST) // unit * unit)
    if piece % unit or first >= piece:
        first = piece // 2
    return [(0, first), (first, piece)]


def chunked(ref, *index):
    return jnp.concatenate(
        [ref[(chip, *index, slice(*cut))] for cut in cuts(ref.shape[-2]) for chip in range(ref.shape[0])]
    )


def fetch(slab, bound, coupling, kept, entering, coupling_out, sems):
    _, core = chip_and_core()
    copies = [
        pltpu.make_async_copy(source, target, sems.at[k])
        for k, (source, target) in enumerate(
            ((slab.at[:, core], kept), (bound.at[:, core], entering), (coupling, coupling_out))
        )
    ]
    for copy in copies:
        copy.start()
    for copy in copies:
        copy.wait()


def prepare(count, *refs):
    refs = iter(refs)
    own, other = take(refs, count), take(refs, count)
    given, kept, entering, coupling = take(refs, 4)
    map_ref, both_ref, coupling_out = take(refs, 3)
    part_refs, carry_refs = take(refs, CHUNKS), take(refs, CHUNKS)
    inverse, beneath, part = take(refs, 3)
    chip, core = chip_and_core()
    coupling_out[...] = coupling[...]
    height = own[0].shape[0] // 2
    for at, shift in enumerate(weight_shifts(count)):
        rows = shard_rows(count, shift, height)
        for slot, shards in ((core, own), (1 - core, other)):
            inverse[slot, rows, :] = shards[at][:height, :]
            beneath[slot, rows, :] = shards[at][height:, :]
    inverse_a, inverse_b = split(inverse[0]), split(inverse[1])
    map_ref[...] = dot3(inverse_a, split(beneath[0]), NN)
    map_a = split(map_ref[...])
    map_b = split(dot3(inverse_b, split(beneath[1]), NN))
    both_ref[...] = dot3(map_b, map_a, NN)
    first = core == 0
    got, keep = chunked(given, core), chunked(kept)
    part[...] = dot3(split(jnp.where(first, keep, got)), inverse_a, NT)

    @pl.when(chip == 0)
    def _():
        part[...] -= dot3(split(chunked(entering)), map_a, NT)

    carry = dot3(split(jnp.where(first, got, keep)), inverse_b, NT)
    carry -= dot3(split(part[...]), map_b, NT)
    start = 0
    for k in range(CHUNKS):
        end = start + part_refs[k].shape[0]
        part_refs[k][...] = part[start:end, :]
        carry_refs[k][...] = carry[start:end]
        start = end


def inclusive(carry, prior, both, out):
    out[...] = carry[...] + dot3(split(prior[...]), split(both[...]), NT)


def total(refs):
    value = refs[0][...]
    for more in refs[1:]:
        value = value + more[...]
    return value


def absorb(half, prior, across, arrived, put):
    chip, _ = chip_and_core()
    inner = lax.rem(chip, half) != 0

    @pl.when(inner)
    def _():
        put(prior[...] + dot3(split(total(arrived)), split(across[...]), NT))

    @pl.when(jnp.logical_not(inner))
    def _():
        put(prior[...] + total(arrived))


def advance(half, prior, across, *refs):
    *arrived, out = refs

    def put(value):
        out[...] = value

    absorb(half, prior, across, arrived, put)


def extend(half, across, arrived, out):
    chip, _ = chip_and_core()
    inner = lax.rem(chip, half) != 0
    upper = lax.rem(chip, 2 * half) >= half
    out[...] = across[...]

    @pl.when(jnp.logical_and(upper, inner))
    def _():
        out[...] = dot3(split(across[...]), split(arrived[...]), NN)

    @pl.when(jnp.logical_and(upper, jnp.logical_not(inner)))
    def _():
        out[...] = arrived[...]


def joined(half, both, across, out):
    chip, _ = chip_and_core()
    out[...] = both[...]

    @pl.when(lax.rem(chip, half) != 0)
    def _():
        out[...] = dot3(split(both[...]), split(across[...]), NN)


def finish(half, arrivals, *refs):
    refs = iter(refs)
    part, carry, map_ref, both = take(refs, 4)
    across = next(refs) if arrivals else None
    prior = next(refs)
    arrived = take(refs, arrivals)
    stay, leave, entering = take(refs, 3)
    _, core = chip_and_core()
    first = core == 0

    def put(value):
        entering[...] = value

    if arrivals:
        absorb(half, prior, across, arrived, put)
    else:
        put(prior[...])
    incoming = split(entering[...])
    solved_a = part[...] - dot3(incoming, split(map_ref[...]), NT)
    solved_b = carry[...] + dot3(incoming, split(both[...]), NT)
    stay[...] = jnp.where(first, solved_a, solved_b)
    leave[...] = jnp.where(first, solved_b, solved_a)


def shared(chips, *refs):
    refs = iter(refs)
    stays, leaves = take(refs, CHUNKS), take(refs, CHUNKS)
    own, other = take(refs, 2)
    outs, tails = take(refs, chips), take(refs, CHUNKS)
    chip, _ = chip_and_core()
    own, other = split(own[...]), split(other[...])
    for k in range(CHUNKS):
        tails[k][...] = dot3(split(stays[k][...]), own, NN) + dot3(split(leaves[k][...]), other, NN)
    for shift in range(chips):
        for k, (begin, end) in enumerate(cuts(outs[0].shape[0])):
            height = end - begin
            start = pl.multiple_of(destination(chip, shift, chips) * height, height)
            outs[shift][begin:end, :] = tails[k][pl.ds(start, height), :]


def destination(chip, shift, chips):
    return chip ^ shift if chips & (chips - 1) == 0 else (chip + shift) % chips


def stacked(count, *refs):
    *shards, out = refs
    height = shards[0].shape[0]
    for shift in range(count):
        out[shard_rows(count, shift, height), :] = shards[shift][...]


def interleave(*refs):
    *sources, out, token, sems = refs
    _, core = chip_and_core()
    copies = []
    for at, source in enumerate(sources):
        begin, end = cuts(out.shape[2])[at % CHUNKS]
        height = end - begin
        for chip in range(out.shape[0]):
            target = out.at[chip, core if at < CHUNKS else 1 - core, pl.ds(begin, height)]
            copies.append(pltpu.make_async_copy(source.at[pl.ds(chip * height, height)], target, sems.at[at, chip]))
    for copy in copies:
        copy.start()
    token[...] = jnp.zeros_like(token)
    for copy in copies:
        copy.wait()


def subtract(cols, *refs):
    *shares, out = refs
    total = shares[0][...]
    for share in shares[1:]:
        total = total + share[...]
    out[...] = cols[...] - total


def between_chips(value, pairs):
    pairs = [(2 * a + core, 2 * b + core) for a, b in pairs for core in (0, 1)]
    return lax.ppermute(value, "panel", pairs)


def to_other_core(value):
    return lax.ppermute(value, "panel", [(q, q ^ 1) for q in range(lax.axis_size("panel"))])


def gather_rows(value, order):
    count = lax.axis_size("row")
    moved = [lax.ppermute(value, "row", [(j, (j + s) % count) for j in range(count)]) for s in order if s]
    return [value, *moved]


def on_device(slab, boundary, diag_inverse, sub_block, tail_coupling, tail_cols):
    panels, count = lax.axis_size("panel"), lax.axis_size("row")
    chips = panels // 2
    chip, core = chip_and_core()
    rows, width = slab.shape
    piece = rows // panels
    held = chips * piece

    def blocks(array):
        return array.reshape(chips, 2, piece, width)

    own = gather_rows(jnp.concatenate([diag_inverse, sub_block]), weight_shifts(count))
    across_slab = to_other_core(slab)
    other = [to_other_core(shard) for shard in own]
    square = (width, width)
    part = (held, width)
    slices = [(chips * (end - begin), width) for begin, end in cuts(piece)]
    three = (chips, piece, width)
    kept, entering, coupling = call(
        fetch,
        [three, three, tail_coupling.shape],
        [blocks(slab), blocks(boundary), tail_coupling],
        [pltpu.SemaphoreType.DMA((3,))],
        hbm=3,
    )
    map_a, both, coupling, *made = call(
        functools.partial(prepare, count),
        [square, square, tail_coupling.shape] + slices * 2,
        [*own, *other, blocks(across_slab), kept, entering, coupling],
        [pltpu.VMEM((2, *square), jnp.float32)] * 2 + [pltpu.VMEM(part, jnp.float32)],
        width * width * (3 * width + 4 * held),
    )
    parts, carries = made[:CHUNKS], made[CHUNKS:]

    def spread(after):
        shards = gather_rows(coupling, range(count))
        return call(functools.partial(stacked, count), [square], shards, after=after)[0]

    def send_map(value, groups):
        return sum(between_chips(value, group) for group in groups if group)

    own_coupling = None
    priors, across = None, None
    half = 1
    while True:
        last = 2 * half >= chips
        sources = [s for s in range(half - 1, chips - 1, 2 * half)]
        pairs = [[(s, s + 1 + j) for s in sources if s + 1 + j < chips] for j in range(half)]
        maps = [[(s, t) for s, t in group if s >= half] for group in pairs]
        arrived, done = [], []
        for k in range(CHUNKS):
            value = carries[k]
            if priors is not None:
                if k == CHUNKS - 1 and half == 2:
                    own_coupling = spread(done)
                    done = [*done, own_coupling]
                (value,) = call(inclusive, [slices[k]], [value, priors[k], both], (), width * value.size, after=done)
                done = [value]
            arrived.append([between_chips(value, group) for group in reversed(pairs)])
        if last and priors is not None:
            break
        if priors is None:
            priors = [a[0] for a in arrived]
            if any(maps):
                across = send_map(both, maps)
        else:
            (send,) = call(functools.partial(joined, half), [square], [both, across], (), width**3)
            step_map = send_map(send, maps)
            priors = [
                call(
                    functools.partial(advance, half),
                    [slices[k]],
                    [priors[k], across, *arrived[k]],
                    (),
                    width * priors[k].size,
                )[0]
                for k in range(CHUNKS)
            ]
            (across,) = call(functools.partial(extend, half), [square], [across, step_map], (), width**3)
        if last:
            arrived = [[] for _ in range(CHUNKS)]
            break
        half *= 2

    if own_coupling is None:
        own_coupling = spread([])
    other_coupling = to_other_core(own_coupling)
    arrivals = len(arrived[0])
    stays, leaves = [], []
    for k in range(CHUNKS):
        stay, leave = call(
            functools.partial(finish, half, arrivals),
            [slices[k]] * 2,
            [parts[k], carries[k], map_a, both] + ([across] if arrivals else []) + [priors[k], *arrived[k]],
            [pltpu.VMEM(slices[k], jnp.float32)],
            3 * width * parts[k].size,
            after=stays[-1:],
        )
        stays.append(stay)
        leaves.append(leave)
    shares = call(
        functools.partial(shared, chips),
        [(piece, width)] * chips,
        [*stays, *leaves, own_coupling, other_coupling],
        [pltpu.VMEM(shape, jnp.float32) for shape in slices],
        2 * width * width * held,
    )
    shares = list(shares)
    for k in reversed(range(1, chips)):
        shares[k] = between_chips(shares[k], [(a, destination(a, k, chips)) for a in range(chips)])
    came = [to_other_core(leave) for leave in leaves]
    factor, token = pl.pallas_call(
        interleave,
        out_shape=[
            jax.ShapeDtypeStruct((chips, 2, piece, width), jnp.float32),
            jax.ShapeDtypeStruct((8, 128), jnp.float32),
        ],
        in_specs=[VMEM] * (2 * CHUNKS),
        out_specs=[HBM, VMEM],
        scratch_shapes=[pltpu.SemaphoreType.DMA((2 * CHUNKS, chips))],
        compiler_params=pltpu.CompilerParams(vmem_limit_bytes=4 << 20),
        cost_estimate=pl.CostEstimate(flops=0, bytes_accessed=16 * held * width, transcendentals=0),
    )(*stays, *came)
    (tail_out,) = call(subtract, [tail_cols.shape], [tail_cols, *shares], after=[token])
    return factor.reshape(rows, width), tail_out


def solution(mesh):
    placed = (
        P("row", "panel"),
        P("row", None),
        P(("panel", "row"), None),
        P(("panel", "row"), None),
        P(("panel", "row"), None),
        P(("row", "panel"), None),
    )
    return jax.shard_map(
        on_device,
        mesh=mesh,
        in_specs=placed,
        out_specs=(P("row", "panel"), P(("row", "panel"), None)),
        check_vma=False,
    )
```

time: 63.2 us -> 60.9 us (0.964)
  waiting for transfers between devices: 22.7 us -> 16.6 us
  starting transfers between devices: 31.8 us -> 35.1 us
    ppermute x6, waiting for transfers between devices: 15 us -> 11.1 us  [gather_rows(): lax.ppermute(value, 'row', [(j, (j + s) % count) for j in range(count)])]
    ppermute x6, starting transfers between devices: 9.55 us -> 12.9 us  [gather_rows(): lax.ppermute(value, 'row', [(j, (j + s) % count) for j in range(count)])]
    ppermute x8, waiting for transfers between devices: 1.31 us -> 0.1 us  [to_other_core(): lax.ppermute(value, 'panel', [(q, q ^ 1) for q in range(lax.axis_size('pa...]
    ppermute x10, waiting for transfers between devices: 6.33 us -> 5.33 us  [between_chips(): return lax.ppermute(value, 'panel', pairs)]
    pallas_call x8 -> x9, Pallas kernels: 5.64 us -> 6.06 us  [call(): pl.pallas_call(body, out_shape=[jax.ShapeDtypeStruct(o, jnp.float32) for...]
  transfers between devices with their start and end apart: 24 -> 24, of which waited for: 9 -> 8; matrix products, arithmetic and copies ran while one was open for 1% -> 1% of each run, Pallas kernels for 5% -> 7%
where the time goes in v4:
time: 60.9 us; the launch traced here: 60.6 us
  starting transfers between devices  35.1 us (58%)
  waiting for transfers between devices  16.6 us (27%)
  Pallas kernels  7.16 us (12%)
  between operations  0.89 us (1%)
  local copies, waits for them, and re-layouts  0.86 us (1%)
    ppermute x10, starting transfers between devices, between_chips(): return lax.ppermute(value, 'panel', pairs)  20.6 us
    ppermute x6, starting transfers between devices, gather_rows(): lax.ppermute(value, 'row', [(j, (j + s) % count) for j in range(count)])  12.9 us
    ppermute x6, waiting for transfers between devices, gather_rows(): lax.ppermute(value, 'row', [(j, (j + s) % count) for j in range(count)])  11.1 us
    pallas_call x9, Pallas kernels, call(): pl.pallas_call(body, out_shape=[jax.ShapeDtypeStruct(o, jnp.float32) for...  6.06 us
    ppermute x10, waiting for transfers between devices, between_chips(): return lax.ppermute(value, 'panel', pairs)  5.33 us
    ppermute x8, starting transfers between devices, to_other_core(): lax.ppermute(value, 'panel', [(q, q ^ 1) for q in range(lax.axis_size('pa...  1.66 us
  transfers between devices with their start and end apart: 24, of which 8 were waited for; matrix products, arithmetic and copies ran while one was open for 1% of the time, Pallas kernels for 7%

profile of v4, /device:TPU:0, one launch (start us, length us, event | category | flops | bytes accessed | tf_op | source)
XLA Modules:
  0.0 60.6 jit_solution(14725657739327136364)
XLA Ops:
  0.6 0.0 copy-start.1
  0.6 0.5 collective-permute-start.7
  1.2 0.8 %constant_dynamic-update-slice_fusion.1 = f32[128,256]{1,0:T(8,128)S(1)} fusion(f32[64,256]{1,0:T(8,128)} %param.8), kind=kLoop, calls=%fused_computation.1 | loop fusion | bytes 131072
  2.0 0.0 copy-done.1
  2.0 3.7 %collective-permute-start.2 = (f32[128,256]{1,0:T(8,128)S(1)}, f32[128,256]{1,0:T(8,128)S(1)}, u32[]{:S(2)}, u32[]{:S(2)}) collective-permute-start(f32[128,256]{1,0:T(8,128)S(1)} %constant_dynamic-update-slice_fusion.refs_0_), channel_id=1, source_target_pairs={{0,2},{1,3},{2,0},{3,1},{4,6},{5,7},{6,4},{7,5},{8,10},{9,11},{10,... | collective-permute-start | bytes 393224 | tf_op jit(solution)/shard_map/ppermute | solution.py:277
  5.7 1.3 %collective-permute-start.1 = (f32[128,256]{1,0:T(8,128)S(1)}, f32[128,256]{1,0:T(8,128)S(1)}, u32[]{:S(2)}, u32[]{:S(2)}) collective-permute-start(f32[128,256]{1,0:T(8,128)S(1)} %constant_dynamic-update-slice_fusion.refs_0_), channel_id=1, source_target_pairs={{0,3},{1,0},{2,1},{3,2},{4,7},{5,4},{6,5},{7,6},{8,11},{9,8},{10,9... | collective-permute-start | bytes 393224 | tf_op jit(solution)/shard_map/ppermute | solution.py:277
  7.0 0.7 %collective-permute-start = (f32[128,256]{1,0:T(8,128)S(1)}, f32[128,256]{1,0:T(8,128)S(1)}, u32[]{:S(2)}, u32[]{:S(2)}) collective-permute-start(f32[128,256]{1,0:T(8,128)S(1)} %constant_dynamic-update-slice_fusion.refs_0_), channel_id=1, source_target_pairs={{0,1},{1,2},{2,3},{3,0},{4,5},{5,6},{6,7},{7,4},{8,9},{9,10},{10,1... | collective-permute-start | bytes 393224 | tf_op jit(solution)/shard_map/ppermute | solution.py:277
  7.7 0.0 collective-permute-start.3
  7.7 5.2 %collective-permute-done.2.refs_3_ = f32[128,256]{1,0:T(8,128)S(1)} collective-permute-done((f32[128,256]{1,0:T(8,128)S(1)}, f32[128,256]{1,0:T(8,128)S(1)}, u32[]{:S(2)}, u32[]{:S(2)}) %collective-permute-start.2) | collective-permute-done | bytes 131104 | tf_op jit(solution)/shard_map/ppermute | solution.py:277
  12.9 0.0 collective-permute-start.6
  12.9 0.1 collective-permute-done.1.refs_2_
  12.9 0.5 collective-permute-start.5
  13.4 3.3 %collective-permute-done.refs_1_ = f32[128,256]{1,0:T(8,128)S(1)} collective-permute-done((f32[128,256]{1,0:T(8,128)S(1)}, f32[128,256]{1,0:T(8,128)S(1)}, u32[]{:S(2)}, u32[]{:S(2)}) %collective-permute-start) | collective-permute-done | bytes 131104 | tf_op jit(solution)/shard_map/ppermute | solution.py:277
  16.7 0.0 collective-permute-start.4
  16.7 1.2 %shard_map.77 = (f32[4,128,256]{2,1,0:T(8,128)S(1)}, f32[4,128,256]{2,1,0:T(8,128)S(1)}, f32[64,256]{1,0:T(8,128)S(1)}) custom-call(f32[4,2,128,256]{3,2,1,0:T(8,128)} %bitcast.6, f32[4,2,128,256]{3,2,1,0:T(8,128)} %bitcast.5, f32[64,256]{1,0:T(8,128)} %refs_2_.1), custom_call_target="tpu_custom_call" | custom-call | bytes 3276800 | tf_op jit(solution)/shard_map/pallas_call | solution.py:43
  17.9 0.0 collective-permute-done.3.refs_4_
  17.9 0.0 collective-permute-done.6.refs_7_
  17.9 0.0 collective-permute-done.5.refs_6_
  17.9 0.1 collective-permute-done.4.refs_5_
  18.0 0.0 collective-permute-done.7
  18.0 1.9 %shard_map.78 = (f32[256,256]{1,0:T(8,128)S(1)}, f32[256,256]{1,0:T(8,128)S(1)}, f32[64,256]{1,0:T(8,128)S(1)}, f32[256,256]{1,0:T(8,128)S(1)}, f32[256,256]{1,0...) custom-call(f32[128,256]{1,0:T(8,128)S(1)} %constant_dynamic-update-slice_fusion.refs_0_, ...), custom_call_target="tpu_custom_call" | custom-call | flops 1107296256 | bytes 4849664 | tf_op jit(solution)/shard_map/pallas_call | solution.py:43
  20.0 3.0 %collective-permute-start.9 = (f32[256,256]{1,0:T(8,128)S(1)}, f32[256,256]{1,0:T(8,128)S(1)}, u32[]{:S(2)}, u32[]{:S(2)}) collective-permute-start(f32[256,256]{1,0:T(8,128)S(1)} %get-tuple-element.26.refs_0_.refs_1_), channel_id=1, source_target_pairs={{0,8},{4,12},{16,24},{20,28},{1,9},{5,13},{17,25},{21,29},{2,10},{... | collective-permute-start | bytes 786440 | tf_op jit(solution)/shard_map/ppermute | solution.py:268
  23.0 1.3 %collective-permute-start.12 = (f32[256,256]{1,0:T(8,128)S(1)}, f32[256,256]{1,0:T(8,128)S(1)}, u32[]{:S(2)}, u32[]{:S(2)}) collective-permute-start(f32[256,256]{1,0:T(8,128)S(1)} %get-tuple-element.31.refs_0_.refs_1_), channel_id=1, source_target_pairs={{0,8},{4,12},{16,24},{20,28},{1,9},{5,13},{17,25},{21,29},{2,10},{... | collective-permute-start | bytes 786440 | tf_op jit(solution)/shard_map/ppermute | solution.py:268
  24.3 0.7 %collective-permute-start.8 = (f32[256,256]{1,0:T(8,128)S(1)}, f32[256,256]{1,0:T(8,128)S(1)}, u32[]{:S(2)}, u32[]{:S(2)}) collective-permute-start(f32[256,256]{1,0:T(8,128)S(1)} %get-tuple-element.28.refs_2_.refs_3_), channel_id=1, source_target_pairs={{16,24},{20,28},{17,25},{21,29},{18,26},{22,30},{19,27},{23,31}} | collective-permute-start | bytes 786440 | tf_op jit(solution)/shard_map/ppermute | solution.py:268
  25.0 3.0 %collective-permute-start.15 = (f32[64,256]{1,0:T(8,128)S(1)}, f32[64,256]{1,0:T(8,128)S(1)}, u32[]{:S(2)}, u32[]{:S(2)}) collective-permute-start(f32[64,256]{1,0:T(8,128)S(1)} %get-tuple-element.32.refs_0_), channel_id=1, source_target_pairs={{0,3},{1,0},{2,1},{3,2},{4,7},{5,4},{6,5},{7,6},{8,11},{9,8},{10,9... | collective-permute-start | bytes 196616 | tf_op jit(solution)/shard_map/ppermute | solution.py:277
  28.0 1.4 %collective-permute-start.14 = (f32[64,256]{1,0:T(8,128)S(1)}, f32[64,256]{1,0:T(8,128)S(1)}, u32[]{:S(2)}, u32[]{:S(2)}) collective-permute-start(f32[64,256]{1,0:T(8,128)S(1)} %get-tuple-element.32.refs_0_), channel_id=1, source_target_pairs={{0,2},{1,3},{2,0},{3,1},{4,6},{5,7},{6,4},{7,5},{8,10},{9,11},{10,... | collective-permute-start | bytes 196616 | tf_op jit(solution)/shard_map/ppermute | solution.py:277
  29.4 0.2 collective-permute-done.9.refs_1_.refs_5_
  29.6 2.7 %collective-permute-start.13 = (f32[64,256]{1,0:T(8,128)S(1)}, f32[64,256]{1,0:T(8,128)S(1)}, u32[]{:S(2)}, u32[]{:S(2)}) collective-permute-start(f32[64,256]{1,0:T(8,128)S(1)} %get-tuple-element.32.refs_0_), channel_id=1, source_target_pairs={{0,1},{1,2},{2,3},{3,0},{4,5},{5,6},{6,7},{7,4},{8,9},{9,10},{10,1... | collective-permute-start | bytes 196616 | tf_op jit(solution)/shard_map/ppermute | solution.py:277
  32.3 0.3 shard_map.79.refs_4_.refs_3_
  32.6 0.0 collective-permute-done.15.refs_3_
  32.6 0.7 %collective-permute-start.11 = (f32[256,256]{1,0:T(8,128)S(1)}, f32[256,256]{1,0:T(8,128)S(1)}, u32[]{:S(2)}, u32[]{:S(2)}) collective-permute-start(f32[256,256]{1,0:T(8,128)S(1)} %shard_map.79.refs_4_.refs_3_), channel_id=1, source_target_pairs={{8,16},{12,20},{9,17},{13,21},{10,18},{14,22},{11,19},{15,23}} | collective-permute-start | bytes 786440 | tf_op jit(solution)/shard_map/ppermute | solution.py:268
  33.3 2.6 %collective-permute-done.14.refs_2_ = f32[64,256]{1,0:T(8,128)S(1)} collective-permute-done((f32[64,256]{1,0:T(8,128)S(1)}, f32[64,256]{1,0:T(8,128)S(1)}, u32[]{:S(2)}, u32[]{:S(2)}) %collective-permute-start.14) | collective-permute-done | bytes 65568 | tf_op jit(solution)/shard_map/ppermute | solution.py:277
  36.0 0.7 %collective-permute-start.10 = (f32[256,256]{1,0:T(8,128)S(1)}, f32[256,256]{1,0:T(8,128)S(1)}, u32[]{:S(2)}, u32[]{:S(2)}) collective-permute-start(f32[256,256]{1,0:T(8,128)S(1)} %shard_map.79.refs_4_.refs_3_), channel_id=1, source_target_pairs={{8,24},{12,28},{9,25},{13,29},{10,26},{14,30},{11,27},{15,31}} | collective-permute-start | bytes 786440 | tf_op jit(solution)/shard_map/ppermute | solution.py:268
  36.6 0.0 collective-permute-done.13.refs_1_
  36.7 0.0 collective-permute-done.12.refs_1_.refs_5_
  36.7 0.3 shard_map.82
  37.0 0.7 %collective-permute-start.17 = (f32[256,256]{1,0:T(8,128)S(1)}, f32[256,256]{1,0:T(8,128)S(1)}, u32[]{:S(2)}, u32[]{:S(2)}) collective-permute-start(f32[256,256]{1,0:T(8,128)S(1)} %shard_map.82), channel_id=1, source_target_pairs={{8,16},{12,20},{9,17},{13,21},{10,18},{14,22},{11,19},{15,23}} | collective-permute-start | bytes 786440 | tf_op jit(solution)/shard_map/ppermute | solution.py:268
  37.7 0.7 %collective-permute-start.16 = (f32[256,256]{1,0:T(8,128)S(1)}, f32[256,256]{1,0:T(8,128)S(1)}, u32[]{:S(2)}, u32[]{:S(2)}) collective-permute-start(f32[256,256]{1,0:T(8,128)S(1)} %shard_map.82), channel_id=1, source_target_pairs={{8,24},{12,28},{9,25},{13,29},{10,26},{14,30},{11,27},{15,31}} | collective-permute-start | bytes 786440 | tf_op jit(solution)/shard_map/ppermute | solution.py:268
  38.4 0.0 collective-permute-done.8.refs_4_
  38.4 0.1 collective-permute-start.20
  38.5 0.0 collective-permute-done.11.refs_7_
  38.5 0.0 collective-permute-done.10.refs_6_
  38.5 0.5 shard_map.80
  39.0 0.0 collective-permute-done.17.refs_7_
  39.0 0.0 collective-permute-done.16.refs_6_
  39.0 0.5 shard_map.83
  39.5 0.5 collective-permute-start.19
  40.0 0.1 collective-permute-start.18
  40.1 0.0 collective-permute-done.20.refs_5_
  40.1 0.6 %shard_map.85 = (f32[128,256]{1,0:T(8,128)S(1)}, f32[128,256]{1,0:T(8,128)S(1)}, f32[128,256]{1,0:T(8,128)S(1)}, f32[128,256]{1,0:T(8,128)S(1)}) custom-call(f32[256,256]{1,0:T(8,128)S(1)} %get-tuple-element.29.refs_8_.refs_0_, f32[256,256]{1,0:T(8,128)S(1)} %get-tuple-element.33.refs_1_, f32[256,256]{1,0:T(8,128)S(1)} %get-tuple-element.34.refs_2_, ...), custom_call_target="tpu_custom_call" | custom-call | flops 402653184 | bytes 2097152 | tf_op jit(solution)/shard_map/pallas_call | solution.py:43
  40.7 10.5 %collective-permute-start.21 = (f32[128,256]{1,0:T(8,128)S(1)}, f32[128,256]{1,0:T(8,128)S(1)}, u32[]{:S(2)}, u32[]{:S(2)}) collective-permute-start(f32[128,256]{1,0:T(8,128)S(1)} %get-tuple-element.38), channel_id=1, source_target_pairs={{0,8},{4,12},{8,0},{12,4},{16,24},{20,28},{24,16},{28,20},{1,9},{5... | collective-permute-start | bytes 393224 | tf_op jit(solution)/shard_map/ppermute | solution.py:268
  51.2 2.5 %collective-permute-start.22 = (f32[128,256]{1,0:T(8,128)S(1)}, f32[128,256]{1,0:T(8,128)S(1)}, u32[]{:S(2)}, u32[]{:S(2)}) collective-permute-start(f32[128,256]{1,0:T(8,128)S(1)} %get-tuple-element.39), channel_id=1, source_target_pairs={{0,16},{4,20},{8,24},{12,28},{16,0},{20,4},{24,8},{28,12},{1,17},{... | collective-permute-start | bytes 393224 | tf_op jit(solution)/shard_map/ppermute | solution.py:268
  53.6 0.0 copy-start
  53.6 0.0 collective-permute-start.23
  53.6 0.0 collective-permute-done.19.refs_3_
  53.6 0.0 collective-permute-done.18.refs_2_
  53.7 1.1 %shard_map.84 = (f32[4,2,128,256]{3,2,1,0:T(8,128)}, f32[8,128]{1,0:T(8,128)S(1)}) custom-call(f32[256,256]{1,0:T(8,128)S(1)} %get-tuple-element.29.refs_8_.refs_0_, f32[256,256]{1,0:T(8,128)S(1)} %get-tuple-element.33.refs_1_, f32[256,256]{1,0:T(8,128)S(1)} %collective-permute-done.18.refs_2_, f32[256,256]{1,0:T(8,128)S(1)} %collective-permute-done.19.refs_3_), custom_call_target="tpu_custom_call" | custom-call | bytes 2097152 | tf_op jit(solution)/shard_map/pallas_call | solution.py:392
  54.8 0.1 collective-permute-done.21.refs_2_
  54.9 5.0 %collective-permute-done.22.refs_3_ = f32[128,256]{1,0:T(8,128)S(1)} collective-permute-done((f32[128,256]{1,0:T(8,128)S(1)}, f32[128,256]{1,0:T(8,128)S(1)}, u32[]{:S(2)}, u32[]{:S(2)}) %collective-permute-start.22) | collective-permute-done | bytes 131104 | tf_op jit(solution)/shard_map/ppermute | solution.py:268
  59.9 0.0 collective-permute-done.23.refs_4_
  59.9 0.0 copy-done
  59.9 0.7 %shard_map.86 = f32[128,256]{1,0:T(8,128)} custom-call(f32[128,256]{1,0:T(8,128)S(1)} %copy-done, f32[128,256]{1,0:T(8,128)S(1)} %get-tuple-element.37.refs_1_, f32[128,256]{1,0:T(8,128)S(1)} %collective-permute-done.21.refs_2_, f32[128,256]{1,0:T(8,128)S(1)} %collective-permute-done.22.refs_3_, f32[128,256]{1,0:T(8,128)S(1)} %collective-permute-done.23.refs_4_, ...), custom_call_target="tpu_custom_call" | custom-call | bytes 786432 | tf_op jit(solution)/shard_map/pallas_call | solution.py:43
  (2 shorter events, 0.0 us)
Async XLA Ops:
  0.6 1.4 %copy-start.1 = (f32[64,256]{1,0:T(8,128)S(1)}, f32[64,256]{1,0:T(8,128)}, u32[]{:S(2)}) copy-start(f32[64,256]{1,0:T(8,128)} %param.9) | copy-start | bytes 196612
  0.6 17.4 %collective-permute-start.7 = (f32[1024,256]{1,0:T(8,128)}, f32[1024,256]{1,0:T(8,128)S(1)}, u32[]{:S(2)}, u32[]{:S(2)}) collective-permute-start(f32[1024,256]{1,0:T(8,128)} %param.6), channel_id=1, source_target_pairs={{0,4},{4,0},{8,12},{12,8},{16,20},{20,16},{24,28},{28,24},{1,5},{5... | collective-permute-start | bytes 3145736 | tf_op jit(solution)/shard_map/ppermute | solution.py:272
  2.0 10.9 %collective-permute-start.2 = (f32[128,256]{1,0:T(8,128)S(1)}, f32[128,256]{1,0:T(8,128)S(1)}, u32[]{:S(2)}, u32[]{:S(2)}) collective-permute-start(f32[128,256]{1,0:T(8,128)S(1)} %constant_dynamic-update-slice_fusion.refs_0_), channel_id=1, source_target_pairs={{0,2},{1,3},{2,0},{3,1},{4,6},{5,7},{6,4},{7,5},{8,10},{9,11},{10,... | collective-permute-start | bytes 393224 | tf_op jit(solution)/shard_map/ppermute | solution.py:277
  5.7 7.3 %collective-permute-start.1 = (f32[128,256]{1,0:T(8,128)S(1)}, f32[128,256]{1,0:T(8,128)S(1)}, u32[]{:S(2)}, u32[]{:S(2)}) collective-permute-start(f32[128,256]{1,0:T(8,128)S(1)} %constant_dynamic-update-slice_fusion.refs_0_), channel_id=1, source_target_pairs={{0,3},{1,0},{2,1},{3,2},{4,7},{5,4},{6,5},{7,6},{8,11},{9,8},{10,9... | collective-permute-start | bytes 393224 | tf_op jit(solution)/shard_map/ppermute | solution.py:277
  7.0 9.6 %collective-permute-start = (f32[128,256]{1,0:T(8,128)S(1)}, f32[128,256]{1,0:T(8,128)S(1)}, u32[]{:S(2)}, u32[]{:S(2)}) collective-permute-start(f32[128,256]{1,0:T(8,128)S(1)} %constant_dynamic-update-slice_fusion.refs_0_), channel_id=1, source_target_pairs={{0,1},{1,2},{2,3},{3,0},{4,5},{5,6},{6,7},{7,4},{8,9},{9,10},{10,1... | collective-permute-start | bytes 393224 | tf_op jit(solution)/shard_map/ppermute | solution.py:277
  7.7 10.2 %collective-permute-start.3 = (f32[128,256]{1,0:T(8,128)S(1)}, f32[128,256]{1,0:T(8,128)S(1)}, u32[]{:S(2)}, u32[]{:S(2)}) collective-permute-start(f32[128,256]{1,0:T(8,128)S(1)} %constant_dynamic-update-slice_fusion.refs_0_), channel_id=1, source_target_pairs={{0,4},{4,0},{8,12},{12,8},{16,20},{20,16},{24,28},{28,24},{1,5},{5... | collective-permute-start | bytes 393224 | tf_op jit(solution)/shard_map/ppermute | solution.py:272
  12.9 5.0 %collective-permute-start.6 = (f32[128,256]{1,0:T(8,128)S(1)}, f32[128,256]{1,0:T(8,128)S(1)}, u32[]{:S(2)}, u32[]{:S(2)}) collective-permute-start(f32[128,256]{1,0:T(8,128)S(1)} %collective-permute-done.2.refs_3_), channel_id=1, source_target_pairs={{0,4},{4,0},{8,12},{12,8},{16,20},{20,16},{24,28},{28,24},{1,5},{5... | collective-permute-start | bytes 393224 | tf_op jit(solution)/shard_map/ppermute | solution.py:272
  12.9 5.0 %collective-permute-start.5 = (f32[128,256]{1,0:T(8,128)S(1)}, f32[128,256]{1,0:T(8,128)S(1)}, u32[]{:S(2)}, u32[]{:S(2)}) collective-permute-start(f32[128,256]{1,0:T(8,128)S(1)} %collective-permute-done.1.refs_2_), channel_id=1, source_target_pairs={{0,4},{4,0},{8,12},{12,8},{16,20},{20,16},{24,28},{28,24},{1,5},{5... | collective-permute-start | bytes 393224 | tf_op jit(solution)/shard_map/ppermute | solution.py:272
  16.7 1.3 %collective-permute-start.4 = (f32[128,256]{1,0:T(8,128)S(1)}, f32[128,256]{1,0:T(8,128)S(1)}, u32[]{:S(2)}, u32[]{:S(2)}) collective-permute-start(f32[128,256]{1,0:T(8,128)S(1)} %collective-permute-done.refs_1_), channel_id=1, source_target_pairs={{0,4},{4,0},{8,12},{12,8},{16,20},{20,16},{24,28},{28,24},{1,5},{5... | collective-permute-start | bytes 393224 | tf_op jit(solution)/shard_map/ppermute | solution.py:272
  20.0 9.6 %collective-permute-start.9 = (f32[256,256]{1,0:T(8,128)S(1)}, f32[256,256]{1,0:T(8,128)S(1)}, u32[]{:S(2)}, u32[]{:S(2)}) collective-permute-start(f32[256,256]{1,0:T(8,128)S(1)} %get-tuple-element.26.refs_0_.refs_1_), channel_id=1, source_target_pairs={{0,8},{4,12},{16,24},{20,28},{1,9},{5,13},{17,25},{21,29},{2,10},{... | collective-permute-start | bytes 786440 | tf_op jit(solution)/shard_map/ppermute | solution.py:268
  23.0 13.7 %collective-permute-start.12 = (f32[256,256]{1,0:T(8,128)S(1)}, f32[256,256]{1,0:T(8,128)S(1)}, u32[]{:S(2)}, u32[]{:S(2)}) collective-permute-start(f32[256,256]{1,0:T(8,128)S(1)} %get-tuple-element.31.refs_0_.refs_1_), channel_id=1, source_target_pairs={{0,8},{4,12},{16,24},{20,28},{1,9},{5,13},{17,25},{21,29},{2,10},{... | collective-permute-start | bytes 786440 | tf_op jit(solution)/shard_map/ppermute | solution.py:268
  24.3 14.1 %collective-permute-start.8 = (f32[256,256]{1,0:T(8,128)S(1)}, f32[256,256]{1,0:T(8,128)S(1)}, u32[]{:S(2)}, u32[]{:S(2)}) collective-permute-start(f32[256,256]{1,0:T(8,128)S(1)} %get-tuple-element.28.refs_2_.refs_3_), channel_id=1, source_target_pairs={{16,24},{20,28},{17,25},{21,29},{18,26},{22,30},{19,27},{23,31}} | collective-permute-start | bytes 786440 | tf_op jit(solution)/shard_map/ppermute | solution.py:268
  25.0 7.6 %collective-permute-start.15 = (f32[64,256]{1,0:T(8,128)S(1)}, f32[64,256]{1,0:T(8,128)S(1)}, u32[]{:S(2)}, u32[]{:S(2)}) collective-permute-start(f32[64,256]{1,0:T(8,128)S(1)} %get-tuple-element.32.refs_0_), channel_id=1, source_target_pairs={{0,3},{1,0},{2,1},{3,2},{4,7},{5,4},{6,5},{7,6},{8,11},{9,8},{10,9... | collective-permute-start | bytes 196616 | tf_op jit(solution)/shard_map/ppermute | solution.py:277
  28.0 8.0 %collective-permute-start.14 = (f32[64,256]{1,0:T(8,128)S(1)}, f32[64,256]{1,0:T(8,128)S(1)}, u32[]{:S(2)}, u32[]{:S(2)}) collective-permute-start(f32[64,256]{1,0:T(8,128)S(1)} %get-tuple-element.32.refs_0_), channel_id=1, source_target_pairs={{0,2},{1,3},{2,0},{3,1},{4,6},{5,7},{6,4},{7,5},{8,10},{9,11},{10,... | collective-permute-start | bytes 196616 | tf_op jit(solution)/shard_map/ppermute | solution.py:277
  29.6 7.1 %collective-permute-start.13 = (f32[64,256]{1,0:T(8,128)S(1)}, f32[64,256]{1,0:T(8,128)S(1)}, u32[]{:S(2)}, u32[]{:S(2)}) collective-permute-start(f32[64,256]{1,0:T(8,128)S(1)} %get-tuple-element.32.refs_0_), channel_id=1, source_target_pairs={{0,1},{1,2},{2,3},{3,0},{4,5},{5,6},{6,7},{7,4},{8,9},{9,10},{10,1... | collective-permute-start | bytes 196616 | tf_op jit(solution)/shard_map/ppermute | solution.py:277
  32.6 5.8 %collective-permute-start.11 = (f32[256,256]{1,0:T(8,128)S(1)}, f32[256,256]{1,0:T(8,128)S(1)}, u32[]{:S(2)}, u32[]{:S(2)}) collective-permute-start(f32[256,256]{1,0:T(8,128)S(1)} %shard_map.79.refs_4_.refs_3_), channel_id=1, source_target_pairs={{8,16},{12,20},{9,17},{13,21},{10,18},{14,22},{11,19},{15,23}} | collective-permute-start | bytes 786440 | tf_op jit(solution)/shard_map/ppermute | solution.py:268
  36.0 2.5 %collective-permute-start.10 = (f32[256,256]{1,0:T(8,128)S(1)}, f32[256,256]{1,0:T(8,128)S(1)}, u32[]{:S(2)}, u32[]{:S(2)}) collective-permute-start(f32[256,256]{1,0:T(8,128)S(1)} %shard_map.79.refs_4_.refs_3_), channel_id=1, source_target_pairs={{8,24},{12,28},{9,25},{13,29},{10,26},{14,30},{11,27},{15,31}} | collective-permute-start | bytes 786440 | tf_op jit(solution)/shard_map/ppermute | solution.py:268
  37.0 2.0 %collective-permute-start.17 = (f32[256,256]{1,0:T(8,128)S(1)}, f32[256,256]{1,0:T(8,128)S(1)}, u32[]{:S(2)}, u32[]{:S(2)}) collective-permute-start(f32[256,256]{1,0:T(8,128)S(1)} %shard_map.82), channel_id=1, source_target_pairs={{8,16},{12,20},{9,17},{13,21},{10,18},{14,22},{11,19},{15,23}} | collective-permute-start | bytes 786440 | tf_op jit(solution)/shard_map/ppermute | solution.py:268
  37.7 1.3 %collective-permute-start.16 = (f32[256,256]{1,0:T(8,128)S(1)}, f32[256,256]{1,0:T(8,128)S(1)}, u32[]{:S(2)}, u32[]{:S(2)}) collective-permute-start(f32[256,256]{1,0:T(8,128)S(1)} %shard_map.82), channel_id=1, source_target_pairs={{8,24},{12,28},{9,25},{13,29},{10,26},{14,30},{11,27},{15,31}} | collective-permute-start | bytes 786440 | tf_op jit(solution)/shard_map/ppermute | solution.py:268
  38.4 1.7 %collective-permute-start.20 = (f32[256,256]{1,0:T(8,128)S(1)}, f32[256,256]{1,0:T(8,128)S(1)}, u32[]{:S(2)}, u32[]{:S(2)}) collective-permute-start(f32[256,256]{1,0:T(8,128)S(1)} %shard_map.81.refs_4_), channel_id=1, source_target_pairs={{0,4},{4,0},{8,12},{12,8},{16,20},{20,16},{24,28},{28,24},{1,5},{5... | collective-permute-start | bytes 786440 | tf_op jit(solution)/shard_map/ppermute | solution.py:272
  39.5 14.2 %collective-permute-start.19 = (f32[256,256]{1,0:T(8,128)S(1)}, f32[256,256]{1,0:T(8,128)S(1)}, u32[]{:S(2)}, u32[]{:S(2)}) collective-permute-start(f32[256,256]{1,0:T(8,128)S(1)} %get-tuple-element.35.refs_3_), channel_id=1, source_target_pairs={{0,4},{4,0},{8,12},{12,8},{16,20},{20,16},{24,28},{28,24},{1,5},{5... | collective-permute-start | bytes 786440 | tf_op jit(solution)/shard_map/ppermute | solution.py:272
  40.0 13.7 %collective-permute-start.18 = (f32[256,256]{1,0:T(8,128)S(1)}, f32[256,256]{1,0:T(8,128)S(1)}, u32[]{:S(2)}, u32[]{:S(2)}) collective-permute-start(f32[256,256]{1,0:T(8,128)S(1)} %get-tuple-element.34.refs_2_), channel_id=1, source_target_pairs={{0,4},{4,0},{8,12},{12,8},{16,20},{20,16},{24,28},{28,24},{1,5},{5... | collective-permute-start | bytes 786440 | tf_op jit(solution)/shard_map/ppermute | solution.py:272
  40.7 14.2 %collective-permute-start.21 = (f32[128,256]{1,0:T(8,128)S(1)}, f32[128,256]{1,0:T(8,128)S(1)}, u32[]{:S(2)}, u32[]{:S(2)}) collective-permute-start(f32[128,256]{1,0:T(8,128)S(1)} %get-tuple-element.38), channel_id=1, source_target_pairs={{0,8},{4,12},{8,0},{12,4},{16,24},{20,28},{24,16},{28,20},{1,9},{5... | collective-permute-start | bytes 393224 | tf_op jit(solution)/shard_map/ppermute | solution.py:268
  51.2 8.8 %collective-permute-start.22 = (f32[128,256]{1,0:T(8,128)S(1)}, f32[128,256]{1,0:T(8,128)S(1)}, u32[]{:S(2)}, u32[]{:S(2)}) collective-permute-start(f32[128,256]{1,0:T(8,128)S(1)} %get-tuple-element.39), channel_id=1, source_target_pairs={{0,16},{4,20},{8,24},{12,28},{16,0},{20,4},{24,8},{28,12},{1,17},{... | collective-permute-start | bytes 393224 | tf_op jit(solution)/shard_map/ppermute | solution.py:268
  53.6 6.3 %copy-start = (f32[128,256]{1,0:T(8,128)S(1)}, f32[128,256]{1,0:T(8,128)}, u32[]{:S(2)}) copy-start(f32[128,256]{1,0:T(8,128)} %refs_0_.1) | copy-start | bytes 393220
  53.6 6.3 %collective-permute-start.23 = (f32[128,256]{1,0:T(8,128)S(1)}, f32[128,256]{1,0:T(8,128)S(1)}, u32[]{:S(2)}, u32[]{:S(2)}) collective-permute-start(f32[128,256]{1,0:T(8,128)S(1)} %get-tuple-element.40), channel_id=1, source_target_pairs={{0,24},{4,28},{8,16},{12,20},{16,8},{20,12},{24,0},{28,4},{1,25},{... | collective-permute-start | bytes 393224 | tf_op jit(solution)/shard_map/ppermute | solution.py:268

commit v5 on v4

--- a/solution.py
+++ b/solution.py
@@ -10,6 +10,8 @@
 
 CHUNKS = 2
 FIRST = 1 / 2
+SCAN_SPAN = 2_000_000_000
+FINISH_SPAN = 4_000_000_000
 NT = (((1,), (1,)), ((), ()))
 NN = (((1,), (0,)), ((), ()))
 VMEM = pl.BlockSpec(memory_space=pltpu.VMEM)
@@ -32,7 +34,7 @@
     return lax.div(panel, 2), lax.rem(panel, 2)
 
 
-def call(kernel, outs, args, scratch=(), products=0, hbm=0, after=()):
+def call(kernel, outs, args, scratch=(), span=0, hbm=0, after=()):
     size = sum(a.size * 4 for a in args) + sum(math.prod(o) * 4 for o in outs)
     inputs = len(args)
     args = [*args[: inputs - hbm], *(pltpu.with_memory_space_constraint(a, pltpu.HBM) for a in args[inputs - hbm :])]
@@ -47,12 +49,12 @@
         out_specs=[VMEM] * len(outs),
         scratch_shapes=list(scratch),
         compiler_params=pltpu.CompilerParams(vmem_limit_bytes=40 << 20),
-        cost_estimate=pl.CostEstimate(flops=6 * products, bytes_accessed=size, transcendentals=0),
+        cost_estimate=pl.CostEstimate(flops=2 * span, bytes_accessed=size, transcendentals=0),
     )(*args, *after)
 
 
 def weight_shifts(count):
-    return sorted(range(count), key=lambda s: (min(s, count - s), s))
+    return [0, *reversed(range(1, count))]
 
 
 def shard_rows(count, shift, height):
@@ -231,11 +233,24 @@
     return chip ^ shift if chips & (chips - 1) == 0 else (chip + shift) % chips
 
 
+def packed(*refs):
+    *sources, out = refs
+    at = 0
+    for source in sources:
+        out[at : at + source.shape[0], :] = source[...]
+        at += source.shape[0]
+
+
 def stacked(count, *refs):
-    *shards, out = refs
-    height = shards[0].shape[0]
-    for shift in range(count):
-        out[shard_rows(count, shift, height), :] = shards[shift][...]
+    *sources, out = refs
+    row = lax.axis_index("row")
+    height = out.shape[0] // count
+    at = 0
+    for source in sources:
+        for k in range(source.shape[0] // height):
+            start = pl.multiple_of((row ^ at) * height, height)
+            out[pl.ds(start, height), :] = source[k * height : (k + 1) * height, :]
+            at += 1
 
 
 def interleave(*refs):
@@ -308,13 +323,17 @@
         [square, square, tail_coupling.shape] + slices * 2,
         [*own, *other, blocks(across_slab), kept, entering, coupling],
         [pltpu.VMEM((2, *square), jnp.float32)] * 2 + [pltpu.VMEM(part, jnp.float32)],
-        width * width * (3 * width + 4 * held),
     )
     parts, carries = made[:CHUNKS], made[CHUNKS:]
 
     def spread(after):
-        shards = gather_rows(coupling, range(count))
-        return call(functools.partial(stacked, count), [square], shards, after=after)[0]
+        near, pieces = 1, [coupling]
+        while near < count:
+            if len(pieces) > 1:
+                pieces = call(packed, [(near * coupling.shape[0], width)], pieces)
+            pieces = [pieces[0], lax.ppermute(pieces[0], "row", [(j, j ^ near) for j in range(count)])]
+            near *= 2
+        return call(functools.partial(stacked, count), [square], pieces, after=after)[0]
 
     def send_map(value, groups):
         return sum(between_chips(value, group) for group in groups if group)
@@ -331,11 +350,10 @@
         for k in range(CHUNKS):
             value = carries[k]
             if priors is not None:
-                if k == CHUNKS - 1 and half == 2:
+                (value,) = call(inclusive, [slices[k]], [value, priors[k], both], span=SCAN_SPAN, after=done)
+                done = [value]
+                if k == 0 and half == 2:
                     own_coupling = spread(done)
-                    done = [*done, own_coupling]
-                (value,) = call(inclusive, [slices[k]], [value, priors[k], both], (), width * value.size, after=done)
-                done = [value]
             arrived.append([between_chips(value, group) for group in reversed(pairs)])
         if last and priors is not None:
             break
@@ -344,19 +362,17 @@
             if any(maps):
                 across = send_map(both, maps)
         else:
-            (send,) = call(functools.partial(joined, half), [square], [both, across], (), width**3)
+            (send,) = call(functools.partial(joined, half), [square], [both, across])
             step_map = send_map(send, maps)
             priors = [
                 call(
                     functools.partial(advance, half),
                     [slices[k]],
                     [priors[k], across, *arrived[k]],
-                    (),
-                    width * priors[k].size,
                 )[0]
                 for k in range(CHUNKS)
             ]
-            (across,) = call(functools.partial(extend, half), [square], [across, step_map], (), width**3)
+            (across,) = call(functools.partial(extend, half), [square], [across, step_map])
         if last:
             arrived = [[] for _ in range(CHUNKS)]
             break
@@ -373,7 +389,7 @@
             [slices[k]] * 2,
             [parts[k], carries[k], map_a, both] + ([across] if arrivals else []) + [priors[k], *arrived[k]],
             [pltpu.VMEM(slices[k], jnp.float32)],
-            3 * width * parts[k].size,
+            span=FINISH_SPAN,
             after=stays[-1:],
         )
         stays.append(stay)
@@ -383,7 +399,6 @@
         [(piece, width)] * chips,
         [*stays, *leaves, own_coupling, other_coupling],
         [pltpu.VMEM(shape, jnp.float32) for shape in slices],
-        2 * width * width * held,
     )
     shares = list(shares)
     for k in reversed(range(1, chips)):

time: 60.9 us -> 59.8 us (0.982)
  starting transfers between devices: 35.1 us -> 32.9 us
  waiting for transfers between devices: 16.6 us -> 17.7 us
    ppermute x6 -> x3, starting transfers between devices: 12.9 us -> 6.58 us  [gather_rows(): lax.ppermute(value, 'row', [(j, (j + s) % count) for j in range(count)])]
    ppermute x0 -> x2, starting transfers between devices: none -> 4.87 us  [spread(): lax.ppermute(pieces[0], 'row', [(j, j ^ near) for j in range(count)])]
    ppermute x6 -> x3, waiting for transfers between devices: 11.1 us -> 7.92 us  [gather_rows(): lax.ppermute(value, 'row', [(j, (j + s) % count) for j in range(count)])]
    ppermute x0 -> x2, waiting for transfers between devices: none -> 2.27 us  [spread(): lax.ppermute(pieces[0], 'row', [(j, j ^ near) for j in range(count)])]
    ppermute x10, waiting for transfers between devices: 5.33 us -> 7.52 us  [between_chips(): return lax.ppermute(value, 'panel', pairs)]
    ppermute x10, starting transfers between devices: 20.6 us -> 19.7 us  [between_chips(): return lax.ppermute(value, 'panel', pairs)]
    pallas_call x9 -> x10, Pallas kernels: 6.06 us -> 6.08 us  [call(): pl.pallas_call(body, out_shape=[jax.ShapeDtypeStruct(o, jnp.float32) for...]
  transfers between devices with their start and end apart: 24 -> 23, of which waited for: 8 -> 7; matrix products, arithmetic and copies ran while one was open for 1% -> 1% of each run, Pallas kernels for 7% -> 8%
where the time goes in v5:
time: 59.8 us; the launch traced here: 59.5 us
  starting transfers between devices  32.9 us (55%)
  waiting for transfers between devices  17.7 us (30%)
  Pallas kernels  7.18 us (12%)
  between operations  0.88 us (1%)
  local copies, waits for them, and re-layouts  0.86 us (1%)
    ppermute x10, starting transfers between devices, between_chips(): return lax.ppermute(value, 'panel', pairs)  19.7 us
    ppermute x3, waiting for transfers between devices, gather_rows(): lax.ppermute(value, 'row', [(j, (j + s) % count) for j in range(count)])  7.92 us
    ppermute x10, waiting for transfers between devices, between_chips(): return lax.ppermute(value, 'panel', pairs)  7.52 us
    ppermute x3, starting transfers between devices, gather_rows(): lax.ppermute(value, 'row', [(j, (j + s) % count) for j in range(count)])  6.58 us
    pallas_call x10, Pallas kernels, call(): pl.pallas_call(body, out_shape=[jax.ShapeDtypeStruct(o, jnp.float32) for...  6.08 us
    ppermute x2, starting transfers between devices, spread(): lax.ppermute(pieces[0], 'row', [(j, j ^ near) for j in range(count)])  4.87 us
    ppermute x2, waiting for transfers between devices, spread(): lax.ppermute(pieces[0], 'row', [(j, j ^ near) for j in range(count)])  2.27 us
    ppermute x8, starting transfers between devices, to_other_core(): lax.ppermute(value, 'panel', [(q, q ^ 1) for q in range(lax.axis_size('pa...  1.71 us
  transfers between devices with their start and end apart: 23, of which 7 were waited for; matrix products, arithmetic and copies ran while one was open for 1% of the time, Pallas kernels for 8%

profile of v5, /device:TPU:0, one launch (start us, length us, event | category | flops | bytes accessed | tf_op | source)
XLA Modules:
  0.0 59.5 jit_solution(11046025946954362520)
XLA Ops:
  0.6 0.0 copy-start.1
  0.6 0.5 collective-permute-start.7
  1.2 0.8 %constant_dynamic-update-slice_fusion.1 = f32[128,256]{1,0:T(8,128)S(1)} fusion(f32[64,256]{1,0:T(8,128)} %param.8), kind=kLoop, calls=%fused_computation.1 | loop fusion | bytes 131072
  2.0 0.0 copy-done.1
  2.0 2.6 %collective-permute-start.2 = (f32[128,256]{1,0:T(8,128)S(1)}, f32[128,256]{1,0:T(8,128)S(1)}, u32[]{:S(2)}, u32[]{:S(2)}) collective-permute-start(f32[128,256]{1,0:T(8,128)S(1)} %constant_dynamic-update-slice_fusion.refs_0_), channel_id=1, source_target_pairs={{0,1},{1,2},{2,3},{3,0},{4,5},{5,6},{6,7},{7,4},{8,9},{9,10},{10,1... | collective-permute-start | bytes 393224 | tf_op jit(solution)/shard_map/ppermute | solution.py:292
  4.7 2.6 %collective-permute-start.1 = (f32[128,256]{1,0:T(8,128)S(1)}, f32[128,256]{1,0:T(8,128)S(1)}, u32[]{:S(2)}, u32[]{:S(2)}) collective-permute-start(f32[128,256]{1,0:T(8,128)S(1)} %constant_dynamic-update-slice_fusion.refs_0_), channel_id=1, source_target_pairs={{0,2},{1,3},{2,0},{3,1},{4,6},{5,7},{6,4},{7,5},{8,10},{9,11},{10,... | collective-permute-start | bytes 393224 | tf_op jit(solution)/shard_map/ppermute | solution.py:292
  7.2 1.3 %collective-permute-start = (f32[128,256]{1,0:T(8,128)S(1)}, f32[128,256]{1,0:T(8,128)S(1)}, u32[]{:S(2)}, u32[]{:S(2)}) collective-permute-start(f32[128,256]{1,0:T(8,128)S(1)} %constant_dynamic-update-slice_fusion.refs_0_), channel_id=1, source_target_pairs={{0,3},{1,0},{2,1},{3,2},{4,7},{5,4},{6,5},{7,6},{8,11},{9,8},{10,9... | collective-permute-start | bytes 393224 | tf_op jit(solution)/shard_map/ppermute | solution.py:292
  8.6 0.0 collective-permute-start.3
  8.6 2.5 %collective-permute-done.2.refs_3_ = f32[128,256]{1,0:T(8,128)S(1)} collective-permute-done((f32[128,256]{1,0:T(8,128)S(1)}, f32[128,256]{1,0:T(8,128)S(1)}, u32[]{:S(2)}, u32[]{:S(2)}) %collective-permute-start.2) | collective-permute-done | bytes 131104 | tf_op jit(solution)/shard_map/ppermute | solution.py:292
  11.1 0.0 collective-permute-start.6
  11.1 5.4 %collective-permute-done.1.refs_2_ = f32[128,256]{1,0:T(8,128)S(1)} collective-permute-done((f32[128,256]{1,0:T(8,128)S(1)}, f32[128,256]{1,0:T(8,128)S(1)}, u32[]{:S(2)}, u32[]{:S(2)}) %collective-permute-start.1) | collective-permute-done | bytes 131104 | tf_op jit(solution)/shard_map/ppermute | solution.py:292
  16.5 0.0 collective-permute-start.5
  16.5 0.0 collective-permute-done.refs_1_
  16.5 0.5 collective-permute-start.4
  17.0 1.2 %shard_map.77 = (f32[4,128,256]{2,1,0:T(8,128)S(1)}, f32[4,128,256]{2,1,0:T(8,128)S(1)}, f32[64,256]{1,0:T(8,128)S(1)}) custom-call(f32[4,2,128,256]{3,2,1,0:T(8,128)} %bitcast.6, f32[4,2,128,256]{3,2,1,0:T(8,128)} %bitcast.5, f32[64,256]{1,0:T(8,128)} %refs_2_.1), custom_call_target="tpu_custom_call" | custom-call | bytes 3276800 | tf_op jit(solution)/shard_map/pallas_call | solution.py:45
  18.3 0.0 collective-permute-done.3.refs_4_
  18.3 0.0 collective-permute-done.6.refs_7_
  18.3 0.0 collective-permute-done.5.refs_6_
  18.3 0.0 collective-permute-done.4.refs_5_
  18.3 0.0 collective-permute-done.7
  18.3 1.9 %shard_map.78 = (f32[256,256]{1,0:T(8,128)S(1)}, f32[256,256]{1,0:T(8,128)S(1)}, f32[64,256]{1,0:T(8,128)S(1)}, f32[256,256]{1,0:T(8,128)S(1)}, f32[256,256]{1,0...) custom-call(f32[128,256]{1,0:T(8,128)S(1)} %constant_dynamic-update-slice_fusion.refs_0_, ...), custom_call_target="tpu_custom_call" | custom-call | bytes 4849664 | tf_op jit(solution)/shard_map/pallas_call | solution.py:45
  20.3 3.0 %collective-permute-start.9 = (f32[256,256]{1,0:T(8,128)S(1)}, f32[256,256]{1,0:T(8,128)S(1)}, u32[]{:S(2)}, u32[]{:S(2)}) collective-permute-start(f32[256,256]{1,0:T(8,128)S(1)} %get-tuple-element.26.refs_0_.refs_1_), channel_id=1, source_target_pairs={{0,8},{4,12},{16,24},{20,28},{1,9},{5,13},{17,25},{21,29},{2,10},{... | collective-permute-start | bytes 786440 | tf_op jit(solution)/shard_map/ppermute | solution.py:283
  23.3 2.9 %collective-permute-start.17 = (f32[64,256]{1,0:T(8,128)S(1)}, f32[64,256]{1,0:T(8,128)S(1)}, u32[]{:S(2)}, u32[]{:S(2)}) collective-permute-start(f32[64,256]{1,0:T(8,128)S(1)} %get-tuple-element.36.refs_0_), channel_id=1, source_target_pairs={{0,1},{1,0},{2,3},{3,2},{4,5},{5,4},{6,7},{7,6},{8,9},{9,8},{10,11... | collective-permute-start | bytes 196616 | tf_op jit(solution)/shard_map/ppermute | solution.py:334
  26.2 1.3 %collective-permute-start.12 = (f32[256,256]{1,0:T(8,128)S(1)}, f32[256,256]{1,0:T(8,128)S(1)}, u32[]{:S(2)}, u32[]{:S(2)}) collective-permute-start(f32[256,256]{1,0:T(8,128)S(1)} %get-tuple-element.31.refs_0_.refs_1_), channel_id=1, source_target_pairs={{0,8},{4,12},{16,24},{20,28},{1,9},{5,13},{17,25},{21,29},{2,10},{... | collective-permute-start | bytes 786440 | tf_op jit(solution)/shard_map/ppermute | solution.py:283
  27.5 0.7 %collective-permute-start.8 = (f32[256,256]{1,0:T(8,128)S(1)}, f32[256,256]{1,0:T(8,128)S(1)}, u32[]{:S(2)}, u32[]{:S(2)}) collective-permute-start(f32[256,256]{1,0:T(8,128)S(1)} %get-tuple-element.28.refs_2_.refs_3_), channel_id=1, source_target_pairs={{16,24},{20,28},{17,25},{21,29},{18,26},{22,30},{19,27},{23,31}} | collective-permute-start | bytes 786440 | tf_op jit(solution)/shard_map/ppermute | solution.py:283
  28.2 0.4 collective-permute-done.17.refs_1_
  28.6 2.0 %collective-permute-start.18 = (f32[128,256]{1,0:T(8,128)S(1)}, f32[128,256]{1,0:T(8,128)S(1)}, u32[]{:S(2)}, u32[]{:S(2)}) collective-permute-start(f32[128,256]{1,0:T(8,128)S(1)} %shard_map.84.refs_0_), channel_id=1, source_target_pairs={{0,2},{1,3},{2,0},{3,1},{4,6},{5,7},{6,4},{7,5},{8,10},{9,11},{10,... | collective-permute-start | bytes 393224 | tf_op jit(solution)/shard_map/ppermute | solution.py:334
  30.6 0.0 collective-permute-done.9.refs_1_.refs_5_
  30.6 0.3 shard_map.79.refs_3_.refs_2_
  30.9 0.7 %collective-permute-start.11 = (f32[256,256]{1,0:T(8,128)S(1)}, f32[256,256]{1,0:T(8,128)S(1)}, u32[]{:S(2)}, u32[]{:S(2)}) collective-permute-start(f32[256,256]{1,0:T(8,128)S(1)} %shard_map.79.refs_3_.refs_2_), channel_id=1, source_target_pairs={{8,16},{12,20},{9,17},{13,21},{10,18},{14,22},{11,19},{15,23}} | collective-permute-start | bytes 786440 | tf_op jit(solution)/shard_map/ppermute | solution.py:283
  31.6 0.7 %collective-permute-start.10 = (f32[256,256]{1,0:T(8,128)S(1)}, f32[256,256]{1,0:T(8,128)S(1)}, u32[]{:S(2)}, u32[]{:S(2)}) collective-permute-start(f32[256,256]{1,0:T(8,128)S(1)} %shard_map.79.refs_3_.refs_2_), channel_id=1, source_target_pairs={{8,24},{12,28},{9,25},{13,29},{10,26},{14,30},{11,27},{15,31}} | collective-permute-start | bytes 786440 | tf_op jit(solution)/shard_map/ppermute | solution.py:283
  32.3 2.4 %collective-permute-done.12.refs_1_.refs_5_ = f32[256,256]{1,0:T(8,128)S(1)} collective-permute-done((f32[256,256]{1,0:T(8,128)S(1)}, f32[256,256]{1,0:T(8,128)S(1)}, u32[]{:S(2)}, u32[]{:S(2)}) %collective-permute-start.12) | collective-permute-done | bytes 262176 | tf_op jit(solution)/shard_map/ppermute | solution.py:283
  34.7 0.3 shard_map.81
  35.0 0.7 %collective-permute-start.14 = (f32[256,256]{1,0:T(8,128)S(1)}, f32[256,256]{1,0:T(8,128)S(1)}, u32[]{:S(2)}, u32[]{:S(2)}) collective-permute-start(f32[256,256]{1,0:T(8,128)S(1)} %shard_map.81), channel_id=1, source_target_pairs={{8,16},{12,20},{9,17},{13,21},{10,18},{14,22},{11,19},{15,23}} | collective-permute-start | bytes 786440 | tf_op jit(solution)/shard_map/ppermute | solution.py:283
  35.7 1.8 %collective-permute-done.18.refs_1_ = f32[128,256]{1,0:T(8,128)S(1)} collective-permute-done((f32[128,256]{1,0:T(8,128)S(1)}, f32[128,256]{1,0:T(8,128)S(1)}, u32[]{:S(2)}, u32[]{:S(2)}) %collective-permute-start.18) | collective-permute-done | bytes 131104 | tf_op jit(solution)/shard_map/ppermute | solution.py:334
  37.5 0.7 %collective-permute-start.13 = (f32[256,256]{1,0:T(8,128)S(1)}, f32[256,256]{1,0:T(8,128)S(1)}, u32[]{:S(2)}, u32[]{:S(2)}) collective-permute-start(f32[256,256]{1,0:T(8,128)S(1)} %shard_map.81), channel_id=1, source_target_pairs={{8,24},{12,28},{9,25},{13,29},{10,26},{14,30},{11,27},{15,31}} | collective-permute-start | bytes 786440 | tf_op jit(solution)/shard_map/ppermute | solution.py:283
  38.2 0.0 collective-permute-done.8.refs_4_
  38.2 0.1 collective-permute-start.19
  38.3 0.0 collective-permute-done.11.refs_7_
  38.3 0.0 collective-permute-done.10.refs_6_
  38.3 0.5 shard_map.80
  38.8 0.0 collective-permute-done.14.refs_7_
  38.8 0.0 collective-permute-done.13.refs_6_
  38.8 0.5 shard_map.82
  39.3 0.5 collective-permute-start.16
  39.8 0.1 collective-permute-start.15
  39.9 0.0 collective-permute-done.19.refs_5_
  39.9 0.6 %shard_map.86 = (f32[128,256]{1,0:T(8,128)S(1)}, f32[128,256]{1,0:T(8,128)S(1)}, f32[128,256]{1,0:T(8,128)S(1)}, f32[128,256]{1,0:T(8,128)S(1)}) custom-call(f32[256,256]{1,0:T(8,128)S(1)} %get-tuple-element.29.refs_8_.refs_0_, f32[256,256]{1,0:T(8,128)S(1)} %get-tuple-element.32.refs_1_, f32[256,256]{1,0:T(8,128)S(1)} %get-tuple-element.33.refs_2_, ...), custom_call_target="tpu_custom_call" | custom-call | bytes 2097152 | tf_op jit(solution)/shard_map/pallas_call | solution.py:45
  40.5 9.5 %collective-permute-start.20 = (f32[128,256]{1,0:T(8,128)S(1)}, f32[128,256]{1,0:T(8,128)S(1)}, u32[]{:S(2)}, u32[]{:S(2)}) collective-permute-start(f32[128,256]{1,0:T(8,128)S(1)} %get-tuple-element.38), channel_id=1, source_target_pairs={{0,8},{4,12},{8,0},{12,4},{16,24},{20,28},{24,16},{28,20},{1,9},{5... | collective-permute-start | bytes 393224 | tf_op jit(solution)/shard_map/ppermute | solution.py:283
  50.0 2.5 %collective-permute-start.21 = (f32[128,256]{1,0:T(8,128)S(1)}, f32[128,256]{1,0:T(8,128)S(1)}, u32[]{:S(2)}, u32[]{:S(2)}) collective-permute-start(f32[128,256]{1,0:T(8,128)S(1)} %get-tuple-element.39), channel_id=1, source_target_pairs={{0,16},{4,20},{8,24},{12,28},{16,0},{20,4},{24,8},{28,12},{1,17},{... | collective-permute-start | bytes 393224 | tf_op jit(solution)/shard_map/ppermute | solution.py:283
  52.5 0.0 copy-start
  52.5 0.0 collective-permute-start.22
  52.5 0.0 collective-permute-done.16.refs_3_
  52.5 0.0 collective-permute-done.15.refs_2_
  52.6 1.1 %shard_map.83 = (f32[4,2,128,256]{3,2,1,0:T(8,128)}, f32[8,128]{1,0:T(8,128)S(1)}) custom-call(f32[256,256]{1,0:T(8,128)S(1)} %get-tuple-element.29.refs_8_.refs_0_, f32[256,256]{1,0:T(8,128)S(1)} %get-tuple-element.32.refs_1_, f32[256,256]{1,0:T(8,128)S(1)} %collective-permute-done.15.refs_2_, f32[256,256]{1,0:T(8,128)S(1)} %collective-permute-done.16.refs_3_), custom_call_target="tpu_custom_call" | custom-call | bytes 2097152 | tf_op jit(solution)/shard_map/pallas_call | solution.py:407
  53.7 0.1 collective-permute-done.20.refs_2_
  53.8 5.0 %collective-permute-done.21.refs_3_ = f32[128,256]{1,0:T(8,128)S(1)} collective-permute-done((f32[128,256]{1,0:T(8,128)S(1)}, f32[128,256]{1,0:T(8,128)S(1)}, u32[]{:S(2)}, u32[]{:S(2)}) %collective-permute-start.21) | collective-permute-done | bytes 131104 | tf_op jit(solution)/shard_map/ppermute | solution.py:283
  58.8 0.0 collective-permute-done.22.refs_4_
  58.8 0.0 copy-done
  58.8 0.7 %shard_map.87 = f32[128,256]{1,0:T(8,128)} custom-call(f32[128,256]{1,0:T(8,128)S(1)} %copy-done, f32[128,256]{1,0:T(8,128)S(1)} %get-tuple-element.37.refs_1_, f32[128,256]{1,0:T(8,128)S(1)} %collective-permute-done.20.refs_2_, f32[128,256]{1,0:T(8,128)S(1)} %collective-permute-done.21.refs_3_, f32[128,256]{1,0:T(8,128)S(1)} %collective-permute-done.22.refs_4_, ...), custom_call_target="tpu_custom_call" | custom-call | bytes 786432 | tf_op jit(solution)/shard_map/pallas_call | solution.py:45
  (3 shorter events, 0.0 us)
Async XLA Ops:
  0.6 1.4 %copy-start.1 = (f32[64,256]{1,0:T(8,128)S(1)}, f32[64,256]{1,0:T(8,128)}, u32[]{:S(2)}) copy-start(f32[64,256]{1,0:T(8,128)} %param.9) | copy-start | bytes 196612
  0.6 17.7 %collective-permute-start.7 = (f32[1024,256]{1,0:T(8,128)}, f32[1024,256]{1,0:T(8,128)S(1)}, u32[]{:S(2)}, u32[]{:S(2)}) collective-permute-start(f32[1024,256]{1,0:T(8,128)} %param.6), channel_id=1, source_target_pairs={{0,4},{4,0},{8,12},{12,8},{16,20},{20,16},{24,28},{28,24},{1,5},{5... | collective-permute-start | bytes 3145736 | tf_op jit(solution)/shard_map/ppermute | solution.py:287
  2.0 9.1 %collective-permute-start.2 = (f32[128,256]{1,0:T(8,128)S(1)}, f32[128,256]{1,0:T(8,128)S(1)}, u32[]{:S(2)}, u32[]{:S(2)}) collective-permute-start(f32[128,256]{1,0:T(8,128)S(1)} %constant_dynamic-update-slice_fusion.refs_0_), channel_id=1, source_target_pairs={{0,1},{1,2},{2,3},{3,0},{4,5},{5,6},{6,7},{7,4},{8,9},{9,10},{10,1... | collective-permute-start | bytes 393224 | tf_op jit(solution)/shard_map/ppermute | solution.py:292
  4.7 11.9 %collective-permute-start.1 = (f32[128,256]{1,0:T(8,128)S(1)}, f32[128,256]{1,0:T(8,128)S(1)}, u32[]{:S(2)}, u32[]{:S(2)}) collective-permute-start(f32[128,256]{1,0:T(8,128)S(1)} %constant_dynamic-update-slice_fusion.refs_0_), channel_id=1, source_target_pairs={{0,2},{1,3},{2,0},{3,1},{4,6},{5,7},{6,4},{7,5},{8,10},{9,11},{10,... | collective-permute-start | bytes 393224 | tf_op jit(solution)/shard_map/ppermute | solution.py:292
  7.2 9.3 %collective-permute-start = (f32[128,256]{1,0:T(8,128)S(1)}, f32[128,256]{1,0:T(8,128)S(1)}, u32[]{:S(2)}, u32[]{:S(2)}) collective-permute-start(f32[128,256]{1,0:T(8,128)S(1)} %constant_dynamic-update-slice_fusion.refs_0_), channel_id=1, source_target_pairs={{0,3},{1,0},{2,1},{3,2},{4,7},{5,4},{6,5},{7,6},{8,11},{9,8},{10,9... | collective-permute-start | bytes 393224 | tf_op jit(solution)/shard_map/ppermute | solution.py:292
  8.6 9.7 %collective-permute-start.3 = (f32[128,256]{1,0:T(8,128)S(1)}, f32[128,256]{1,0:T(8,128)S(1)}, u32[]{:S(2)}, u32[]{:S(2)}) collective-permute-start(f32[128,256]{1,0:T(8,128)S(1)} %constant_dynamic-update-slice_fusion.refs_0_), channel_id=1, source_target_pairs={{0,4},{4,0},{8,12},{12,8},{16,20},{20,16},{24,28},{28,24},{1,5},{5... | collective-permute-start | bytes 393224 | tf_op jit(solution)/shard_map/ppermute | solution.py:287
  11.1 7.2 %collective-permute-start.6 = (f32[128,256]{1,0:T(8,128)S(1)}, f32[128,256]{1,0:T(8,128)S(1)}, u32[]{:S(2)}, u32[]{:S(2)}) collective-permute-start(f32[128,256]{1,0:T(8,128)S(1)} %collective-permute-done.2.refs_3_), channel_id=1, source_target_pairs={{0,4},{4,0},{8,12},{12,8},{16,20},{20,16},{24,28},{28,24},{1,5},{5... | collective-permute-start | bytes 393224 | tf_op jit(solution)/shard_map/ppermute | solution.py:287
  16.5 1.8 %collective-permute-start.5 = (f32[128,256]{1,0:T(8,128)S(1)}, f32[128,256]{1,0:T(8,128)S(1)}, u32[]{:S(2)}, u32[]{:S(2)}) collective-permute-start(f32[128,256]{1,0:T(8,128)S(1)} %collective-permute-done.1.refs_2_), channel_id=1, source_target_pairs={{0,4},{4,0},{8,12},{12,8},{16,20},{20,16},{24,28},{28,24},{1,5},{5... | collective-permute-start | bytes 393224 | tf_op jit(solution)/shard_map/ppermute | solution.py:287
  16.5 1.8 %collective-permute-start.4 = (f32[128,256]{1,0:T(8,128)S(1)}, f32[128,256]{1,0:T(8,128)S(1)}, u32[]{:S(2)}, u32[]{:S(2)}) collective-permute-start(f32[128,256]{1,0:T(8,128)S(1)} %collective-permute-done.refs_1_), channel_id=1, source_target_pairs={{0,4},{4,0},{8,12},{12,8},{16,20},{20,16},{24,28},{28,24},{1,5},{5... | collective-permute-start | bytes 393224 | tf_op jit(solution)/shard_map/ppermute | solution.py:287
  20.3 10.3 %collective-permute-start.9 = (f32[256,256]{1,0:T(8,128)S(1)}, f32[256,256]{1,0:T(8,128)S(1)}, u32[]{:S(2)}, u32[]{:S(2)}) collective-permute-start(f32[256,256]{1,0:T(8,128)S(1)} %get-tuple-element.26.refs_0_.refs_1_), channel_id=1, source_target_pairs={{0,8},{4,12},{16,24},{20,28},{1,9},{5,13},{17,25},{21,29},{2,10},{... | collective-permute-start | bytes 786440 | tf_op jit(solution)/shard_map/ppermute | solution.py:283
  23.3 5.3 %collective-permute-start.17 = (f32[64,256]{1,0:T(8,128)S(1)}, f32[64,256]{1,0:T(8,128)S(1)}, u32[]{:S(2)}, u32[]{:S(2)}) collective-permute-start(f32[64,256]{1,0:T(8,128)S(1)} %get-tuple-element.36.refs_0_), channel_id=1, source_target_pairs={{0,1},{1,0},{2,3},{3,2},{4,5},{5,4},{6,7},{7,6},{8,9},{9,8},{10,11... | collective-permute-start | bytes 196616 | tf_op jit(solution)/shard_map/ppermute | solution.py:334
  26.2 8.5 %collective-permute-start.12 = (f32[256,256]{1,0:T(8,128)S(1)}, f32[256,256]{1,0:T(8,128)S(1)}, u32[]{:S(2)}, u32[]{:S(2)}) collective-permute-start(f32[256,256]{1,0:T(8,128)S(1)} %get-tuple-element.31.refs_0_.refs_1_), channel_id=1, source_target_pairs={{0,8},{4,12},{16,24},{20,28},{1,9},{5,13},{17,25},{21,29},{2,10},{... | collective-permute-start | bytes 786440 | tf_op jit(solution)/shard_map/ppermute | solution.py:283
  27.5 10.7 %collective-permute-start.8 = (f32[256,256]{1,0:T(8,128)S(1)}, f32[256,256]{1,0:T(8,128)S(1)}, u32[]{:S(2)}, u32[]{:S(2)}) collective-permute-start(f32[256,256]{1,0:T(8,128)S(1)} %get-tuple-element.28.refs_2_.refs_3_), channel_id=1, source_target_pairs={{16,24},{20,28},{17,25},{21,29},{18,26},{22,30},{19,27},{23,31}} | collective-permute-start | bytes 786440 | tf_op jit(solution)/shard_map/ppermute | solution.py:283
  28.6 8.8 %collective-permute-start.18 = (f32[128,256]{1,0:T(8,128)S(1)}, f32[128,256]{1,0:T(8,128)S(1)}, u32[]{:S(2)}, u32[]{:S(2)}) collective-permute-start(f32[128,256]{1,0:T(8,128)S(1)} %shard_map.84.refs_0_), channel_id=1, source_target_pairs={{0,2},{1,3},{2,0},{3,1},{4,6},{5,7},{6,4},{7,5},{8,10},{9,11},{10,... | collective-permute-start | bytes 393224 | tf_op jit(solution)/shard_map/ppermute | solution.py:334
  30.9 7.4 %collective-permute-start.11 = (f32[256,256]{1,0:T(8,128)S(1)}, f32[256,256]{1,0:T(8,128)S(1)}, u32[]{:S(2)}, u32[]{:S(2)}) collective-permute-start(f32[256,256]{1,0:T(8,128)S(1)} %shard_map.79.refs_3_.refs_2_), channel_id=1, source_target_pairs={{8,16},{12,20},{9,17},{13,21},{10,18},{14,22},{11,19},{15,23}} | collective-permute-start | bytes 786440 | tf_op jit(solution)/shard_map/ppermute | solution.py:283
  31.6 6.7 %collective-permute-start.10 = (f32[256,256]{1,0:T(8,128)S(1)}, f32[256,256]{1,0:T(8,128)S(1)}, u32[]{:S(2)}, u32[]{:S(2)}) collective-permute-start(f32[256,256]{1,0:T(8,128)S(1)} %shard_map.79.refs_3_.refs_2_), channel_id=1, source_target_pairs={{8,24},{12,28},{9,25},{13,29},{10,26},{14,30},{11,27},{15,31}} | collective-permute-start | bytes 786440 | tf_op jit(solution)/shard_map/ppermute | solution.py:283
  35.0 3.8 %collective-permute-start.14 = (f32[256,256]{1,0:T(8,128)S(1)}, f32[256,256]{1,0:T(8,128)S(1)}, u32[]{:S(2)}, u32[]{:S(2)}) collective-permute-start(f32[256,256]{1,0:T(8,128)S(1)} %shard_map.81), channel_id=1, source_target_pairs={{8,16},{12,20},{9,17},{13,21},{10,18},{14,22},{11,19},{15,23}} | collective-permute-start | bytes 786440 | tf_op jit(solution)/shard_map/ppermute | solution.py:283
  37.5 1.3 %collective-permute-start.13 = (f32[256,256]{1,0:T(8,128)S(1)}, f32[256,256]{1,0:T(8,128)S(1)}, u32[]{:S(2)}, u32[]{:S(2)}) collective-permute-start(f32[256,256]{1,0:T(8,128)S(1)} %shard_map.81), channel_id=1, source_target_pairs={{8,24},{12,28},{9,25},{13,29},{10,26},{14,30},{11,27},{15,31}} | collective-permute-start | bytes 786440 | tf_op jit(solution)/shard_map/ppermute | solution.py:283
  38.2 1.7 %collective-permute-start.19 = (f32[256,256]{1,0:T(8,128)S(1)}, f32[256,256]{1,0:T(8,128)S(1)}, u32[]{:S(2)}, u32[]{:S(2)}) collective-permute-start(f32[256,256]{1,0:T(8,128)S(1)} %shard_map.85.refs_4_), channel_id=1, source_target_pairs={{0,4},{4,0},{8,12},{12,8},{16,20},{20,16},{24,28},{28,24},{1,5},{5... | collective-permute-start | bytes 786440 | tf_op jit(solution)/shard_map/ppermute | solution.py:287
  39.3 13.3 %collective-permute-start.16 = (f32[256,256]{1,0:T(8,128)S(1)}, f32[256,256]{1,0:T(8,128)S(1)}, u32[]{:S(2)}, u32[]{:S(2)}) collective-permute-start(f32[256,256]{1,0:T(8,128)S(1)} %get-tuple-element.34.refs_3_), channel_id=1, source_target_pairs={{0,4},{4,0},{8,12},{12,8},{16,20},{20,16},{24,28},{28,24},{1,5},{5... | collective-permute-start | bytes 786440 | tf_op jit(solution)/shard_map/ppermute | solution.py:287
  39.8 12.7 %collective-permute-start.15 = (f32[256,256]{1,0:T(8,128)S(1)}, f32[256,256]{1,0:T(8,128)S(1)}, u32[]{:S(2)}, u32[]{:S(2)}) collective-permute-start(f32[256,256]{1,0:T(8,128)S(1)} %get-tuple-element.33.refs_2_), channel_id=1, source_target_pairs={{0,4},{4,0},{8,12},{12,8},{16,20},{20,16},{24,28},{28,24},{1,5},{5... | collective-permute-start | bytes 786440 | tf_op jit(solution)/shard_map/ppermute | solution.py:287
  40.5 13.3 %collective-permute-start.20 = (f32[128,256]{1,0:T(8,128)S(1)}, f32[128,256]{1,0:T(8,128)S(1)}, u32[]{:S(2)}, u32[]{:S(2)}) collective-permute-start(f32[128,256]{1,0:T(8,128)S(1)} %get-tuple-element.38), channel_id=1, source_target_pairs={{0,8},{4,12},{8,0},{12,4},{16,24},{20,28},{24,16},{28,20},{1,9},{5... | collective-permute-start | bytes 393224 | tf_op jit(solution)/shard_map/ppermute | solution.py:283
  50.0 8.8 %collective-permute-start.21 = (f32[128,256]{1,0:T(8,128)S(1)}, f32[128,256]{1,0:T(8,128)S(1)}, u32[]{:S(2)}, u32[]{:S(2)}) collective-permute-start(f32[128,256]{1,0:T(8,128)S(1)} %get-tuple-element.39), channel_id=1, source_target_pairs={{0,16},{4,20},{8,24},{12,28},{16,0},{20,4},{24,8},{28,12},{1,17},{... | collective-permute-start | bytes 393224 | tf_op jit(solution)/shard_map/ppermute | solution.py:283
  52.5 6.3 %copy-start = (f32[128,256]{1,0:T(8,128)S(1)}, f32[128,256]{1,0:T(8,128)}, u32[]{:S(2)}) copy-start(f32[128,256]{1,0:T(8,128)} %refs_0_.1) | copy-start | bytes 393220
  52.5 6.3 %collective-permute-start.22 = (f32[128,256]{1,0:T(8,128)S(1)}, f32[128,256]{1,0:T(8,128)S(1)}, u32[]{:S(2)}, u32[]{:S(2)}) collective-permute-start(f32[128,256]{1,0:T(8,128)S(1)} %get-tuple-element.40), channel_id=1, source_target_pairs={{0,24},{4,28},{8,16},{12,20},{16,8},{20,12},{24,0},{28,4},{1,25},{... | collective-permute-start | bytes 393224 | tf_op jit(solution)/shard_map/ppermute | solution.py:283

commit v6 on v5

--- a/solution.py
+++ b/solution.py
@@ -10,8 +10,9 @@
 
 CHUNKS = 2
 FIRST = 1 / 2
-SCAN_SPAN = 2_000_000_000
-FINISH_SPAN = 4_000_000_000
+SCAN_SPAN = 4_000_000_000
+FINISH_SPAN = 2_000_000_000
+TAIL_SPAN = 8_000_000_000
 NT = (((1,), (1,)), ((), ()))
 NN = (((1,), (0,)), ((), ()))
 VMEM = pl.BlockSpec(memory_space=pltpu.VMEM)
@@ -213,20 +214,14 @@
     leave[...] = jnp.where(first, solved_b, solved_a)
 
 
-def shared(chips, *refs):
-    refs = iter(refs)
-    stays, leaves = take(refs, CHUNKS), take(refs, CHUNKS)
-    own, other = take(refs, 2)
-    outs, tails = take(refs, chips), take(refs, CHUNKS)
+def shared(chips, stay, leave, own, other, *refs):
+    *outs, tail = refs
     chip, _ = chip_and_core()
-    own, other = split(own[...]), split(other[...])
-    for k in range(CHUNKS):
-        tails[k][...] = dot3(split(stays[k][...]), own, NN) + dot3(split(leaves[k][...]), other, NN)
+    tail[...] = dot3(split(stay[...]), split(own[...]), NN) + dot3(split(leave[...]), split(other[...]), NN)
+    height = outs[0].shape[0]
     for shift in range(chips):
-        for k, (begin, end) in enumerate(cuts(outs[0].shape[0])):
-            height = end - begin
-            start = pl.multiple_of(destination(chip, shift, chips) * height, height)
-            outs[shift][begin:end, :] = tails[k][pl.ds(start, height), :]
+        start = pl.multiple_of(destination(chip, shift, chips) * height, height)
+        outs[shift][...] = tail[pl.ds(start, height), :]
 
 
 def destination(chip, shift, chips):
@@ -270,12 +265,10 @@
         copy.wait()
 
 
-def subtract(cols, *refs):
+def subtract(chips, cols, *refs):
     *shares, out = refs
-    total = shares[0][...]
-    for share in shares[1:]:
-        total = total + share[...]
-    out[...] = cols[...] - total
+    for k, (begin, end) in enumerate(cuts(out.shape[0])):
+        out[begin:end, :] = cols[begin:end, :] - total(shares[k * chips : (k + 1) * chips])
 
 
 def between_chips(value, pairs):
@@ -382,7 +375,7 @@
         own_coupling = spread([])
     other_coupling = to_other_core(own_coupling)
     arrivals = len(arrived[0])
-    stays, leaves = [], []
+    stays, leaves, shares = [], [], []
     for k in range(CHUNKS):
         stay, leave = call(
             functools.partial(finish, half, arrivals),
@@ -390,19 +383,21 @@
             [parts[k], carries[k], map_a, both] + ([across] if arrivals else []) + [priors[k], *arrived[k]],
             [pltpu.VMEM(slices[k], jnp.float32)],
             span=FINISH_SPAN,
-            after=stays[-1:],
+            after=shares[-1:],
         )
         stays.append(stay)
         leaves.append(leave)
-    shares = call(
-        functools.partial(shared, chips),
-        [(piece, width)] * chips,
-        [*stays, *leaves, own_coupling, other_coupling],
-        [pltpu.VMEM(shape, jnp.float32) for shape in slices],
-    )
-    shares = list(shares)
-    for k in reversed(range(1, chips)):
-        shares[k] = between_chips(shares[k], [(a, destination(a, k, chips)) for a in range(chips)])
+        begin, end = cuts(piece)[k]
+        own_share, *others = call(
+            functools.partial(shared, chips),
+            [(end - begin, width)] * chips,
+            [stay, leave, own_coupling, other_coupling],
+            [pltpu.VMEM(slices[k], jnp.float32)],
+            span=TAIL_SPAN,
+        )
+        for j in reversed(range(1, chips)):
+            others[j - 1] = between_chips(others[j - 1], [(a, destination(a, j, chips)) for a in range(chips)])
+        shares += [*others, own_share]
     came = [to_other_core(leave) for leave in leaves]
     factor, token = pl.pallas_call(
         interleave,
@@ -416,7 +411,7 @@
         compiler_params=pltpu.CompilerParams(vmem_limit_bytes=4 << 20),
         cost_estimate=pl.CostEstimate(flops=0, bytes_accessed=16 * held * width, transcendentals=0),
     )(*stays, *came)
-    (tail_out,) = call(subtract, [tail_cols.shape], [tail_cols, *shares], after=[token])
+    (tail_out,) = call(functools.partial(subtract, chips), [tail_cols.shape], [tail_cols, *shares], after=[token])
     return factor.reshape(rows, width), tail_out
 
 

time: 59.8 us -> 58.7 us (0.982)
  waiting for transfers between devices: 17.7 us -> 15.2 us
  starting transfers between devices: 32.9 us -> 34.1 us
    ppermute x10 -> x13, waiting for transfers between devices: 7.52 us -> 4.46 us  [between_chips(): return lax.ppermute(value, 'panel', pairs)]
    ppermute x10 -> x13, starting transfers between devices: 19.7 us -> 20.9 us  [between_chips(): return lax.ppermute(value, 'panel', pairs)]
    pallas_call x10 -> x11, Pallas kernels: 6.08 us -> 6.28 us  [call(): pl.pallas_call(body, out_shape=[jax.ShapeDtypeStruct(o, jnp.float32) for...]
  transfers between devices with their start and end apart: 23 -> 26, of which waited for: 7 -> 8; matrix products, arithmetic and copies ran while one was open for 1% -> 1% of each run, Pallas kernels for 8% -> 8%
where the time goes in v6:
time: 58.7 us; the launch traced here: 58.4 us
  starting transfers between devices  34.1 us (58%)
  waiting for transfers between devices  15.2 us (26%)
  Pallas kernels  7.36 us (13%)
  between operations  0.91 us (2%)
  local copies, waits for them, and re-layouts  0.86 us (1%)
    ppermute x13, starting transfers between devices, between_chips(): return lax.ppermute(value, 'panel', pairs)  20.9 us
    ppermute x3, waiting for transfers between devices, gather_rows(): lax.ppermute(value, 'row', [(j, (j + s) % count) for j in range(count)])  7.92 us
    ppermute x3, starting transfers between devices, gather_rows(): lax.ppermute(value, 'row', [(j, (j + s) % count) for j in range(count)])  6.58 us
    pallas_call x11, Pallas kernels, call(): pl.pallas_call(body, out_shape=[jax.ShapeDtypeStruct(o, jnp.float32) for...  6.28 us
    ppermute x2, starting transfers between devices, spread(): lax.ppermute(pieces[0], 'row', [(j, j ^ near) for j in range(count)])  4.87 us
    ppermute x13, waiting for transfers between devices, between_chips(): return lax.ppermute(value, 'panel', pairs)  4.46 us
    ppermute x2, waiting for transfers between devices, spread(): lax.ppermute(pieces[0], 'row', [(j, j ^ near) for j in range(count)])  2.27 us
    ppermute x8, starting transfers between devices, to_other_core(): lax.ppermute(value, 'panel', [(q, q ^ 1) for q in range(lax.axis_size('pa...  1.7 us
  transfers between devices with their start and end apart: 26, of which 8 were waited for; matrix products, arithmetic and copies ran while one was open for 1% of the time, Pallas kernels for 8%

profile of v6, /device:TPU:0, one launch (start us, length us, event | category | flops | bytes accessed | tf_op | source)
XLA Modules:
  0.0 58.4 jit_solution(6698462722089298604)
XLA Ops:
  0.6 0.5 collective-permute-start.7
  1.2 0.8 %constant_dynamic-update-slice_fusion.1 = f32[128,256]{1,0:T(8,128)S(1)} fusion(f32[64,256]{1,0:T(8,128)} %param.8), kind=kLoop, calls=%fused_computation.1 | loop fusion | bytes 131072
  2.0 0.0 copy-done.1
  2.0 2.6 %collective-permute-start.2 = (f32[128,256]{1,0:T(8,128)S(1)}, f32[128,256]{1,0:T(8,128)S(1)}, u32[]{:S(2)}, u32[]{:S(2)}) collective-permute-start(f32[128,256]{1,0:T(8,128)S(1)} %constant_dynamic-update-slice_fusion.refs_0_), channel_id=1, source_target_pairs={{0,1},{1,2},{2,3},{3,0},{4,5},{5,6},{6,7},{7,4},{8,9},{9,10},{10,1... | collective-permute-start | bytes 393224 | tf_op jit(solution)/shard_map/ppermute | solution.py:285
  4.7 2.6 %collective-permute-start.1 = (f32[128,256]{1,0:T(8,128)S(1)}, f32[128,256]{1,0:T(8,128)S(1)}, u32[]{:S(2)}, u32[]{:S(2)}) collective-permute-start(f32[128,256]{1,0:T(8,128)S(1)} %constant_dynamic-update-slice_fusion.refs_0_), channel_id=1, source_target_pairs={{0,2},{1,3},{2,0},{3,1},{4,6},{5,7},{6,4},{7,5},{8,10},{9,11},{10,... | collective-permute-start | bytes 393224 | tf_op jit(solution)/shard_map/ppermute | solution.py:285
  7.2 1.3 %collective-permute-start = (f32[128,256]{1,0:T(8,128)S(1)}, f32[128,256]{1,0:T(8,128)S(1)}, u32[]{:S(2)}, u32[]{:S(2)}) collective-permute-start(f32[128,256]{1,0:T(8,128)S(1)} %constant_dynamic-update-slice_fusion.refs_0_), channel_id=1, source_target_pairs={{0,3},{1,0},{2,1},{3,2},{4,7},{5,4},{6,5},{7,6},{8,11},{9,8},{10,9... | collective-permute-start | bytes 393224 | tf_op jit(solution)/shard_map/ppermute | solution.py:285
  8.6 0.0 collective-permute-start.3
  8.6 2.5 %collective-permute-done.2.refs_3_ = f32[128,256]{1,0:T(8,128)S(1)} collective-permute-done((f32[128,256]{1,0:T(8,128)S(1)}, f32[128,256]{1,0:T(8,128)S(1)}, u32[]{:S(2)}, u32[]{:S(2)}) %collective-permute-start.2) | collective-permute-done | bytes 131104 | tf_op jit(solution)/shard_map/ppermute | solution.py:285
  11.1 0.0 collective-permute-start.6
  11.1 5.4 %collective-permute-done.1.refs_2_ = f32[128,256]{1,0:T(8,128)S(1)} collective-permute-done((f32[128,256]{1,0:T(8,128)S(1)}, f32[128,256]{1,0:T(8,128)S(1)}, u32[]{:S(2)}, u32[]{:S(2)}) %collective-permute-start.1) | collective-permute-done | bytes 131104 | tf_op jit(solution)/shard_map/ppermute | solution.py:285
  16.5 0.0 collective-permute-start.5
  16.5 0.0 collective-permute-done.refs_1_
  16.5 0.5 collective-permute-start.4
  17.0 1.2 %shard_map.77 = (f32[4,128,256]{2,1,0:T(8,128)S(1)}, f32[4,128,256]{2,1,0:T(8,128)S(1)}, f32[64,256]{1,0:T(8,128)S(1)}) custom-call(f32[4,2,128,256]{3,2,1,0:T(8,128)} %bitcast.6, f32[4,2,128,256]{3,2,1,0:T(8,128)} %bitcast.5, f32[64,256]{1,0:T(8,128)} %refs_2_.1), custom_call_target="tpu_custom_call" | custom-call | bytes 3276800 | tf_op jit(solution)/shard_map/pallas_call | solution.py:46
  18.3 0.0 collective-permute-done.3.refs_4_
  18.3 0.0 collective-permute-done.6.refs_7_
  18.3 0.0 collective-permute-done.5.refs_6_
  18.3 0.0 collective-permute-done.4.refs_5_
  18.3 0.0 collective-permute-done.7
  18.3 1.9 %shard_map.78 = (f32[256,256]{1,0:T(8,128)S(1)}, f32[256,256]{1,0:T(8,128)S(1)}, f32[64,256]{1,0:T(8,128)S(1)}, f32[256,256]{1,0:T(8,128)S(1)}, f32[256,256]{1,0...) custom-call(f32[128,256]{1,0:T(8,128)S(1)} %constant_dynamic-update-slice_fusion.refs_0_, ...), custom_call_target="tpu_custom_call" | custom-call | bytes 4849664 | tf_op jit(solution)/shard_map/pallas_call | solution.py:46
  20.3 3.0 %collective-permute-start.9 = (f32[256,256]{1,0:T(8,128)S(1)}, f32[256,256]{1,0:T(8,128)S(1)}, u32[]{:S(2)}, u32[]{:S(2)}) collective-permute-start(f32[256,256]{1,0:T(8,128)S(1)} %get-tuple-element.30.refs_0_.refs_1_), channel_id=1, source_target_pairs={{0,8},{4,12},{16,24},{20,28},{1,9},{5,13},{17,25},{21,29},{2,10},{... | collective-permute-start | bytes 786440 | tf_op jit(solution)/shard_map/ppermute | solution.py:276
  23.3 2.9 %collective-permute-start.15 = (f32[64,256]{1,0:T(8,128)S(1)}, f32[64,256]{1,0:T(8,128)S(1)}, u32[]{:S(2)}, u32[]{:S(2)}) collective-permute-start(f32[64,256]{1,0:T(8,128)S(1)} %get-tuple-element.37.refs_0_), channel_id=1, source_target_pairs={{0,1},{1,0},{2,3},{3,2},{4,5},{5,4},{6,7},{7,6},{8,9},{9,8},{10,11... | collective-permute-start | bytes 196616 | tf_op jit(solution)/shard_map/ppermute | solution.py:327
  26.2 1.3 %collective-permute-start.12 = (f32[256,256]{1,0:T(8,128)S(1)}, f32[256,256]{1,0:T(8,128)S(1)}, u32[]{:S(2)}, u32[]{:S(2)}) collective-permute-start(f32[256,256]{1,0:T(8,128)S(1)} %get-tuple-element.35.refs_0_.refs_1_), channel_id=1, source_target_pairs={{0,8},{4,12},{16,24},{20,28},{1,9},{5,13},{17,25},{21,29},{2,10},{... | collective-permute-start | bytes 786440 | tf_op jit(solution)/shard_map/ppermute | solution.py:276
  27.5 0.7 %collective-permute-start.8 = (f32[256,256]{1,0:T(8,128)S(1)}, f32[256,256]{1,0:T(8,128)S(1)}, u32[]{:S(2)}, u32[]{:S(2)}) collective-permute-start(f32[256,256]{1,0:T(8,128)S(1)} %get-tuple-element.32.refs_2_.refs_3_), channel_id=1, source_target_pairs={{16,24},{20,28},{17,25},{21,29},{18,26},{22,30},{19,27},{23,31}} | collective-permute-start | bytes 786440 | tf_op jit(solution)/shard_map/ppermute | solution.py:276
  28.2 0.4 collective-permute-done.15.refs_1_
  28.6 2.0 %collective-permute-start.16 = (f32[128,256]{1,0:T(8,128)S(1)}, f32[128,256]{1,0:T(8,128)S(1)}, u32[]{:S(2)}, u32[]{:S(2)}) collective-permute-start(f32[128,256]{1,0:T(8,128)S(1)} %shard_map.82.refs_0_), channel_id=1, source_target_pairs={{0,2},{1,3},{2,0},{3,1},{4,6},{5,7},{6,4},{7,5},{8,10},{9,11},{10,... | collective-permute-start | bytes 393224 | tf_op jit(solution)/shard_map/ppermute | solution.py:327
  30.6 0.0 collective-permute-done.9.refs_1_.refs_5_
  30.6 0.3 shard_map.79.refs_3_.refs_2_
  30.9 0.7 %collective-permute-start.11 = (f32[256,256]{1,0:T(8,128)S(1)}, f32[256,256]{1,0:T(8,128)S(1)}, u32[]{:S(2)}, u32[]{:S(2)}) collective-permute-start(f32[256,256]{1,0:T(8,128)S(1)} %shard_map.79.refs_3_.refs_2_), channel_id=1, source_target_pairs={{8,16},{12,20},{9,17},{13,21},{10,18},{14,22},{11,19},{15,23}} | collective-permute-start | bytes 786440 | tf_op jit(solution)/shard_map/ppermute | solution.py:276
  31.6 0.7 %collective-permute-start.10 = (f32[256,256]{1,0:T(8,128)S(1)}, f32[256,256]{1,0:T(8,128)S(1)}, u32[]{:S(2)}, u32[]{:S(2)}) collective-permute-start(f32[256,256]{1,0:T(8,128)S(1)} %shard_map.79.refs_3_.refs_2_), channel_id=1, source_target_pairs={{8,24},{12,28},{9,25},{13,29},{10,26},{14,30},{11,27},{15,31}} | collective-permute-start | bytes 786440 | tf_op jit(solution)/shard_map/ppermute | solution.py:276
  32.3 2.4 %collective-permute-done.12.refs_1_.refs_5_ = f32[256,256]{1,0:T(8,128)S(1)} collective-permute-done((f32[256,256]{1,0:T(8,128)S(1)}, f32[256,256]{1,0:T(8,128)S(1)}, u32[]{:S(2)}, u32[]{:S(2)}) %collective-permute-start.12) | collective-permute-done | bytes 262176 | tf_op jit(solution)/shard_map/ppermute | solution.py:276
  34.7 0.3 shard_map.81
  35.0 0.7 %collective-permute-start.14 = (f32[256,256]{1,0:T(8,128)S(1)}, f32[256,256]{1,0:T(8,128)S(1)}, u32[]{:S(2)}, u32[]{:S(2)}) collective-permute-start(f32[256,256]{1,0:T(8,128)S(1)} %shard_map.81), channel_id=1, source_target_pairs={{8,16},{12,20},{9,17},{13,21},{10,18},{14,22},{11,19},{15,23}} | collective-permute-start | bytes 786440 | tf_op jit(solution)/shard_map/ppermute | solution.py:276
  35.7 1.8 %collective-permute-done.16.refs_1_ = f32[128,256]{1,0:T(8,128)S(1)} collective-permute-done((f32[128,256]{1,0:T(8,128)S(1)}, f32[128,256]{1,0:T(8,128)S(1)}, u32[]{:S(2)}, u32[]{:S(2)}) %collective-permute-start.16) | collective-permute-done | bytes 131104 | tf_op jit(solution)/shard_map/ppermute | solution.py:327
  37.5 0.7 %collective-permute-start.13 = (f32[256,256]{1,0:T(8,128)S(1)}, f32[256,256]{1,0:T(8,128)S(1)}, u32[]{:S(2)}, u32[]{:S(2)}) collective-permute-start(f32[256,256]{1,0:T(8,128)S(1)} %shard_map.81), channel_id=1, source_target_pairs={{8,24},{12,28},{9,25},{13,29},{10,26},{14,30},{11,27},{15,31}} | collective-permute-start | bytes 786440 | tf_op jit(solution)/shard_map/ppermute | solution.py:276
  38.2 0.0 collective-permute-done.8.refs_4_
  38.2 0.1 collective-permute-start.17
  38.3 0.0 collective-permute-done.11.refs_7_
  38.3 0.0 collective-permute-done.10.refs_6_
  38.3 0.5 shard_map.80
  38.8 0.5 collective-permute-start.18
  39.3 0.5 collective-permute-done.17.refs_3_
  39.8 0.4 shard_map.84
  40.2 5.0 %collective-permute-start.20 = (f32[64,256]{1,0:T(8,128)S(1)}, f32[64,256]{1,0:T(8,128)S(1)}, u32[]{:S(2)}, u32[]{:S(2)}) collective-permute-start(f32[64,256]{1,0:T(8,128)S(1)} %get-tuple-element.42), channel_id=1, source_target_pairs={{0,8},{4,12},{8,0},{12,4},{16,24},{20,28},{24,16},{28,20},{1,9},{5... | collective-permute-start | bytes 196616 | tf_op jit(solution)/shard_map/ppermute | solution.py:276
  45.2 2.5 %collective-permute-start.21 = (f32[64,256]{1,0:T(8,128)S(1)}, f32[64,256]{1,0:T(8,128)S(1)}, u32[]{:S(2)}, u32[]{:S(2)}) collective-permute-start(f32[64,256]{1,0:T(8,128)S(1)} %get-tuple-element.43), channel_id=1, source_target_pairs={{0,16},{4,20},{8,24},{12,28},{16,0},{20,4},{24,8},{28,12},{1,17},{... | collective-permute-start | bytes 196616 | tf_op jit(solution)/shard_map/ppermute | solution.py:276
  47.7 0.0 collective-permute-done.14.refs_7_
  47.7 0.0 collective-permute-start.22
  47.7 0.0 collective-permute-done.13.refs_6_
  47.7 0.5 shard_map.85
  48.2 0.1 collective-permute-start.19
  48.3 0.4 shard_map.87
  48.7 0.0 collective-permute-done.20.refs_1_
  48.7 3.3 %collective-permute-start.23 = (f32[64,256]{1,0:T(8,128)S(1)}, f32[64,256]{1,0:T(8,128)S(1)}, u32[]{:S(2)}, u32[]{:S(2)}) collective-permute-start(f32[64,256]{1,0:T(8,128)S(1)} %get-tuple-element.45), channel_id=1, source_target_pairs={{0,8},{4,12},{8,0},{12,4},{16,24},{20,28},{24,16},{28,20},{1,9},{5... | collective-permute-start | bytes 196616 | tf_op jit(solution)/shard_map/ppermute | solution.py:276
  52.0 0.0 collective-permute-done.19.refs_3_
  52.0 0.5 collective-permute-start.24
  52.5 0.0 collective-permute-done.18.refs_2_
  52.5 2.0 %collective-permute-start.25 = (f32[64,256]{1,0:T(8,128)S(1)}, f32[64,256]{1,0:T(8,128)S(1)}, u32[]{:S(2)}, u32[]{:S(2)}) collective-permute-start(f32[64,256]{1,0:T(8,128)S(1)} %get-tuple-element.47), channel_id=1, source_target_pairs={{0,24},{4,28},{8,16},{12,20},{16,8},{20,12},{24,0},{28,4},{1,25},{... | collective-permute-start | bytes 196616 | tf_op jit(solution)/shard_map/ppermute | solution.py:276
  54.5 1.1 %shard_map.86 = (f32[4,2,128,256]{3,2,1,0:T(8,128)}, f32[8,128]{1,0:T(8,128)S(1)}) custom-call(f32[256,256]{1,0:T(8,128)S(1)} %get-tuple-element.33.refs_0_, f32[256,256]{1,0:T(8,128)S(1)} %get-tuple-element.39.refs_1_.refs_0_, f32[256,256]{1,0:T(8,128)S(1)} %collective-permute-done.18.refs_2_, f32[256,256]{1,0:T(8,128)S(1)} %collective-permute-done.19.refs_3_), custom_call_target="tpu_custom_call" | custom-call | bytes 2097152 | tf_op jit(solution)/shard_map/pallas_call | solution.py:402
  55.6 0.0 collective-permute-done.21.refs_2_
  55.6 0.0 collective-permute-done.22.refs_3_
  55.6 0.0 collective-permute-done.23.refs_5_
  55.6 1.4 %collective-permute-done.24.refs_6_ = f32[64,256]{1,0:T(8,128)S(1)} collective-permute-done((f32[64,256]{1,0:T(8,128)S(1)}, f32[64,256]{1,0:T(8,128)S(1)}, u32[]{:S(2)}, u32[]{:S(2)}) %collective-permute-start.24) | collective-permute-done | bytes 65568 | tf_op jit(solution)/shard_map/ppermute | solution.py:276
  57.0 0.7 %collective-permute-done.25.refs_7_ = f32[64,256]{1,0:T(8,128)S(1)} collective-permute-done((f32[64,256]{1,0:T(8,128)S(1)}, f32[64,256]{1,0:T(8,128)S(1)}, u32[]{:S(2)}, u32[]{:S(2)}) %collective-permute-start.25) | collective-permute-done | bytes 65568 | tf_op jit(solution)/shard_map/ppermute | solution.py:276
  57.7 0.7 %shard_map.88 = f32[128,256]{1,0:T(8,128)} custom-call(f32[128,256]{1,0:T(8,128)S(1)} %copy-done, f32[64,256]{1,0:T(8,128)S(1)} %collective-permute-done.20.refs_1_, f32[64,256]{1,0:T(8,128)S(1)} %collective-permute-done.21.refs_2_, f32[64,256]{1,0:T(8,128)S(1)} %collective-permute-done.22.refs_3_, f32[64,256]{1,0:T(8,128)S(1)} %get-tuple-element.38.refs_8_.refs_4_, ...), custom_call_target="tpu_custom_call" | custom-call | bytes 786432 | tf_op jit(solution)/shard_map/pallas_call | solution.py:46
  (6 shorter events, 0.0 us)
Async XLA Ops:
  0.6 1.4 %copy-start.1 = (f32[64,256]{1,0:T(8,128)S(1)}, f32[64,256]{1,0:T(8,128)}, u32[]{:S(2)}) copy-start(f32[64,256]{1,0:T(8,128)} %param.9) | copy-start | bytes 196612
  0.6 17.7 %collective-permute-start.7 = (f32[1024,256]{1,0:T(8,128)}, f32[1024,256]{1,0:T(8,128)S(1)}, u32[]{:S(2)}, u32[]{:S(2)}) collective-permute-start(f32[1024,256]{1,0:T(8,128)} %param.6), channel_id=1, source_target_pairs={{0,4},{4,0},{8,12},{12,8},{16,20},{20,16},{24,28},{28,24},{1,5},{5... | collective-permute-start | bytes 3145736 | tf_op jit(solution)/shard_map/ppermute | solution.py:280
  2.0 9.1 %collective-permute-start.2 = (f32[128,256]{1,0:T(8,128)S(1)}, f32[128,256]{1,0:T(8,128)S(1)}, u32[]{:S(2)}, u32[]{:S(2)}) collective-permute-start(f32[128,256]{1,0:T(8,128)S(1)} %constant_dynamic-update-slice_fusion.refs_0_), channel_id=1, source_target_pairs={{0,1},{1,2},{2,3},{3,0},{4,5},{5,6},{6,7},{7,4},{8,9},{9,10},{10,1... | collective-permute-start | bytes 393224 | tf_op jit(solution)/shard_map/ppermute | solution.py:285
  4.7 11.9 %collective-permute-start.1 = (f32[128,256]{1,0:T(8,128)S(1)}, f32[128,256]{1,0:T(8,128)S(1)}, u32[]{:S(2)}, u32[]{:S(2)}) collective-permute-start(f32[128,256]{1,0:T(8,128)S(1)} %constant_dynamic-update-slice_fusion.refs_0_), channel_id=1, source_target_pairs={{0,2},{1,3},{2,0},{3,1},{4,6},{5,7},{6,4},{7,5},{8,10},{9,11},{10,... | collective-permute-start | bytes 393224 | tf_op jit(solution)/shard_map/ppermute | solution.py:285
  7.2 9.3 %collective-permute-start = (f32[128,256]{1,0:T(8,128)S(1)}, f32[128,256]{1,0:T(8,128)S(1)}, u32[]{:S(2)}, u32[]{:S(2)}) collective-permute-start(f32[128,256]{1,0:T(8,128)S(1)} %constant_dynamic-update-slice_fusion.refs_0_), channel_id=1, source_target_pairs={{0,3},{1,0},{2,1},{3,2},{4,7},{5,4},{6,5},{7,6},{8,11},{9,8},{10,9... | collective-permute-start | bytes 393224 | tf_op jit(solution)/shard_map/ppermute | solution.py:285
  8.6 9.7 %collective-permute-start.3 = (f32[128,256]{1,0:T(8,128)S(1)}, f32[128,256]{1,0:T(8,128)S(1)}, u32[]{:S(2)}, u32[]{:S(2)}) collective-permute-start(f32[128,256]{1,0:T(8,128)S(1)} %constant_dynamic-update-slice_fusion.refs_0_), channel_id=1, source_target_pairs={{0,4},{4,0},{8,12},{12,8},{16,20},{20,16},{24,28},{28,24},{1,5},{5... | collective-permute-start | bytes 393224 | tf_op jit(solution)/shard_map/ppermute | solution.py:280
  11.1 7.2 %collective-permute-start.6 = (f32[128,256]{1,0:T(8,128)S(1)}, f32[128,256]{1,0:T(8,128)S(1)}, u32[]{:S(2)}, u32[]{:S(2)}) collective-permute-start(f32[128,256]{1,0:T(8,128)S(1)} %collective-permute-done.2.refs_3_), channel_id=1, source_target_pairs={{0,4},{4,0},{8,12},{12,8},{16,20},{20,16},{24,28},{28,24},{1,5},{5... | collective-permute-start | bytes 393224 | tf_op jit(solution)/shard_map/ppermute | solution.py:280
  16.5 1.8 %collective-permute-start.5 = (f32[128,256]{1,0:T(8,128)S(1)}, f32[128,256]{1,0:T(8,128)S(1)}, u32[]{:S(2)}, u32[]{:S(2)}) collective-permute-start(f32[128,256]{1,0:T(8,128)S(1)} %collective-permute-done.1.refs_2_), channel_id=1, source_target_pairs={{0,4},{4,0},{8,12},{12,8},{16,20},{20,16},{24,28},{28,24},{1,5},{5... | collective-permute-start | bytes 393224 | tf_op jit(solution)/shard_map/ppermute | solution.py:280
  16.5 1.8 %collective-permute-start.4 = (f32[128,256]{1,0:T(8,128)S(1)}, f32[128,256]{1,0:T(8,128)S(1)}, u32[]{:S(2)}, u32[]{:S(2)}) collective-permute-start(f32[128,256]{1,0:T(8,128)S(1)} %collective-permute-done.refs_1_), channel_id=1, source_target_pairs={{0,4},{4,0},{8,12},{12,8},{16,20},{20,16},{24,28},{28,24},{1,5},{5... | collective-permute-start | bytes 393224 | tf_op jit(solution)/shard_map/ppermute | solution.py:280
  20.3 10.3 %collective-permute-start.9 = (f32[256,256]{1,0:T(8,128)S(1)}, f32[256,256]{1,0:T(8,128)S(1)}, u32[]{:S(2)}, u32[]{:S(2)}) collective-permute-start(f32[256,256]{1,0:T(8,128)S(1)} %get-tuple-element.30.refs_0_.refs_1_), channel_id=1, source_target_pairs={{0,8},{4,12},{16,24},{20,28},{1,9},{5,13},{17,25},{21,29},{2,10},{... | collective-permute-start | bytes 786440 | tf_op jit(solution)/shard_map/ppermute | solution.py:276
  23.3 5.3 %collective-permute-start.15 = (f32[64,256]{1,0:T(8,128)S(1)}, f32[64,256]{1,0:T(8,128)S(1)}, u32[]{:S(2)}, u32[]{:S(2)}) collective-permute-start(f32[64,256]{1,0:T(8,128)S(1)} %get-tuple-element.37.refs_0_), channel_id=1, source_target_pairs={{0,1},{1,0},{2,3},{3,2},{4,5},{5,4},{6,7},{7,6},{8,9},{9,8},{10,11... | collective-permute-start | bytes 196616 | tf_op jit(solution)/shard_map/ppermute | solution.py:327
  26.2 8.5 %collective-permute-start.12 = (f32[256,256]{1,0:T(8,128)S(1)}, f32[256,256]{1,0:T(8,128)S(1)}, u32[]{:S(2)}, u32[]{:S(2)}) collective-permute-start(f32[256,256]{1,0:T(8,128)S(1)} %get-tuple-element.35.refs_0_.refs_1_), channel_id=1, source_target_pairs={{0,8},{4,12},{16,24},{20,28},{1,9},{5,13},{17,25},{21,29},{2,10},{... | collective-permute-start | bytes 786440 | tf_op jit(solution)/shard_map/ppermute | solution.py:276
  27.5 10.7 %collective-permute-start.8 = (f32[256,256]{1,0:T(8,128)S(1)}, f32[256,256]{1,0:T(8,128)S(1)}, u32[]{:S(2)}, u32[]{:S(2)}) collective-permute-start(f32[256,256]{1,0:T(8,128)S(1)} %get-tuple-element.32.refs_2_.refs_3_), channel_id=1, source_target_pairs={{16,24},{20,28},{17,25},{21,29},{18,26},{22,30},{19,27},{23,31}} | collective-permute-start | bytes 786440 | tf_op jit(solution)/shard_map/ppermute | solution.py:276
  28.6 8.8 %collective-permute-start.16 = (f32[128,256]{1,0:T(8,128)S(1)}, f32[128,256]{1,0:T(8,128)S(1)}, u32[]{:S(2)}, u32[]{:S(2)}) collective-permute-start(f32[128,256]{1,0:T(8,128)S(1)} %shard_map.82.refs_0_), channel_id=1, source_target_pairs={{0,2},{1,3},{2,0},{3,1},{4,6},{5,7},{6,4},{7,5},{8,10},{9,11},{10,... | collective-permute-start | bytes 393224 | tf_op jit(solution)/shard_map/ppermute | solution.py:327
  30.9 7.4 %collective-permute-start.11 = (f32[256,256]{1,0:T(8,128)S(1)}, f32[256,256]{1,0:T(8,128)S(1)}, u32[]{:S(2)}, u32[]{:S(2)}) collective-permute-start(f32[256,256]{1,0:T(8,128)S(1)} %shard_map.79.refs_3_.refs_2_), channel_id=1, source_target_pairs={{8,16},{12,20},{9,17},{13,21},{10,18},{14,22},{11,19},{15,23}} | collective-permute-start | bytes 786440 | tf_op jit(solution)/shard_map/ppermute | solution.py:276
  31.6 6.7 %collective-permute-start.10 = (f32[256,256]{1,0:T(8,128)S(1)}, f32[256,256]{1,0:T(8,128)S(1)}, u32[]{:S(2)}, u32[]{:S(2)}) collective-permute-start(f32[256,256]{1,0:T(8,128)S(1)} %shard_map.79.refs_3_.refs_2_), channel_id=1, source_target_pairs={{8,24},{12,28},{9,25},{13,29},{10,26},{14,30},{11,27},{15,31}} | collective-permute-start | bytes 786440 | tf_op jit(solution)/shard_map/ppermute | solution.py:276
  35.0 12.8 %collective-permute-start.14 = (f32[256,256]{1,0:T(8,128)S(1)}, f32[256,256]{1,0:T(8,128)S(1)}, u32[]{:S(2)}, u32[]{:S(2)}) collective-permute-start(f32[256,256]{1,0:T(8,128)S(1)} %shard_map.81), channel_id=1, source_target_pairs={{8,16},{12,20},{9,17},{13,21},{10,18},{14,22},{11,19},{15,23}} | collective-permute-start | bytes 786440 | tf_op jit(solution)/shard_map/ppermute | solution.py:276
  37.5 10.2 %collective-permute-start.13 = (f32[256,256]{1,0:T(8,128)S(1)}, f32[256,256]{1,0:T(8,128)S(1)}, u32[]{:S(2)}, u32[]{:S(2)}) collective-permute-start(f32[256,256]{1,0:T(8,128)S(1)} %shard_map.81), channel_id=1, source_target_pairs={{8,24},{12,28},{9,25},{13,29},{10,26},{14,30},{11,27},{15,31}} | collective-permute-start | bytes 786440 | tf_op jit(solution)/shard_map/ppermute | solution.py:276
  38.2 1.6 %collective-permute-start.17 = (f32[256,256]{1,0:T(8,128)S(1)}, f32[256,256]{1,0:T(8,128)S(1)}, u32[]{:S(2)}, u32[]{:S(2)}) collective-permute-start(f32[256,256]{1,0:T(8,128)S(1)} %shard_map.83.refs_2_), channel_id=1, source_target_pairs={{0,4},{4,0},{8,12},{12,8},{16,20},{20,16},{24,28},{28,24},{1,5},{5... | collective-permute-start | bytes 786440 | tf_op jit(solution)/shard_map/ppermute | solution.py:280
  38.8 13.7 %collective-permute-start.18 = (f32[256,256]{1,0:T(8,128)S(1)}, f32[256,256]{1,0:T(8,128)S(1)}, u32[]{:S(2)}, u32[]{:S(2)}) collective-permute-start(f32[256,256]{1,0:T(8,128)S(1)} %get-tuple-element.36.refs_1_), channel_id=1, source_target_pairs={{0,4},{4,0},{8,12},{12,8},{16,20},{20,16},{24,28},{28,24},{1,5},{5... | collective-permute-start | bytes 786440 | tf_op jit(solution)/shard_map/ppermute | solution.py:280
  40.2 8.5 %collective-permute-start.20 = (f32[64,256]{1,0:T(8,128)S(1)}, f32[64,256]{1,0:T(8,128)S(1)}, u32[]{:S(2)}, u32[]{:S(2)}) collective-permute-start(f32[64,256]{1,0:T(8,128)S(1)} %get-tuple-element.42), channel_id=1, source_target_pairs={{0,8},{4,12},{8,0},{12,4},{16,24},{20,28},{24,16},{28,20},{1,9},{5... | collective-permute-start | bytes 196616 | tf_op jit(solution)/shard_map/ppermute | solution.py:276
  45.2 10.4 %collective-permute-start.21 = (f32[64,256]{1,0:T(8,128)S(1)}, f32[64,256]{1,0:T(8,128)S(1)}, u32[]{:S(2)}, u32[]{:S(2)}) collective-permute-start(f32[64,256]{1,0:T(8,128)S(1)} %get-tuple-element.43), channel_id=1, source_target_pairs={{0,16},{4,20},{8,24},{12,28},{16,0},{20,4},{24,8},{28,12},{1,17},{... | collective-permute-start | bytes 196616 | tf_op jit(solution)/shard_map/ppermute | solution.py:276
  47.7 7.9 %collective-permute-start.22 = (f32[64,256]{1,0:T(8,128)S(1)}, f32[64,256]{1,0:T(8,128)S(1)}, u32[]{:S(2)}, u32[]{:S(2)}) collective-permute-start(f32[64,256]{1,0:T(8,128)S(1)} %get-tuple-element.44), channel_id=1, source_target_pairs={{0,24},{4,28},{8,16},{12,20},{16,8},{20,12},{24,0},{28,4},{1,25},{... | collective-permute-start | bytes 196616 | tf_op jit(solution)/shard_map/ppermute | solution.py:276
  48.2 3.8 %collective-permute-start.19 = (f32[256,256]{1,0:T(8,128)S(1)}, f32[256,256]{1,0:T(8,128)S(1)}, u32[]{:S(2)}, u32[]{:S(2)}) collective-permute-start(f32[256,256]{1,0:T(8,128)S(1)} %get-tuple-element.40.refs_1_), channel_id=1, source_target_pairs={{0,4},{4,0},{8,12},{12,8},{16,20},{20,16},{24,28},{28,24},{1,5},{5... | collective-permute-start | bytes 786440 | tf_op jit(solution)/shard_map/ppermute | solution.py:280
  48.7 6.9 %collective-permute-start.23 = (f32[64,256]{1,0:T(8,128)S(1)}, f32[64,256]{1,0:T(8,128)S(1)}, u32[]{:S(2)}, u32[]{:S(2)}) collective-permute-start(f32[64,256]{1,0:T(8,128)S(1)} %get-tuple-element.45), channel_id=1, source_target_pairs={{0,8},{4,12},{8,0},{12,4},{16,24},{20,28},{24,16},{28,20},{1,9},{5... | collective-permute-start | bytes 196616 | tf_op jit(solution)/shard_map/ppermute | solution.py:276
  52.0 5.0 %collective-permute-start.24 = (f32[64,256]{1,0:T(8,128)S(1)}, f32[64,256]{1,0:T(8,128)S(1)}, u32[]{:S(2)}, u32[]{:S(2)}) collective-permute-start(f32[64,256]{1,0:T(8,128)S(1)} %get-tuple-element.46), channel_id=1, source_target_pairs={{0,16},{4,20},{8,24},{12,28},{16,0},{20,4},{24,8},{28,12},{1,17},{... | collective-permute-start | bytes 196616 | tf_op jit(solution)/shard_map/ppermute | solution.py:276
  52.5 5.2 %copy-start = (f32[128,256]{1,0:T(8,128)S(1)}, f32[128,256]{1,0:T(8,128)}, u32[]{:S(2)}) copy-start(f32[128,256]{1,0:T(8,128)} %refs_0_.1) | copy-start | bytes 393220
  52.5 5.2 %collective-permute-start.25 = (f32[64,256]{1,0:T(8,128)S(1)}, f32[64,256]{1,0:T(8,128)S(1)}, u32[]{:S(2)}, u32[]{:S(2)}) collective-permute-start(f32[64,256]{1,0:T(8,128)S(1)} %get-tuple-element.47), channel_id=1, source_target_pairs={{0,24},{4,28},{8,16},{12,20},{16,8},{20,12},{24,0},{28,4},{1,25},{... | collective-permute-start | bytes 196616 | tf_op jit(solution)/shard_map/ppermute | solution.py:276
